TPU v7x, 32 devices: a whole 2x2x4 slice. The times are simulated.
32 devices in a mesh: dp: 8 (over z, y), head: 4 (over x, core).
Axes of the slice: x: 2, y: 2, z: 4, core: 2. Of those that a mesh axis runs over, the one named last changes fastest.
Arguments:
- tokens: bfloat16 [50176, 384], P(('dp', 'head')), may hold values from -6 to 6
- crop_ids: int32 [50176], P('dp'), may hold values from 0 to 1023, as said below
- grad_out: bfloat16 [50176, 384], P(('dp', 'head')), may hold values from -6 to 6
- query_key_value: float32 [3, 384, 384], P(None, 'dp', 'head'), may hold values from -0.3125 to 0.3125
- output_weight: float32 [384, 384], P('head', 'dp'), may hold values from -1.25 to 1.25
- expand_weight: float32 [384, 1536], P('dp', 'head'), may hold values from -0.3125 to 0.3125
- contract_weight: float32 [1536, 384], P('head', 'dp'), may hold values from -0.15625 to 0.15625
- query_value_bias: float32 [2, 384], P(None, 'head'), may hold values from -3 to 3
- expand_bias: float32 [1536], P('head'), may hold values from -3 to 3
- position_table: float32 [169, 12], P(None, 'head'), may hold values from -4 to 4
- norm_params: float32 [6, 384], replicated, may hold values from -0.5 to 1.4
- query_key_value_moment: float32 [3, 384, 384], P(None, 'dp', 'head'), may hold values from -80 to 80
- query_key_value_square: float32 [3, 384, 384], P(None, 'dp', 'head'), may hold values from 6.272 to 100.352
- output_weight_moment: float32 [384, 384], P('head', 'dp'), may hold values from -80 to 80
- output_weight_square: float32 [384, 384], P('head', 'dp'), may hold values from 6.272 to 100.352
- expand_weight_moment: float32 [384, 1536], P('dp', 'head'), may hold values from -80 to 80
- expand_weight_square: float32 [384, 1536], P('dp', 'head'), may hold values from 6.272 to 100.352
- contract_weight_moment: float32 [1536, 384], P('head', 'dp'), may hold values from -80 to 80
- contract_weight_square: float32 [1536, 384], P('head', 'dp'), may hold values from 6.272 to 100.352
- query_value_bias_moment: float32 [2, 384], P(None, 'head'), may hold values from -80 to 80
- query_value_bias_square: float32 [2, 384], P(None, 'head'), may hold values from 6.272 to 100.352
- expand_bias_moment: float32 [1536], P('head'), may hold values from -80 to 80
- expand_bias_square: float32 [1536], P('head'), may hold values from 6.272 to 100.352
- position_table_moment: float32 [169, 12], P(None, 'head'), may hold values from -80 to 80
- position_table_square: float32 [169, 12], P(None, 'head'), may hold values from 6.272 to 100.352
- norm_params_moment: float32 [6, 384], replicated, may hold values from -160 to 160
- norm_params_square: float32 [6, 384], replicated, may hold values from 25.088 to 401.408
Outputs:
- block_out: bfloat16 [50176, 384], P(('dp', 'head'))
- grad_tokens: float32 [50176, 384], P(('dp', 'head'))
- query_key_value_updated: float32 [3, 384, 384], P(None, 'dp', 'head')
- query_key_value_moment_next: float32 [3, 384, 384], P(None, 'dp', 'head')
- query_key_value_square_next: float32 [3, 384, 384], P(None, 'dp', 'head')
- output_weight_updated: float32 [384, 384], P('head', 'dp')
- output_weight_moment_next: float32 [384, 384], P('head', 'dp')
- output_weight_square_next: float32 [384, 384], P('head', 'dp')
- expand_weight_updated: float32 [384, 1536], P('dp', 'head')
- expand_weight_moment_next: float32 [384, 1536], P('dp', 'head')
- expand_weight_square_next: float32 [384, 1536], P('dp', 'head')
- contract_weight_updated: float32 [1536, 384], P('head', 'dp')
- contract_weight_moment_next: float32 [1536, 384], P('head', 'dp')
- contract_weight_square_next: float32 [1536, 384], P('head', 'dp')
- query_value_bias_updated: float32 [2, 384], P(None, 'head')
- query_value_bias_moment_next: float32 [2, 384], P(None, 'head')
- query_value_bias_square_next: float32 [2, 384], P(None, 'head')
- expand_bias_updated: float32 [1536], P('head')
- expand_bias_moment_next: float32 [1536], P('head')
- expand_bias_square_next: float32 [1536], P('head')
- position_table_updated: float32 [169, 12], P(None, 'head')
- position_table_moment_next: float32 [169, 12], P(None, 'head')
- position_table_square_next: float32 [169, 12], P(None, 'head')
- norm_params_updated: float32 [6, 384], replicated
- norm_params_moment_next: float32 [6, 384], replicated
- norm_params_square_next: float32 [6, 384], replicated
Inputs may be any that keep to these rules, and one draw needn't show every extreme that they name: `crop_ids`: each canvas is cut by one row and one column, each drawn from 4 to 10, into four rectangular crops; crop numbers are 4 * canvas + quadrant.
All inputs are finite; a program needn't handle non-finite values.
Results may differ from a plain program's by a relative error of at most 0.015.
Values may be sent and summed in bfloat16 or wider, within the bound.
No kernel may reach another device: no remote copies, remote signals or barrier semaphores. Data moves between devices by JAX's collectives and lax.ppermute only.
A program may use at most 128 MiB of HBM per device.

v0:
```python
import math

import jax
import jax.numpy as jnp
from jax import lax
from jax.sharding import PartitionSpec as P

HEAD_DIM = 32
WINDOW = 7
SIDE = 14
SHIFT = 3
STEP = 10


NORM_EPS = 1e-05
BETA_ONE = 0.9
BETA_TWO = 0.999
ADAM_EPS = 1e-08
RATE_MATRIX = 0.1
RATE_SMALL = 0.5
DECAY_MATRIX = 0.05
MASKED = -1e30
ROOT_HALF = 0.7071067811865476
ROOT_TWO_PI = 2.5066282746310002
CONTRACT_ROWS = (((0,), (0,)), ((), ()))


def layer_stats(values):
    centred = values - jnp.mean(values, axis=-1, keepdims=True)
    inv_std = lax.rsqrt(jnp.mean(centred * centred, axis=-1, keepdims=True) + NORM_EPS)
    return (centred * inv_std, inv_std)


def norm_back(grad_norm, normed_hat, inv_std, gain_row):
    grad_hat = grad_norm * gain_row
    inner = grad_hat - jnp.mean(grad_hat, axis=-1, keepdims=True)
    inner = inner - normed_hat * jnp.mean(grad_hat * normed_hat, axis=-1, keepdims=True)
    return inv_std * inner


def to_windows(values):
    canvas_count = values.shape[0] // (SIDE * SIDE)
    per_side = SIDE // WINDOW
    feature_count = values.shape[-1]
    grid = values.reshape(canvas_count, SIDE, SIDE, feature_count)
    grid = jnp.roll(grid, (-SHIFT, -SHIFT), axis=(1, 2))
    grid = grid.reshape(canvas_count, per_side, WINDOW, per_side, WINDOW, feature_count)
    grid = grid.transpose(0, 1, 3, 2, 4, 5)
    return grid.reshape(canvas_count * per_side * per_side, WINDOW * WINDOW, feature_count)


def from_windows(values):
    per_side = SIDE // WINDOW
    canvas_count = values.shape[0] // (per_side * per_side)
    feature_count = values.shape[-1]
    grid = values.reshape(canvas_count, per_side, per_side, WINDOW, WINDOW, feature_count)
    grid = grid.transpose(0, 1, 3, 2, 4, 5).reshape(canvas_count, SIDE, SIDE, feature_count)
    grid = jnp.roll(grid, (SHIFT, SHIFT), axis=(1, 2))
    return grid.reshape(canvas_count * SIDE * SIDE, feature_count)


def region_mask():
    coords = jnp.arange(SIDE)
    band_ids = jnp.where(coords < SIDE - WINDOW, 0, jnp.where(coords < SIDE - SHIFT, 1, 2))
    region = band_ids[:, None] * 3 + band_ids[None, :]
    per_side = SIDE // WINDOW
    region = region.reshape(per_side, WINDOW, per_side, WINDOW).transpose(0, 2, 1, 3)
    region = region.reshape(per_side * per_side, WINDOW * WINDOW)
    return region[:, :, None] == region[:, None, :]


def relative_index():
    places = jnp.arange(WINDOW * WINDOW)
    row_place = places // WINDOW
    col_place = places % WINDOW
    row_diff = row_place[:, None] - row_place[None, :] + WINDOW - 1
    col_diff = col_place[:, None] - col_place[None, :] + WINDOW - 1
    return row_diff * (2 * WINDOW - 1) + col_diff


def bias_lookup(table_b):
    onehot = (relative_index().reshape(-1, 1) == jnp.arange(table_b.shape[0])[None, :]).astype(
        jnp.float32
    )
    looked = jnp.dot(onehot, table_b.astype(jnp.float32), precision=lax.Precision.HIGHEST)
    return (looked.T.reshape(table_b.shape[1], WINDOW * WINDOW, WINDOW * WINDOW), onehot)


def split_heads(window_vals, head_span):
    window_shape = (window_vals.shape[0], WINDOW * WINDOW, head_span // HEAD_DIM, HEAD_DIM)
    query_w = window_vals[:, :, :head_span].reshape(window_shape)
    key_w = window_vals[:, :, head_span : 2 * head_span].reshape(window_shape)
    value_w = window_vals[:, :, 2 * head_span :].reshape(window_shape)
    return (query_w, key_w, value_w)


def allowed_pairs(crop_rows):
    crop_windows = to_windows(crop_rows[:, None])[:, :, 0]
    same_crop = crop_windows[:, :, None] == crop_windows[:, None, :]
    per_canvas = SIDE // WINDOW * (SIDE // WINDOW)
    return same_crop & jnp.tile(region_mask(), (crop_windows.shape[0] // per_canvas, 1, 1))


def masked_scores(query_w, key_w, bias_heads, crop_rows):
    raw_scores = jnp.einsum("wqhd,wkhd->whqk", query_w, key_w, preferred_element_type=jnp.float32)
    scores = raw_scores * HEAD_DIM ** (-0.5) + bias_heads[None]
    return jnp.where(allowed_pairs(crop_rows)[:, None], scores, MASKED)


def attend_block(packed, crop_rows, bias_heads):
    head_span = packed.shape[1] // 3
    query_w, key_w, value_w = split_heads(to_windows(packed), head_span)
    scores = masked_scores(query_w, key_w, bias_heads, crop_rows)
    top_score = jnp.max(scores, axis=-1, keepdims=True)
    exp_scores = jnp.exp(scores - top_score)
    row_total = jnp.sum(exp_scores, axis=-1, keepdims=True)
    probs_b = (exp_scores / row_total).astype(jnp.bfloat16)
    mixed_rows = jnp.einsum("whqk,wkhd->wqhd", probs_b, value_w, preferred_element_type=jnp.float32)
    log_total = top_score[..., 0] + jnp.log(row_total[..., 0])
    mixed_rows = mixed_rows.astype(jnp.bfloat16).reshape(
        mixed_rows.shape[0], WINDOW * WINDOW, head_span
    )
    return (from_windows(mixed_rows), log_total)


def attend_back(packed, crop_rows, grad_merged, log_total, bias_heads):
    head_span = packed.shape[1] // 3
    query_w, key_w, value_w = split_heads(to_windows(packed), head_span)
    scores = masked_scores(query_w, key_w, bias_heads, crop_rows)
    probs = jnp.exp(scores - log_total[..., None])
    probs_b = probs.astype(jnp.bfloat16)
    grad_w = to_windows(grad_merged).reshape(query_w.shape)
    grad_probs = jnp.einsum("wqhd,wkhd->whqk", grad_w, value_w, preferred_element_type=jnp.float32)
    grad_scores = probs * (grad_probs - jnp.sum(probs * grad_probs, axis=-1, keepdims=True))
    grad_scores = grad_scores.astype(jnp.bfloat16)
    scale_head = HEAD_DIM ** (-0.5)
    grad_value = jnp.einsum("whqk,wqhd->wkhd", probs_b, grad_w, preferred_element_type=jnp.float32)
    grad_query = (
        jnp.einsum("whqk,wkhd->wqhd", grad_scores, key_w, preferred_element_type=jnp.float32)
        * scale_head
    )
    grad_key = (
        jnp.einsum("whqk,wqhd->wkhd", grad_scores, query_w, preferred_element_type=jnp.float32)
        * scale_head
    )
    flat_shape = (query_w.shape[0], WINDOW * WINDOW, head_span)
    stacked = jnp.concatenate(
        [
            grad_query.reshape(flat_shape),
            grad_key.reshape(flat_shape),
            grad_value.reshape(flat_shape),
        ],
        axis=2,
    )
    table_part = jnp.sum(grad_scores.astype(jnp.float32), axis=0)
    return (from_windows(stacked.astype(jnp.bfloat16)), table_part)


def canvas_blocks(row_total):
    canvas_count = row_total // (SIDE * SIDE)
    per_block = math.gcd(canvas_count, 16)
    return (canvas_count // per_block, per_block * SIDE * SIDE)


def adamw_step(master, grad_value, moment, square, step_rate, decay_rate):
    moment_new = BETA_ONE * moment + (1.0 - BETA_ONE) * grad_value
    square_new = BETA_TWO * square + (1.0 - BETA_TWO) * grad_value * grad_value
    moment_hat = moment_new / (1.0 - BETA_ONE**STEP)
    square_hat = square_new / (1.0 - BETA_TWO**STEP)
    updated = master - step_rate * (
        moment_hat / (jnp.sqrt(square_hat) + ADAM_EPS) + decay_rate * master
    )
    return (updated, moment_new, square_new)


def per_device(
    tokens,
    crop_ids,
    grad_out,
    query_key_value,
    output_weight,
    expand_weight,
    contract_weight,
    query_value_bias,
    expand_bias,
    position_table,
    norm_params,
    query_key_value_moment,
    query_key_value_square,
    output_weight_moment,
    output_weight_square,
    expand_weight_moment,
    expand_weight_square,
    contract_weight_moment,
    contract_weight_square,
    query_value_bias_moment,
    query_value_bias_square,
    expand_bias_moment,
    expand_bias_square,
    position_table_moment,
    position_table_square,
    norm_params_moment,
    norm_params_square,
):
    attn_in, attn_out, expand_w, contract_w = (
        lax.all_gather(query_key_value.astype(jnp.bfloat16), "dp", axis=1, tiled=True),
        lax.all_gather(output_weight.astype(jnp.bfloat16), "dp", axis=1, tiled=True),
        lax.all_gather(expand_weight.astype(jnp.bfloat16), "dp", axis=0, tiled=True),
        lax.all_gather(contract_weight.astype(jnp.bfloat16), "dp", axis=1, tiled=True),
    )
    qv_small = query_value_bias.astype(jnp.bfloat16)
    expand_small = expand_bias.astype(jnp.bfloat16)
    table_small = position_table.astype(jnp.bfloat16)
    slab_rows = tokens.shape[0]
    attn_in, attn_out, expand_w, contract_w, qv_small, expand_small, table_small = (
        lax.all_gather(attn_in, "head", axis=2, tiled=True),
        lax.all_gather(attn_out, "head", axis=0, tiled=True),
        lax.all_gather(expand_w, "head", axis=1, tiled=True),
        lax.all_gather(contract_w, "head", axis=0, tiled=True),
        lax.all_gather(qv_small, "head", axis=1, tiled=True),
        lax.all_gather(expand_small, "head", axis=0, tiled=True),
        lax.all_gather(table_small, "head", axis=1, tiled=True),
    )
    crop_rows = lax.dynamic_slice_in_dim(crop_ids, lax.axis_index("head") * slab_rows, slab_rows, 0)
    head_span = attn_in.shape[2]
    bias_heads, onehot = bias_lookup(table_small)
    tokens_f = tokens.astype(jnp.float32)
    hat_one, inv_one = layer_stats(tokens_f)
    normed_one = (hat_one * norm_params[0] + norm_params[1]).astype(jnp.bfloat16)
    all_rows = normed_one.shape[0]
    packed = jnp.concatenate(
        [
            jnp.dot(normed_one, attn_in[0], preferred_element_type=jnp.float32)
            + qv_small[0].astype(jnp.float32),
            jnp.dot(normed_one, attn_in[1], preferred_element_type=jnp.float32),
            jnp.dot(normed_one, attn_in[2], preferred_element_type=jnp.float32)
            + qv_small[1].astype(jnp.float32),
        ],
        axis=1,
    ).astype(jnp.bfloat16)
    block_count, block_rows = canvas_blocks(all_rows)
    packed_blocks = packed.reshape(block_count, block_rows, 3 * head_span)
    crop_blocks = crop_rows.reshape(block_count, block_rows)

    def forward_block(block_in):
        return attend_block(block_in[0], block_in[1], bias_heads)

    merged_blocks, log_totals = lax.map(forward_block, (packed_blocks, crop_blocks))
    merged = merged_blocks.reshape(all_rows, head_span)
    attn_rows = jnp.dot(merged, attn_out, preferred_element_type=jnp.float32)
    middle = tokens_f + attn_rows + norm_params[4]
    hat_two, inv_two = layer_stats(middle)
    normed_two = (hat_two * norm_params[2] + norm_params[3]).astype(jnp.bfloat16)
    pre_act = jnp.dot(
        normed_two, expand_w, preferred_element_type=jnp.float32
    ) + expand_small.astype(jnp.float32)
    hidden = jax.nn.gelu(pre_act, approximate=False).astype(jnp.bfloat16)
    mlp_rows = jnp.dot(hidden, contract_w, preferred_element_type=jnp.float32)
    block_out = (middle + mlp_rows + norm_params[5]).astype(jnp.bfloat16)
    grad_top = grad_out.astype(jnp.float32)
    grad_hidden = jnp.dot(grad_out, contract_w.T, preferred_element_type=jnp.float32)
    cumulative = 0.5 * (1.0 + lax.erf(pre_act * ROOT_HALF))
    gelu_slope = cumulative + pre_act * jnp.exp(-0.5 * pre_act * pre_act) / ROOT_TWO_PI
    grad_pre = (grad_hidden * gelu_slope).astype(jnp.bfloat16)
    contract_grad = lax.dot_general(
        hidden, grad_out, CONTRACT_ROWS, preferred_element_type=jnp.float32
    )
    expand_grad = lax.dot_general(
        normed_two, grad_pre, CONTRACT_ROWS, preferred_element_type=jnp.float32
    )
    expand_bias_grad = jnp.sum(grad_pre.astype(jnp.float32), axis=0)
    grad_norm_two = jnp.dot(grad_pre, expand_w.T, preferred_element_type=jnp.float32)
    grad_middle = grad_top + norm_back(grad_norm_two, hat_two, inv_two, norm_params[2])
    grad_middle_b = grad_middle.astype(jnp.bfloat16)
    output_grad = lax.dot_general(
        merged, grad_middle_b, CONTRACT_ROWS, preferred_element_type=jnp.float32
    )
    grad_merged = jnp.dot(grad_middle_b, attn_out.T, preferred_element_type=jnp.float32).astype(
        jnp.bfloat16
    )

    def backward_block(block_in):
        return attend_back(block_in[0], block_in[1], block_in[2], block_in[3], bias_heads)

    grad_blocks, table_parts = lax.map(
        backward_block,
        (
            packed_blocks,
            crop_blocks,
            grad_merged.reshape(block_count, block_rows, head_span),
            log_totals,
        ),
    )
    grad_packed = grad_blocks.reshape(all_rows, 3 * head_span)
    table_sum = jnp.sum(table_parts, axis=0)
    table_grad = jnp.dot(
        onehot.T, table_sum.reshape(table_sum.shape[0], -1).T, precision=lax.Precision.HIGHEST
    )
    qv_grad = jnp.stack(
        [
            jnp.sum(grad_packed[:, :head_span].astype(jnp.float32), axis=0),
            jnp.sum(grad_packed[:, 2 * head_span :].astype(jnp.float32), axis=0),
        ]
    )
    grad_three = grad_packed.reshape(all_rows, 3, head_span)
    attn_in_grad = jnp.einsum(
        "rc,rjs->jcs", normed_one, grad_three, preferred_element_type=jnp.float32
    )
    grad_norm_one = jnp.einsum(
        "rjs,jcs->rc", grad_three, attn_in, preferred_element_type=jnp.float32
    )
    grad_tokens = grad_middle + norm_back(grad_norm_one, hat_one, inv_one, norm_params[0])
    norm_grad = jnp.stack(
        [
            jnp.sum(grad_norm_one * hat_one, axis=0),
            jnp.sum(grad_norm_one, axis=0),
            jnp.sum(grad_norm_two * hat_two, axis=0),
            jnp.sum(grad_norm_two, axis=0),
            jnp.sum(grad_middle, axis=0),
            jnp.sum(grad_top, axis=0),
        ]
    )
    attn_in_grad, output_grad, expand_grad, contract_grad, qv_grad, expand_bias_grad, table_grad = (
        lax.psum_scatter(
            attn_in_grad.astype(jnp.bfloat16), "head", scatter_dimension=2, tiled=True
        ).astype(jnp.float32),
        lax.psum_scatter(
            output_grad.astype(jnp.bfloat16), "head", scatter_dimension=0, tiled=True
        ).astype(jnp.float32),
        lax.psum_scatter(
            expand_grad.astype(jnp.bfloat16), "head", scatter_dimension=1, tiled=True
        ).astype(jnp.float32),
        lax.psum_scatter(
            contract_grad.astype(jnp.bfloat16), "head", scatter_dimension=0, tiled=True
        ).astype(jnp.float32),
        lax.psum_scatter(
            qv_grad.astype(jnp.bfloat16), "head", scatter_dimension=1, tiled=True
        ).astype(jnp.float32),
        lax.psum_scatter(
            expand_bias_grad.astype(jnp.bfloat16), "head", scatter_dimension=0, tiled=True
        ).astype(jnp.float32),
        lax.psum_scatter(
            table_grad.astype(jnp.bfloat16), "head", scatter_dimension=1, tiled=True
        ).astype(jnp.float32),
    )
    attn_in_grad, output_grad, expand_grad, contract_grad = (
        lax.psum_scatter(attn_in_grad, "dp", scatter_dimension=1, tiled=True),
        lax.psum_scatter(output_grad, "dp", scatter_dimension=1, tiled=True),
        lax.psum_scatter(expand_grad, "dp", scatter_dimension=0, tiled=True),
        lax.psum_scatter(contract_grad, "dp", scatter_dimension=1, tiled=True),
    )
    qv_grad, expand_bias_grad, table_grad = lax.psum((qv_grad, expand_bias_grad, table_grad), "dp")
    norm_grad = lax.psum(norm_grad, ("dp", "head"))
    first_new = adamw_step(
        query_key_value,
        attn_in_grad,
        query_key_value_moment,
        query_key_value_square,
        RATE_MATRIX,
        DECAY_MATRIX,
    )
    second_new = adamw_step(
        output_weight,
        output_grad,
        output_weight_moment,
        output_weight_square,
        RATE_MATRIX,
        DECAY_MATRIX,
    )
    third_new = adamw_step(
        expand_weight,
        expand_grad,
        expand_weight_moment,
        expand_weight_square,
        RATE_MATRIX,
        DECAY_MATRIX,
    )
    fourth_new = adamw_step(
        contract_weight,
        contract_grad,
        contract_weight_moment,
        contract_weight_square,
        RATE_MATRIX,
        DECAY_MATRIX,
    )
    fifth_new = adamw_step(
        query_value_bias, qv_grad, query_value_bias_moment, query_value_bias_square, RATE_SMALL, 0.0
    )
    sixth_new = adamw_step(
        expand_bias, expand_bias_grad, expand_bias_moment, expand_bias_square, RATE_SMALL, 0.0
    )
    seventh_new = adamw_step(
        position_table, table_grad, position_table_moment, position_table_square, RATE_SMALL, 0.0
    )
    eighth_new = adamw_step(
        norm_params, norm_grad, norm_params_moment, norm_params_square, RATE_SMALL, 0.0
    )
    return (
        block_out,
        grad_tokens,
        first_new[0],
        first_new[1],
        first_new[2],
        second_new[0],
        second_new[1],
        second_new[2],
        third_new[0],
        third_new[1],
        third_new[2],
        fourth_new[0],
        fourth_new[1],
        fourth_new[2],
        fifth_new[0],
        fifth_new[1],
        fifth_new[2],
        sixth_new[0],
        sixth_new[1],
        sixth_new[2],
        seventh_new[0],
        seventh_new[1],
        seventh_new[2],
        eighth_new[0],
        eighth_new[1],
        eighth_new[2],
    )


def solution(mesh):
    in_specs = (
        P(("dp", "head"), None),
        P("dp"),
        P(("dp", "head"), None),
        P(None, "dp", "head"),
        P("head", "dp"),
        P("dp", "head"),
        P("head", "dp"),
        P(None, "head"),
        P("head"),
        P(None, "head"),
        P(),
        P(None, "dp", "head"),
        P(None, "dp", "head"),
        P("head", "dp"),
        P("head", "dp"),
        P("dp", "head"),
        P("dp", "head"),
        P("head", "dp"),
        P("head", "dp"),
        P(None, "head"),
        P(None, "head"),
        P("head"),
        P("head"),
        P(None, "head"),
        P(None, "head"),
        P(),
        P(),
    )
    out_specs = (
        P(("dp", "head"), None),
        P(("dp", "head"), None),
        P(None, "dp", "head"),
        P(None, "dp", "head"),
        P(None, "dp", "head"),
        P("head", "dp"),
        P("head", "dp"),
        P("head", "dp"),
        P("dp", "head"),
        P("dp", "head"),
        P("dp", "head"),
        P("head", "dp"),
        P("head", "dp"),
        P("head", "dp"),
        P(None, "head"),
        P(None, "head"),
        P(None, "head"),
        P("head"),
        P("head"),
        P("head"),
        P(None, "head"),
        P(None, "head"),
        P(None, "head"),
        P(),
        P(),
        P(),
    )
    return jax.shard_map(
        per_device, mesh=mesh, in_specs=in_specs, out_specs=out_specs, check_vma=False
    )
```

profile of v0, /device:TPU:0, one launch (start us, length us, event | category | flops | bytes accessed | tf_op | source)
XLA Modules:
  0.0 855.2 jit_solution(6969740442790782784)
XLA Ops:
  8.3 34.6 %all_gather.39 = bf16[384,384]{1,0:T(8,128)(2,1)} all-gather(bf16[48,384]{1,0:T(8,128)(2,1)S(1)} %convert_element_type.143), channel_id=1, replica_groups=mesh['dp'=8,'head'=4] {'dp'}, dimensions={0}, use_global_device_ids=true | all-gather | bytes 331776 | tf_op jit(solution)/shard_map/all_gather | solution.py:208
  44.7 5.0 all-gather
  50.5 5.2 all-gather.1
  61.5 30.9 %all_gather.33 = bf16[3,384,96]{2,1,0:T(8,128)(2,1)S(1)} all-gather(bf16[3,48,96]{2,1,0:T(8,128)(2,1)S(1)} %convert_element_type.135), channel_id=1, replica_groups=mesh['dp'=8,'head'=4] {'dp'}, dimensions={1}, use_global_device_ids=true | all-gather | bytes 248832 | tf_op jit(solution)/shard_map/all_gather | solution.py:206
  92.6 9.6 %all_gather.34 = bf16[3,384,384]{1,2,0:T(8,128)(2,1)S(1)} all-gather(bf16[3,384,96]{1,2,0:T(8,128)(2,1)S(1)} %copy.292), channel_id=1, replica_groups=mesh['dp'=8,'head'=4] {'head'}, dimensions={2}, use_global_device_ids=true | all-gather | bytes 1105920 | tf_op jit(solution)/shard_map/all_gather | solution.py:216
  106.2 2.2 concatenate.80
  108.4 3.2 fusion.35
  111.6 3.0 concatenate.79
  114.6 2.5 convolution_convert_fusion.3
  122.9 4.6 copy.296
  127.5 8.7 %reshape.369 = bf16[32,49,1152]{2,0,1:T(8,128)(2,1)} reshape(bf16[8,2,2,7,7,1152]{5,2,1,0,4,3:T(2,128)(2,1)} %copy.296) | data formatting | bytes 7225344 | tf_op jit(solution)/shard_map/while/body/eval_jaxpr/reshape | solution.py:49
  136.2 3.9 fusion.89
  140.1 4.3 copy.301
  144.4 4.4 copy.300
  148.8 3.2 copy.297
  152.3 6.1 fusion.90
  158.5 3.6 fusion
  163.3 3.7 convert_bitcast_fusion.1
  167.0 9.2 %copy.304 = bf16[32,49,12,32]{3,2,0,1:T(8,128)(2,1)} copy(bf16[32,49,12,32]{1,3,2,0:T(8,128)(2,1)} %convert_bitcast_fusion.1) | data formatting | bytes 2408448 | tf_op jit(solution)/shard_map/while/body/eval_jaxpr/convert_element_type | solution.py:120
  176.2 8.3 reshape.374
  185.1 5.1 all-gather.2
  190.3 30.5 %all_gather.37 = bf16[96,384]{0,1:T(8,128)(2,1)S(1)} all-gather(bf16[96,48]{0,1:T(8,128)(2,1)S(1)} %convert_element_type.141), channel_id=1, replica_groups=mesh['dp'=8,'head'=4] {'dp'}, dimensions={1}, use_global_device_ids=true | all-gather | bytes 82944 | tf_op jit(solution)/shard_map/all_gather | solution.py:207
  222.6 5.9 all_gather.38
  228.4 2.4 fusion.91
  232.9 26.0 %fusion.3 = (bf16[1568,1536]{1,0:T(8,128)(2,1)S(1)}, f32[1568,1536]{1,0:T(8,128)}) fusion(f32[1536]{0:T(1024)S(1)} %reshape.391, bf16[384,1536]{1,0:T(8,128)(2,1)} %all-gather.6.cloned.1.call-done, f32[1568,384]{1,0:T(8,128)} %copy-done.6, f32[384]{0:T(512)S(1)} %get-tuple-element.209, f32[384]{0:T(512)S(1)} %get-tuple-element.210, ...), kind=kOutput, calls=%fused_computation.12 | convolution fusion | flops 2011656192 | bytes 18060544 | tf_op jit(solution)/shard_map/dot_general | solution.py:254
  258.9 2.2 copy-done.67
  261.1 4.0 convolution_convert_fusion
  265.2 25.7 %reduce-scatter.23.cloned.1.call-done = bf16[384,384]{1,0:T(8,128)(2,1)} async-done(((bf16[1536,384]{1,0:T(8,128)(2,1)}), bf16[384,384]{1,0:T(8,128)(2,1)}) %reduce-scatter.23.cloned.1.call-update) | async-done | bytes 294928 | tf_op jit(solution)/shard_map/reduce_scatter | solution.py:333
  292.9 64.3 %reduce-scatter.29.cloned.1.call-done = f32[48,384]{1,0:T(8,128)} async-done(((f32[384,384]{1,0:T(8,128)}), f32[48,384]{1,0:T(8,128)}) %reduce-scatter.29.cloned.1.call-update) | async-done | bytes 73744
  358.8 32.8 %all_gather.42 = bf16[384,384]{0,1:T(8,128)(2,1)} all-gather(bf16[384,48]{0,1:T(8,128)(2,1)S(1)} %get-tuple-element.253), channel_id=1, replica_groups=mesh['dp'=8,'head'=4] {'dp'}, dimensions={1}, use_global_device_ids=true | all-gather | bytes 331776 | tf_op jit(solution)/shard_map/all_gather | solution.py:209
  391.7 16.5 %all-gather.8.cloned.1.call-done = bf16[1536,384]{0,1:T(8,128)(2,1)} async-done(((bf16[384,384]{0,1:T(8,128)(2,1)}), bf16[1536,384]{0,1:T(8,128)(2,1)}) %all-gather.8.cloned.1.call-update) | async-done | bytes 1179664 | tf_op jit(solution)/shard_map/all_gather | solution.py:219
  408.2 9.1 %fusion.92 = (bf16[1536]{0:T(1024)(128)(2,1)S(1)}, bf16[1568,1536]{1,0:T(8,128)(2,1)S(1)}) fusion(f32[1568,1536]{1,0:T(8,128)} %get-tuple-element.259, bf16[1568,384]{1,0:T(8,128)(2,1)S(1)} %copy-done.22, bf16[1536,384]{0,1:T(8,128)(2,1)} %all-gather.8.cloned.1.call-done), kind=kOutput, calls=%fused_computation.201 | convolution fusion | flops 1876179456 | bytes 16837632 | tf_op jit(solution)/shard_map/dot_general | solution.py:261
  417.4 3.1 multiply_reduce_fusion.1
  425.5 3.1 reshape.377
  433.1 6.3 reshape.379
  439.4 8.7 %copy.310 = bf16[32,49,12,32]{1,3,2,0:T(8,128)(2,1)S(1)} copy(bf16[32,49,12,32]{3,2,0,1:T(8,128)(2,1)} %reshape.379) | data formatting | bytes 2408448 | tf_op jit(solution)/shard_map/while/body/eval_jaxpr/reshape;while/body/eval_jaxpr/reshape | solution.py:132
  448.1 8.9 %convert_bitcast_fusion = bf16[32,49,12,32]{1,3,2,0:T(8,128)(2,1)} fusion(bf16[32,49,12,32]{1,3,2,0:T(8,128)(2,1)S(1)} %copy.310, f32[32,12,49,49]{2,3,1,0:T(8,128)} %copy-done, f32[32,12,49]{2,1,0:T(8,128)S(1)} %log_add_fusion), kind=kOutput, calls=%fused_computation.59 | convolution fusion | flops 61453056 | bytes 6171648 | tf_op jit(solution)/shard_map/while/body/eval_jaxpr/whqk,wqhd->wkhd/dot_general | solution.py:137
  457.1 8.7 %multiply_reduce_fusion = (f32[32,12,49]{2,1,0:T(8,128)S(1)}, f32[32,12,49,49]{2,3,1,0:T(8,128)}) fusion(f32[32,12,49,49]{2,3,1,0:T(8,128)} %copy-done, f32[32,12,49]{2,1,0:T(8,128)S(1)} %log_add_fusion, bf16[32,49,12,32]{1,3,2,0:T(8,128)(2,1)S(1)} %copy.310, bf16[32,49,12,32]{1,3,2,0:T(8,128)(2,1)S(1)} %bitcast.137), kind=kOutput, calls=%fused_computation.4 | convolution fusion | flops 61754112 | bytes 9934848 | tf_op jit(solution)/shard_map/while/body/eval_jaxpr/wqhd,wkhd->whqk/dot_general | solution.py:133
  465.8 10.2 %convert_reduce_fusion = (f32[12,49,49]{1,2,0:T(8,128)}, bf16[32,12,49,49]{2,3,1,0:T(8,128)(2,1)S(1)}) fusion(f32[32,12,49,49]{2,3,1,0:T(8,128)} %get-tuple-element.262, f32[32,12,49]{2,1,0:T(8,128)S(1)} %get-tuple-element.261, f32[32,12,49,49]{2,3,1,0:T(8,128)} %copy-done, f32[32,12,49]{2,1,0:T(8,128)S(1)} %log_add_fusion), kind=kLoop, calls=%fused_computation.2 | loop fusion | flops 5503092 | bytes 9485616 | tf_op jit(solution)/shard_map/while/body/eval_jaxpr/reduce_sum | solution.py:155
  476.0 3.1 fusion.26
  479.1 3.1 fusion.25
  482.2 9.0 %copy.317 = bf16[32,49,12,32]{3,2,0,1:T(8,128)(2,1)} copy(bf16[32,49,12,32]{1,3,2,0:T(8,128)(2,1)} %convert_bitcast_fusion) | data formatting | bytes 2408448 | tf_op jit(solution)/shard_map/while/body/eval_jaxpr/whqk,wqhd->wkhd/transpose | solution.py:137
  491.2 9.1 %concatenate.92 = bf16[8,2,2,7,7,384]{5,2,1,0,4,3:T(2,128)(2,1)} reshape(bf16[32,49,12,32]{3,2,0,1:T(8,128)(2,1)} %copy.317) | data formatting | bytes 2408448 | tf_op jit(solution)/shard_map/while/body/eval_jaxpr/concatenate | solution.py:147
  500.3 9.0 %copy.312 = bf16[32,49,12,32]{3,2,0,1:T(8,128)(2,1)} copy(bf16[32,49,12,32]{1,3,2,0:T(8,128)(2,1)} %fusion.25) | data formatting | bytes 2408448 | tf_op jit(solution)/shard_map/while/body/eval_jaxpr/mul | solution.py:139
  509.3 9.3 %concatenate.90 = bf16[8,2,2,7,7,384]{5,2,1,0,4,3:T(2,128)(2,1)} reshape(bf16[32,49,12,32]{3,2,0,1:T(8,128)(2,1)} %copy.312) | data formatting | bytes 2408448 | tf_op jit(solution)/shard_map/while/body/eval_jaxpr/concatenate | solution.py:147
  518.6 8.8 %copy.314 = bf16[32,49,12,32]{3,2,0,1:T(8,128)(2,1)} copy(bf16[32,49,12,32]{1,3,2,0:T(8,128)(2,1)S(1)} %fusion.26) | data formatting | bytes 2408448 | tf_op jit(solution)/shard_map/while/body/eval_jaxpr/mul | solution.py:143
  527.4 9.2 %concatenate.91 = bf16[8,2,2,7,7,384]{5,2,1,0,4,3:T(2,128)(2,1)} reshape(bf16[32,49,12,32]{3,2,0,1:T(8,128)(2,1)} %copy.314) | data formatting | bytes 2408448 | tf_op jit(solution)/shard_map/while/body/eval_jaxpr/concatenate | solution.py:147
  536.6 4.3 maximum_bitcast_fusion
  542.6 2.3 fusion.24
  544.9 2.6 copy.319
  547.5 10.5 %reshape_reshape.3 = bf16[1568,3,384]{2,1,0:T(4,128)(2,1)} reshape(bf16[8,14,14,1152]{3,2,1,0:T(8,128)(2,1)} %copy.319) | data formatting | bytes 7225344 | tf_op jit(solution)/shard_map/reshape;reshape | solution.py:305
  558.1 5.6 fusion.56
  563.8 6.7 reshape.381
  573.4 5.9 convolution_convert_fusion.1
  579.4 2.6 copy.341
  585.2 6.5 fusion.48
  591.8 2.3 fusion.47
  595.8 6.9 fusion.37
  603.5 39.8 %psum.31 = f32[6,384]{1,0:T(8,128)S(1)} all-reduce(f32[6,384]{1,0:T(8,128)S(1)} %stack.42), channel_id=1, replica_groups=mesh['dp'=8,'head'=4] {'dp','head'}, use_global_device_ids=true, to_apply=%region_35.36 | all-reduce | flops 2304 | bytes 18432 | tf_op jit(solution)/shard_map/psum | solution.py:353
  644.2 10.9 %all-reduce.4 = (bf16[1536]{0:T(1024)(128)(2,1)S(1)}, bf16[169,12]{0,1:T(8,128)(2,1)S(1)}) all-reduce(bf16[1536]{0:T(1024)(128)(2,1)S(1)} %get-tuple-element.264, bf16[169,12]{0,1:T(8,128)(2,1)S(1)} %fusion.63), channel_id=11, replica_groups=mesh['dp'=8,'head'=4] {'head'}, use_global_device_ids=true, to_apply=%region_24.25.clone | all-reduce | flops 3564 | bytes 14256
  658.7 21.0 %all-reduce.3 = (f32[2,96]{1,0:T(2,128)S(1)}, f32[384]{0:T(512)S(1)}, f32[169,3]{0,1:T(4,128)S(1)}) all-reduce(bf16[2,96]{1,0:T(2,128)(2,1)S(1)} %copy.346, f32[384]{0:T(512)S(1)} %dynamic-slice_convert_fusion.1, f32[169,3]{0,1:T(4,128)S(1)} %dynamic-slice_convert_fusion), channel_id=1, replica_groups=mesh['dp'=8,'head'=4] {'dp'}, use_global_device_ids=true, to_apply=%region_22.23 | all-reduce | flops 1083 | bytes 8280 | tf_op jit(solution)/shard_map/psum | solution.py:352
  683.7 21.2 %reduce-scatter.25.cloned.1.call-done = f32[48,96]{1,0:T(8,128)} async-done(((f32[384,96]{1,0:T(8,128)}), f32[48,96]{1,0:T(8,128)}) %reduce-scatter.25.cloned.1.call-update) | async-done | bytes 18448
  706.2 76.0 %all-reduce.7.cloned.1.call-done = f32[3,384,96]{2,0,1:T(4,128)} async-done(((f32[3,384,96]{2,0,1:T(4,128)}), f32[3,384,96]{2,0,1:T(4,128)}) %all-reduce.7.cloned.1.call-update) | async-done | bytes 442384
  783.9 62.9 %reduce-scatter.21.cloned.1.call-done = f32[48,384]{1,0:T(8,128)} async-done(((f32[384,384]{1,0:T(8,128)}), f32[48,384]{1,0:T(8,128)}) %reduce-scatter.21.cloned.1.call-update) | async-done | bytes 73744 | tf_op jit(solution)/shard_map/reduce_scatter | solution.py:349
  (275 shorter events, 59.5 us)
Async XLA Ops:
  7.2 50.1 %copy-start.1 = (bf16[1568,384]{1,0:T(8,128)(2,1)S(1)}, bf16[1568,384]{1,0:T(8,128)(2,1)}, u32[]{:S(2)}) copy-start(bf16[1568,384]{1,0:T(8,128)(2,1)} %param.27) | copy-start | bytes 3612676
  7.2 50.8 %copy-start.42 = (f32[6,384]{1,0:T(8,128)S(1)}, f32[6,384]{1,0:T(8,128)}, u32[]{:S(2)}) copy-start(f32[6,384]{1,0:T(8,128)} %param.37) | copy-start | bytes 27652
  7.2 51.9 %copy-start.26 = (f32[3,48,96]{2,1,0:T(8,128)S(1)}, f32[3,48,96]{2,1,0:T(8,128)}, u32[]{:S(2)}) copy-start(f32[3,48,96]{2,1,0:T(8,128)} %param.30) | copy-start | bytes 165892
  7.2 225.6 %all-gather.6.cloned.1.call-start = ((), (), s32[]{:S(2)}) async-start(), calls=%async_computation.8 | async-start | bytes 1474560 | tf_op jit(solution)/shard_map/all_gather | solution.py:218
  42.9 248.0 %reduce-scatter.23.cloned.1.call-start = ((), (), s32[]{:S(2)}) async-start(), calls=%async_computation.13 | async-start | bytes 1474560 | tf_op jit(solution)/shard_map/reduce_scatter | solution.py:333
  57.3 45.4 %copy-start.29 = (f32[1568]{0:T(1024)}, f32[1568]{0:T(1024)S(1)}, u32[]{:S(2)}) copy-start(f32[1568]{0:T(1024)S(1)} %broadcast_multiply_fusion.5) | copy-start | bytes 18820
  58.1 44.7 %copy-start.40 = (f32[1568]{0:T(1024)}, f32[1568]{0:T(1024)S(1)}, u32[]{:S(2)}) copy-start(f32[1568]{0:T(1024)S(1)} %add_rsqrt_fusion.1) | copy-start | bytes 18820
  58.7 44.1 %copy-start.46 = (f32[384]{0:T(512)}, f32[384]{0:T(512)S(1)}, u32[]{:S(2)}) copy-start(f32[384]{0:T(512)S(1)} %get-tuple-element.213) | copy-start | bytes 4612
  102.2 12.4 %copy-start.18 = (bf16[3,384,384]{1,2,0:T(8,128)(2,1)}, bf16[3,384,384]{1,2,0:T(8,128)(2,1)S(1)}, u32[]{:S(2)}) copy-start(bf16[3,384,384]{1,2,0:T(8,128)(2,1)S(1)} %all_gather.34) | copy-start | bytes 2654212
  158.5 4.8 copy-start
  158.5 4.8 copy-start.11
  162.1 4.9 copy-start.24
  184.4 5.9 copy-start.31
  232.9 28.2 %copy-start.22 = (bf16[1568,384]{1,0:T(8,128)(2,1)S(1)}, bf16[1568,384]{1,0:T(8,128)(2,1)}, u32[]{:S(2)}) copy-start(bf16[1568,384]{1,0:T(8,128)(2,1)} %param.29) | copy-start | bytes 3612676
  261.1 96.1 %copy-start.33 = (f32[384,48]{0,1:T(8,128)S(1)}, f32[384,48]{0,1:T(8,128)}, u32[]{:S(2)}) copy-start(f32[384,48]{0,1:T(8,128)} %param.33) | copy-start | bytes 221188
  261.1 96.1 %copy-start.34 = (f32[384,48]{0,1:T(8,128)S(1)}, f32[384,48]{0,1:T(8,128)}, u32[]{:S(2)}) copy-start(f32[384,48]{0,1:T(8,128)} %param.44) | copy-start | bytes 221188
  261.1 96.1 %copy-start.35 = (f32[384,48]{0,1:T(8,128)S(1)}, f32[384,48]{0,1:T(8,128)}, u32[]{:S(2)}) copy-start(f32[384,48]{0,1:T(8,128)} %param.45) | copy-start | bytes 221188
  265.1 126.6 %copy-start.25 = (f32[32,12,49]{2,1,0:T(8,128)S(1)}, f32[32,12,49]{2,1,0:T(8,128)}, u32[]{:S(2)}) copy-start(f32[32,12,49]{2,1,0:T(8,128)} %copy-done.24) | copy-start | bytes 225796
  265.1 92.1 %reduce-scatter.29.cloned.1.call-start = ((), (), s32[]{:S(2)}) async-start(), calls=%async_computation.16 | async-start | bytes 663552
  292.8 115.4 %all-gather.8.cloned.1.call-start = ((), (), s32[]{:S(2)}) async-start(), calls=%async_computation.9 | async-start | bytes 1474560 | tf_op jit(solution)/shard_map/all_gather | solution.py:219
  391.6 202.5 %reduce-scatter.19.cloned.1.call-start = ((), (), s32[]{:S(2)}) async-start(), calls=%async_computation.11 | async-start | bytes 368640 | tf_op jit(solution)/shard_map/reduce_scatter | solution.py:327
  408.2 9.1 %copy-start.7 = (f32[1568,384]{1,0:T(8,128)S(1)}, f32[1568,384]{1,0:T(8,128)}, u32[]{:S(2)}) copy-start(f32[1568,384]{1,0:T(8,128)} %copy-done.6) | copy-start | bytes 7225348
  408.2 9.1 %copy-start.63 = (bf16[384,1536]{1,0:T(8,128)(2,1)S(1)}, bf16[384,1536]{1,0:T(8,128)(2,1)}, u32[]{:S(2)}) copy-start(bf16[384,1536]{1,0:T(8,128)(2,1)} %all-gather.6.cloned.1.call-done) | copy-start | bytes 3538948
  448.1 8.9 %copy-start.12 = (bf16[32,49,384]{1,2,0:T(8,128)(2,1)S(1)}, bf16[32,49,384]{1,2,0:T(8,128)(2,1)}, u32[]{:S(2)}) copy-start(bf16[32,49,384]{1,2,0:T(8,128)(2,1)} %copy.297) | copy-start | bytes 3612676
  465.8 10.2 %copy-start.4 = (bf16[32,49,384]{1,2,0:T(8,128)(2,1)S(1)}, bf16[32,49,384]{1,2,0:T(8,128)(2,1)}, u32[]{:S(2)}) copy-start(bf16[32,49,384]{1,2,0:T(8,128)(2,1)} %copy.300) | copy-start | bytes 3612676
  527.4 9.2 %copy-start.13 = (bf16[8,2,2,7,7,384]{5,2,1,0,4,3:T(2,128)(2,1)S(1)}, bf16[8,2,2,7,7,384]{5,2,1,0,4,3:T(2,128)(2,1)}, u32[]{:S(2)}) copy-start(bf16[8,2,2,7,7,384]{5,2,1,0,4,3:T(2,128)(2,1)} %concatenate.92) | copy-start | bytes 3612676
  527.4 9.2 %copy-start.14 = (bf16[8,2,2,7,7,384]{5,2,1,0,4,3:T(2,128)(2,1)S(1)}, bf16[8,2,2,7,7,384]{5,2,1,0,4,3:T(2,128)(2,1)}, u32[]{:S(2)}) copy-start(bf16[8,2,2,7,7,384]{5,2,1,0,4,3:T(2,128)(2,1)} %concatenate.90) | copy-start | bytes 3612676
  542.6 112.5 %reduce-scatter.17.cloned.1.call-start = ((), (), s32[]{:S(2)}) async-start(), calls=%async_computation.10 | async-start | bytes 1105920 | tf_op jit(solution)/shard_map/reduce_scatter | solution.py:324
  547.5 10.5 %copy-start.16 = (bf16[1568,384]{1,0:T(8,128)(2,1)S(1)}, bf16[1568,384]{1,0:T(8,128)(2,1)}, u32[]{:S(2)}) copy-start(bf16[1568,384]{1,0:T(8,128)(2,1)} %copy-done.15) | copy-start | bytes 3612676
  563.7 9.7 %copy-start.8 = (f32[1568,384]{1,0:T(8,128)S(1)}, f32[1568,384]{1,0:T(8,128)}, u32[]{:S(2)}) copy-start(f32[1568,384]{1,0:T(8,128)} %copy-done.6) | copy-start | bytes 7225348
  563.7 94.2 %reduce-scatter.31.cloned.1.call-start = ((), (), s32[]{:S(2)}) async-start(), calls=%async_computation.17 | async-start | bytes 122880
  573.4 106.4 %reduce-scatter.27.cloned.1.call-start = ((), (), s32[]{:S(2)}) async-start(), calls=%async_computation.15 | async-start | bytes 1474560
  579.3 5.8 copy-start.2
  579.4 5.8 copy-start.19
  579.4 5.8 copy-start.30
  579.4 5.8 copy-start.41
  579.4 5.8 copy-start.47
  582.0 122.9 %reduce-scatter.25.cloned.1.call-start = ((), (), s32[]{:S(2)}) async-start(), calls=%async_computation.14 | async-start | bytes 221184
  585.2 6.6 copy-start.10
  595.8 186.5 %all-reduce.7.cloned.1.call-start = ((), (), s32[]{:S(2)}) async-start(), calls=%async_computation.18 | async-start | bytes 1572864
  595.8 7.2 copy-start.20
  595.8 47.5 %copy-start.50 = (s32[2401]{0:T(1024)S(1)}, s32[2401]{0:T(1024)}, u32[]{:S(2)}) copy-start(s32[2401]{0:T(1024)} %copy-done.49) | copy-start | bytes 28816
  602.8 54.5 %copy-start.43 = (f32[6,384]{1,0:T(8,128)S(1)}, f32[6,384]{1,0:T(8,128)}, u32[]{:S(2)}) copy-start(f32[6,384]{1,0:T(8,128)} %param.37) | copy-start | bytes 27652
  602.8 54.5 %copy-start.51 = (f32[6,384]{1,0:T(8,128)S(1)}, f32[6,384]{1,0:T(8,128)}, u32[]{:S(2)}) copy-start(f32[6,384]{1,0:T(8,128)} %param.52) | copy-start | bytes 27652
  602.8 54.5 %copy-start.52 = (f32[6,384]{1,0:T(8,128)S(1)}, f32[6,384]{1,0:T(8,128)}, u32[]{:S(2)}) copy-start(f32[6,384]{1,0:T(8,128)} %param.53) | copy-start | bytes 27652
  602.8 79.0 %copy-start.60 = (f32[2,96]{1,0:T(2,128)S(1)}, f32[2,96]{1,0:T(2,128)}, u32[]{:S(2)}) copy-start(f32[2,96]{1,0:T(2,128)} %param.34) | copy-start | bytes 2308
  602.8 79.0 %copy-start.61 = (f32[2,96]{1,0:T(2,128)S(1)}, f32[2,96]{1,0:T(2,128)}, u32[]{:S(2)}) copy-start(f32[2,96]{1,0:T(2,128)} %param.46) | copy-start | bytes 2308
  602.8 79.0 %copy-start.62 = (f32[2,96]{1,0:T(2,128)S(1)}, f32[2,96]{1,0:T(2,128)}, u32[]{:S(2)}) copy-start(f32[2,96]{1,0:T(2,128)} %param.47) | copy-start | bytes 2308
  602.8 79.6 %copy-start.54 = (f32[384]{0:T(512)S(1)}, f32[384]{0:T(512)}, u32[]{:S(2)}) copy-start(f32[384]{0:T(512)} %param.35) | copy-start | bytes 4612
  602.8 79.6 %copy-start.57 = (f32[384]{0:T(512)S(1)}, f32[384]{0:T(512)}, u32[]{:S(2)}) copy-start(f32[384]{0:T(512)} %param.48) | copy-start | bytes 4612
  602.9 79.6 %copy-start.58 = (f32[384]{0:T(512)S(1)}, f32[384]{0:T(512)}, u32[]{:S(2)}) copy-start(f32[384]{0:T(512)} %param.49) | copy-start | bytes 4612
  602.9 80.2 %copy-start.48 = (f32[169,3]{0,1:T(4,128)S(1)}, f32[169,3]{0,1:T(4,128)}, u32[]{:S(2)}) copy-start(f32[169,3]{0,1:T(4,128)} %param.36) | copy-start | bytes 6088
  602.9 80.2 %copy-start.55 = (f32[169,3]{0,1:T(4,128)S(1)}, f32[169,3]{0,1:T(4,128)}, u32[]{:S(2)}) copy-start(f32[169,3]{0,1:T(4,128)} %param.50) | copy-start | bytes 6088
  602.9 80.2 %copy-start.56 = (f32[169,3]{0,1:T(4,128)S(1)}, f32[169,3]{0,1:T(4,128)}, u32[]{:S(2)}) copy-start(f32[169,3]{0,1:T(4,128)} %param.51) | copy-start | bytes 6088
  602.9 102.0 %copy-start.32 = (f32[96,48]{0,1:T(8,128)S(1)}, f32[96,48]{0,1:T(8,128)}, u32[]{:S(2)}) copy-start(f32[96,48]{0,1:T(8,128)} %param.31) | copy-start | bytes 55300
  602.9 102.0 %copy-start.44 = (f32[96,48]{0,1:T(8,128)S(1)}, f32[96,48]{0,1:T(8,128)}, u32[]{:S(2)}) copy-start(f32[96,48]{0,1:T(8,128)} %param.40) | copy-start | bytes 55300
  602.9 101.9 %copy-start.45 = (f32[96,48]{0,1:T(8,128)S(1)}, f32[96,48]{0,1:T(8,128)}, u32[]{:S(2)}) copy-start(f32[96,48]{0,1:T(8,128)} %param.41) | copy-start | bytes 55300
  603.0 180.2 %copy-start.27 = (f32[3,48,96]{2,1,0:T(8,128)S(1)}, f32[3,48,96]{2,1,0:T(8,128)}, u32[]{:S(2)}) copy-start(f32[3,48,96]{2,1,0:T(8,128)} %param.30) | copy-start | bytes 165892
  603.0 180.2 %copy-start.36 = (f32[3,48,96]{2,1,0:T(8,128)S(1)}, f32[3,48,96]{2,1,0:T(8,128)}, u32[]{:S(2)}) copy-start(f32[3,48,96]{2,1,0:T(8,128)} %param.38) | copy-start | bytes 165892
  603.0 180.2 %copy-start.37 = (f32[3,48,96]{2,1,0:T(8,128)S(1)}, f32[3,48,96]{2,1,0:T(8,128)}, u32[]{:S(2)}) copy-start(f32[3,48,96]{2,1,0:T(8,128)} %param.39) | copy-start | bytes 165892
  603.2 243.6 %copy-start.28 = (f32[48,384]{1,0:T(8,128)S(1)}, f32[48,384]{1,0:T(8,128)}, u32[]{:S(2)}) copy-start(f32[48,384]{1,0:T(8,128)} %param.32) | copy-start | bytes 221188
  603.2 243.6 %copy-start.38 = (f32[48,384]{1,0:T(8,128)S(1)}, f32[48,384]{1,0:T(8,128)}, u32[]{:S(2)}) copy-start(f32[48,384]{1,0:T(8,128)} %param.42) | copy-start | bytes 221188
  603.3 243.6 %copy-start.39 = (f32[48,384]{1,0:T(8,128)S(1)}, f32[48,384]{1,0:T(8,128)}, u32[]{:S(2)}) copy-start(f32[48,384]{1,0:T(8,128)} %param.43) | copy-start | bytes 221188
  657.1 189.7 %reduce-scatter.21.cloned.1.call-start = ((), (), s32[]{:S(2)}) async-start(), calls=%async_computation.12 | async-start | bytes 663552 | tf_op jit(solution)/shard_map/reduce_scatter | solution.py:349
  (16 other events, 42.1 us)
Sparse Core Ops, SparseCore 0:
  43.0 18.4 all-gather.5
  265.2 25.5 reduce-scatter.22
  295.1 62.0 reduce-scatter.28
  391.7 16.4 all-gather.7
  542.7 20.2 reduce-scatter.18
  565.6 23.8 reduce-scatter.16
  591.9 19.5 reduce-scatter.30
  614.0 25.9 reduce-scatter.26
  643.6 61.2 reduce-scatter.24
  708.5 73.6 all-reduce.6
  785.5 61.2 reduce-scatter.20
where the time goes:
time: 862 us; the launch traced here: 855 us
  waiting for transfers between devices  267 us (31%)
  blocking collectives  231 us (27%)
  local copies, waits for them, and re-layouts  179 us (21%)
  matrix products  116 us (13%)
  other arithmetic  44.8 us (5%)
  between operations  17.4 us (2%)
    unnamed x16, waiting for transfers between devices  162 us
    reduce_scatter x1, waiting for transfers between devices, per_device(): lax.psum_scatter(expand_grad, 'dp', scatter_dimension=0, tiled=True)  62.9 us
    psum x1, blocking collectives, per_device(): norm_grad = lax.psum(norm_grad, ('dp', 'head'))  39.8 us
    all_gather x1, blocking collectives, per_device(): lax.all_gather(expand_weight.astype(jnp.bfloat16), 'dp', axis=0, tiled=True)  34.6 us
    all_gather x1, blocking collectives, per_device(): lax.all_gather(contract_weight.astype(jnp.bfloat16), 'dp', axis=1, tiled=...  32.8 us
    all_gather x1, blocking collectives, per_device(): lax.all_gather(query_key_value.astype(jnp.bfloat16), 'dp', axis=1, tiled=...  30.9 us
    all_gather x1, blocking collectives, per_device(): lax.all_gather(output_weight.astype(jnp.bfloat16), 'dp', axis=1, tiled=True)  30.5 us
    concatenate x3, local copies, waits for them, and re-layouts, attend_back(): jnp.concatenate([grad_query.reshape(flat_shape), grad_key.reshape(flat_sh...  27.6 us
  transfers between devices with their start and end apart: 11, of which 6 were waited for; matrix products, arithmetic and copies ran while one was open for 19% of the time, Pallas kernels for 0%

commit v1 on v0

v1 whole, which is shorter than its diff:
```python
import functools
import math

import jax
import jax.numpy as jnp
import numpy as np
from jax import lax
from jax.experimental import pallas as pl
from jax.experimental.pallas import tpu as pltpu
from jax.sharding import PartitionSpec as P

HEAD_DIM = 32
WINDOW = 7
SIDE = 14
SHIFT = 3
STEP = 10
CANVAS = SIDE * SIDE
PLACES = WINDOW * WINDOW
SLOT = 64
QUAD_ROWS = 4 * CANVAS
SPAN = 208
WIDTH = 384
GROUPS = 3
PACK = 4
HIDDEN = 1536
CHUNK = 512

NORM_EPS = 1e-05
BETA_ONE = 0.9
BETA_TWO = 0.999
ADAM_EPS = 1e-08
RATE_MATRIX = 0.1
RATE_SMALL = 0.5
DECAY_MATRIX = 0.05
MASKED = -1e30
LOG2E = math.log2(math.e)
SCALE = HEAD_DIM**-0.5
ROOT_HALF = 0.7071067811865476
INV_ROOT_TWO_PI = 1.0 / 2.5066282746310002
BF = jnp.bfloat16
F32 = jnp.float32


def slot_rows():
    rows = -np.ones((4, SLOT), np.int64)
    for win in range(4):
        for place in range(PLACES):
            row = (win // 2) * WINDOW + place // WINDOW
            col = (win % 2) * WINDOW + place % WINDOW
            rows[win, place] = ((row + SHIFT) % SIDE) * SIDE + (col + SHIFT) % SIDE
    return rows.reshape(-1)


def permutations():
    rows = slot_rows()
    to_slots = np.zeros((4, 4 * SLOT, SPAN), np.float32)
    for i in range(4):
        for slot, row in enumerate(rows):
            if row >= 0:
                to_slots[i, slot, 4 * i + row] = 1.0
    return to_slots, to_slots.transpose(0, 2, 1).copy()


def region_codes():
    def band(v):
        return 0 if v < SIDE - WINDOW else (1 if v < SIDE - SHIFT else 2)

    codes = np.full((4, SLOT), 999.0, np.float32)
    for win in range(4):
        for place in range(PLACES):
            row = (win // 2) * WINDOW + place // WINDOW
            col = (win % 2) * WINDOW + place % WINDOW
            codes[win, place] = 4 * (3 * band(row) + band(col))
    return codes.reshape(-1)


def pair_onehot(rows):
    out = np.zeros((rows, SLOT, SLOT), np.float32)
    for key in range(PLACES):
        for query in range(PLACES):
            up = query // WINDOW - key // WINDOW + WINDOW - 1
            side = query % WINDOW - key % WINDOW + WINDOW - 1
            out[up * (2 * WINDOW - 1) + side, key, query] = 1.0
    return out


def dot_nn(a, b):
    return jnp.dot(a, b, preferred_element_type=F32)


def dot_nt(a, b):
    return lax.dot_general(a, b, (((1,), (1,)), ((), ())), preferred_element_type=F32)


def stats(values):
    centred = values - jnp.mean(values, axis=-1, keepdims=True)
    inv_std = lax.rsqrt(jnp.mean(centred * centred, axis=-1, keepdims=True) + NORM_EPS)
    return centred * inv_std, inv_std


def norm_back(grad_norm, hat, inv_std, gain_row):
    grad_hat = grad_norm * gain_row
    inner = grad_hat - jnp.mean(grad_hat, axis=-1, keepdims=True)
    return inv_std * (inner - hat * jnp.mean(grad_hat * hat, axis=-1, keepdims=True))


def owners(idx):
    z, y, x, c = idx[0], idx[1], idx[2], idx[3]
    for e in range(2):
        for k in range(4):
            for s in range(4):
                row = ((z ^ s) * 2 + (y ^ (k >> 1))) * 48
                yield e, k, s, pl.multiple_of(row, 16), (x ^ (k & 1)) * 2 + (c ^ e)


def spread(block):
    four = jnp.concatenate([block] * PACK, axis=1)
    rows = lax.broadcasted_iota(jnp.int32, four.shape, 0) // HEAD_DIM
    lanes = lax.broadcasted_iota(jnp.int32, four.shape, 1) // SLOT
    return jnp.where(rows == lanes, four, jnp.zeros_like(four))


def attention_forward(
    idx, p0, p1, p2, p3, p4, p5, p6, p7, tok, quad, ut, u, reg_row, reg_col, bias, tb, par,
    mrg, qt, kt, vv, pt, mt, n1t, wnat, outt, wout,
    wbuf, waug, wt, n1aug, vt,
):
    step = pl.program_id(0)

    @pl.when(step == 0)
    def _():
        refs = (p0, p1, p2, p3, p4, p5, p6, p7)
        for e, k, s, row, head in owners(idx):
            wbuf[head, pl.ds(row, 48), :] = refs[e * 4 + k][s * 48 : (s + 1) * 48, :]
        for j in range(3):
            waug[0:WIDTH, j * WIDTH : (j + 1) * WIDTH] = jnp.concatenate(
                [wbuf[h, :, 96 * j : 96 * (j + 1)] for h in range(4)], axis=1
            )
        out_t = jnp.concatenate([wbuf[h, :, 288:384] for h in range(4)], axis=1)
        outt[...] = out_t
        wout[...] = out_t.T
        waug[WIDTH : WIDTH + 16, :] = bias[...]
        waug[WIDTH + 16 : 512, :] = jnp.zeros((112, 3 * WIDTH), BF)
        wnat[...] = waug[0:WIDTH, :]
        wt[...] = waug[...].T
        lane = lax.broadcasted_iota(jnp.int32, (4 * SLOT, 128), 1)
        n1aug[:, WIDTH:512] = jnp.where(lane == 0, 1.0, 0.0).astype(BF)

    start = pl.multiple_of((step // 4) * QUAD_ROWS + (step % 4) * 192, 16)
    hat, _ = stats(tok[pl.ds(start, SPAN), :].astype(F32))
    n1 = (hat * par[0:1, :] + par[1:2, :]).astype(BF)
    n1aug[:, 0:WIDTH] = dot_nn(ut[0], n1).astype(BF)
    na = n1aug[...]
    n1t[0] = na.T[0:400, :]
    all_t = dot_nt(wt[...], na).astype(BF)
    qt[0] = all_t[0:WIDTH]
    kt[0] = all_t[WIDTH : 2 * WIDTH]
    vt[...] = all_t[2 * WIDTH :]
    kv = dot_nt(na, wt[WIDTH:, :]).astype(BF)
    vv[0] = kv[:, WIDTH:]
    code_row = dot_nt(quad[0], ut[0]) + reg_row[...]
    code_col = dot_nt(ut[0], quad[0]) + reg_col[...]
    for win in range(4):
        lo, hi = win * SLOT, (win + 1) * SLOT
        same = code_col[lo:hi, 0:1] == jnp.concatenate([code_row[0:1, lo:hi]] * PACK, axis=1)
        mask = jnp.where(same, 0.0, MASKED)
        for g in range(GROUPS):
            fa, fb = g * 128, (g + 1) * 128
            scores = dot_nn(kv[lo:hi, fa:fb], spread(qt[0, fa:fb, lo:hi]))
            scores = scores * (SCALE * LOG2E) + (tb[g] + mask)
            top = jnp.max(scores, axis=0, keepdims=True)
            grown = jnp.exp2(scores - top)
            probs = (grown * (1.0 / jnp.sum(grown, axis=0, keepdims=True))).astype(BF)
            pt[0, win * GROUPS + g] = probs
            mixed = dot_nn(vt[fa:fb, lo:hi], probs)
            for h in range(PACK):
                r = fa + h * HEAD_DIM
                mt[0, r : r + HEAD_DIM, lo:hi] = mixed[
                    h * HEAD_DIM : (h + 1) * HEAD_DIM, h * SLOT : (h + 1) * SLOT
                ].astype(BF)
    back = dot_nt(u[0], mt[0]).astype(BF)

    @pl.when(step % 4 == 0)
    def _():
        mrg[pl.ds(start, 16), :] = back[0:16]

    @pl.when(step % 4 != 0)
    def _():
        mrg[pl.ds(start, 16), :] = mrg[pl.ds(start, 16), :] + back[0:16]

    mrg[pl.ds(pl.multiple_of(start + 16, 16), SPAN - 16), :] = back[16:]


def mlp(
    idx, p0, p1, p2, p3, p4, p5, p6, p7, tok, gout, mrg, outt, eb, par,
    blk, gmid, keep, send, sums, ebg,
    eaug, ct, n2, mid, n2t, got, hid, gpr, acc_m, acc_g, cg, eg,
):
    step = pl.program_id(0)
    last = pl.num_programs(0) - 1
    rows_all = tok.shape[0]
    tile = 224
    tiles = rows_all // tile

    @pl.when(step == 0)
    def _():
        refs = (p0, p1, p2, p3, p4, p5, p6, p7)
        for e, k, s, row, head in owners(idx):
            lanes = pl.ds(pl.multiple_of(head * WIDTH, 128), WIDTH)
            eaug[pl.ds(row, 48), lanes] = refs[e * 4 + k][s * 48 : (s + 1) * 48, 0:WIDTH]
            ct[pl.ds(row, 48), lanes] = refs[e * 4 + k][s * 48 : (s + 1) * 48, WIDTH:]
        eaug[WIDTH : WIDTH + 16, :] = eb[...]
        eaug[WIDTH + 16 : 512, :] = jnp.zeros((112, HIDDEN), BF)
        lane = lax.broadcasted_iota(jnp.int32, (tile, 128), 1)
        ones = jnp.where(lane == 0, 1.0, 0.0).astype(BF)

        def head_rows(t, carry):
            rows = pl.ds(pl.multiple_of(t * tile, 16), tile)
            attn = dot_nt(mrg[rows, :], outt[...])
            middle = tok[rows, :].astype(F32) + attn + par[4:5, :]
            mid[rows, :] = middle
            hat, _ = stats(middle)
            n2[rows, 0:WIDTH] = (hat * par[2:3, :] + par[3:4, :]).astype(BF)
            n2[rows, WIDTH:512] = ones
            acc_m[rows, :] = jnp.zeros((tile, WIDTH), F32)
            acc_g[rows, :] = jnp.zeros((tile, WIDTH), F32)
            return carry

        lax.fori_loop(0, tiles, head_rows, 0)
        n2t[...] = n2[...].T[0:400, :]
        got[...] = gout[...].T

    cols = pl.ds(pl.multiple_of(step * CHUNK, 128), CHUNK)

    def unit_rows(t, carry):
        rows = pl.ds(pl.multiple_of(t * tile, 16), tile)
        pre = dot_nn(n2[rows, :], eaug[:, cols])
        grad_hidden = dot_nn(gout[rows, :], ct[:, cols])
        phi = 0.5 + 0.5 * lax.erf(pre * ROOT_HALF)
        bell = jnp.exp2(pre * pre * (-0.5 * LOG2E)) * INV_ROOT_TWO_PI
        hidden = (pre * phi).astype(BF)
        grad_pre = (grad_hidden * (phi + pre * bell)).astype(BF)
        hid[rows, :] = hidden
        gpr[rows, :] = grad_pre
        acc_m[rows, :] += dot_nt(hidden, ct[:, cols])
        acc_g[rows, :] += dot_nt(grad_pre, eaug[0:WIDTH, cols])
        return carry

    lax.fori_loop(0, tiles, unit_rows, 0)
    cg[:, cols] = dot_nn(got[...], hid[...]).astype(BF)
    grads = dot_nn(n2t[...], gpr[...])
    eg[:, cols] = grads[0:WIDTH].astype(BF)
    ebg[:, cols] = grads[WIDTH : WIDTH + 8]

    @pl.when(step == last)
    def _():
        for e, k, s, row, head in owners(idx):
            dst = (keep, send)[e]
            lanes = pl.ds(pl.multiple_of(head * WIDTH, 128), WIDTH)
            base = (k * 4 + s) * 48
            dst[base : base + 48, 0:WIDTH] = eg[pl.ds(row, 48), lanes]
            dst[base : base + 48, WIDTH:] = cg[pl.ds(row, 48), lanes]

        def tail_rows(t, carry):
            rows = pl.ds(pl.multiple_of(t * tile, 16), tile)
            middle = mid[rows, :]
            blk[rows, :] = (middle + acc_m[rows, :] + par[5:6, :]).astype(BF)
            hat, inv = stats(middle)
            g = acc_g[rows, :]
            top = gout[rows, :].astype(F32)
            grad_mid = top + norm_back(g, hat, inv, par[2:3, :])
            gmid[rows, :] = grad_mid
            parts = (g * hat, g, grad_mid, top)
            return tuple(c + jnp.sum(p, axis=0, keepdims=True) for c, p in zip(carry, parts))

        zero = jnp.zeros((1, WIDTH), F32)
        totals = lax.fori_loop(0, tiles, tail_rows, (zero,) * 4)
        sums[...] = jnp.concatenate([zero, zero, *totals, zero, zero], axis=0)


def attention_backward(
    idx, tok, gmid, qt, kt, vv, pt, mt, n1t, wnat, wout, ut, u, par, sums_in,
    gtok, keep, send, table,
    gtall, ntall, wacc, oacc, csum, gt,
):
    step = pl.program_id(0)
    last = pl.num_programs(0) - 1

    @pl.when(step == 0)
    def _():
        table[...] = jnp.zeros(table.shape, F32)
        oacc[...] = jnp.zeros(oacc.shape, F32)
        wacc[...] = jnp.zeros(wacc.shape, F32)
        csum[...] = sums_in[...]

    start = pl.multiple_of((step // 4) * QUAD_ROWS + (step % 4) * 192, 16)
    rows = pl.ds(start, SPAN)
    grad_mid = gmid[rows, :]
    gmw = dot_nn(ut[0], grad_mid.astype(BF)).astype(BF)
    gmt = dot_nt(wout[...], gmw).astype(BF)
    oacc[...] += dot_nn(mt[0], gmw)
    for win in range(4):
        lo, hi = win * SLOT, (win + 1) * SLOT
        for g in range(GROUPS):
            fa, fb = g * 128, (g + 1) * 128
            gm_s = spread(gmt[fa:fb, lo:hi])
            q_s = spread(qt[0, fa:fb, lo:hi])
            probs_b = pt[0, win * GROUPS + g]
            probs = probs_b.astype(F32)
            gp = dot_nn(vv[0, lo:hi, fa:fb], gm_s)
            delta = jnp.sum(probs * gp, axis=0, keepdims=True)
            gs = (probs * (gp - delta)).astype(BF)
            table[g] += gs.astype(F32)
            gq = dot_nn(kt[0, fa:fb, lo:hi], gs) * SCALE
            for h in range(PACK):
                r = fa + h * HEAD_DIM
                gt[r : r + HEAD_DIM, lo:hi] = gq[
                    h * HEAD_DIM : (h + 1) * HEAD_DIM, h * SLOT : (h + 1) * SLOT
                ].astype(BF)
            gt[WIDTH + fa : WIDTH + fb, lo:hi] = (dot_nt(q_s, gs) * SCALE).astype(BF)
            gt[2 * WIDTH + fa : 2 * WIDTH + fb, lo:hi] = dot_nt(gm_s, probs_b).astype(BF)
    gta = gt[...]
    wacc[...] += dot_nt(n1t[0], gta)
    g1t = dot_nn(wnat[...], gta)
    high = g1t.astype(BF)
    low = (g1t - high.astype(F32)).astype(BF)
    g1 = dot_nt(u[0], high) + dot_nt(u[0], low)
    hat, inv = stats(tok[rows, :].astype(F32))
    csum[0:1, :] += jnp.sum(g1 * hat, axis=0, keepdims=True)
    csum[1:2, :] += jnp.sum(g1, axis=0, keepdims=True)
    part = norm_back(g1, hat, inv, par[0:1, :])

    @pl.when(step % 4 == 0)
    def _():
        gtok[pl.ds(start, 16), :] = grad_mid[0:16] + part[0:16]

    @pl.when(step % 4 != 0)
    def _():
        gtok[pl.ds(start, 16), :] += part[0:16]

    gtok[pl.ds(pl.multiple_of(start + 16, 16), SPAN - 16), :] = grad_mid[16:] + part[16:]

    @pl.when(step == last)
    def _():
        out_t = oacc[...].T
        for h in range(4):
            pieces = [wacc[0:WIDTH, j * WIDTH + 96 * h : j * WIDTH + 96 * (h + 1)] for j in range(3)]
            pieces.append(out_t[:, 96 * h : 96 * (h + 1)])
            ntall[h] = jnp.concatenate(pieces, axis=1).astype(BF)
        for e, k, s, row, head in owners(idx):
            dst = (keep, send)[e]
            base = (k * 4 + s) * 48
            dst[base : base + 48, :] = ntall[head, pl.ds(row, 48), :]
        bias_rows = [wacc[WIDTH : WIDTH + 1, j * WIDTH : (j + 1) * WIDTH] for j in (0, 2)]
        small = jnp.concatenate([csum[0:6, :], *bias_rows], axis=0)
        small = jnp.concatenate([small, jnp.zeros((8, WIDTH), F32)], axis=0).astype(BF)
        keep[768:784, :] = small
        send[768:784, :] = small


def adamw_step(master, grad_value, moment, square, step_rate, decay_rate):
    moment_new = BETA_ONE * moment + (1.0 - BETA_ONE) * grad_value
    square_new = BETA_TWO * square + (1.0 - BETA_TWO) * grad_value * grad_value
    moment_hat = moment_new / (1.0 - BETA_ONE**STEP)
    square_hat = square_new / (1.0 - BETA_TWO**STEP)
    updated = master - step_rate * (
        moment_hat / (jnp.sqrt(square_hat) + ADAM_EPS) + decay_rate * master
    )
    return (updated, moment_new, square_new)


class Links:
    def __init__(self, sizes):
        self.sizes = sizes
        self.outer = sizes["dp"] // 8

    def perm(self, z=0, y=0, x=0, c=0):
        pairs = []
        for flat in range(self.sizes["dp"] * self.sizes["head"]):
            head, dp = flat % 4, flat // 4
            inner, place = dp // self.outer, dp % self.outer
            inner ^= z * 2 + y
            pairs.append((flat, (inner * self.outer + place) * 4 + (head ^ (x * 2 + c))))
        return pairs

    def send(self, value, **flips):
        return lax.ppermute(value, ("dp", "head"), self.perm(**flips))

    def groups(self):
        return [[i * self.outer + j for j in range(self.outer)] for i in range(8)]

    def gather(self, shard):
        if self.outer > 1:
            shard = lax.all_gather(
                shard, "dp", axis=0, tiled=True, axis_index_groups=self.groups()
            )
        line = jnp.concatenate([shard] + [self.send(shard, z=s) for s in range(1, 4)], axis=0)
        plane = [line] + [self.send(line, x=k & 1, y=k >> 1) for k in range(1, 4)]
        return plane + [self.send(part, c=1) for part in plane]

    def outer_sum(self, value):
        if self.outer > 1:
            value = lax.psum_scatter(
                value, "dp", scatter_dimension=0, tiled=True, axis_index_groups=self.groups()
            )
        return value


def whole(shape):
    zeros = (0,) * len(shape)
    return pl.BlockSpec(shape, lambda i: zeros)


def slab(shape):
    zeros = (0,) * (len(shape) - 1)
    return pl.BlockSpec((1, *shape[1:]), lambda i: (i, *zeros))


def turn(shape):
    zeros = (0,) * (len(shape) - 1)
    return pl.BlockSpec((1, *shape[1:]), lambda i: (i % 4, *zeros))


SMEM = pl.BlockSpec(memory_space=pltpu.SMEM)


def per_device(links, *args):
    (
        tokens, crop_ids, grad_out, qkv_w, out_w, exp_w, con_w, qv_b, exp_b, table_w, norm_p,
        qkv_m, qkv_s, out_m, out_s, exp_m, exp_s, con_m, con_s,
        qv_m, qv_s, eb_m, eb_s, tab_m, tab_s, norm_m, norm_s,
    ) = args
    rows_all = tokens.shape[0]
    canvases = rows_all // CANVAS
    head = lax.axis_index("head")
    dp = lax.axis_index("dp") // links.outer
    idx = jnp.stack([dp // 2, dp % 2, head // 2, head % 2]).astype(jnp.int32)

    first = jnp.concatenate([qkv_w[0], qkv_w[1], qkv_w[2], out_w.T], axis=1).astype(BF)
    second = jnp.concatenate([exp_w, con_w.T], axis=1).astype(BF)
    firsts = links.gather(first)
    seconds = links.gather(second)
    own = jnp.concatenate([qv_b.reshape(-1), exp_b, table_w.T.reshape(-1)]).astype(BF)
    own = own.reshape(1, -1)
    pair = jnp.where(idx[3] == 0, 1, 0)
    other = links.send(own, c=1)
    both = jnp.where(pair == 1, jnp.concatenate([own, other]), jnp.concatenate([other, own]))
    other = links.send(both, x=1)
    four = jnp.where(
        idx[2] == 0, jnp.concatenate([both, other]), jnp.concatenate([other, both])
    )
    bias_qv = four[:, 0:192].reshape(4, 2, 96).transpose(1, 0, 2).reshape(2, WIDTH)
    bias_row = jnp.concatenate([bias_qv[0], jnp.zeros((WIDTH,), BF), bias_qv[1]])
    bias16 = jnp.pad(bias_row[None], ((0, 15), (0, 0)))
    eb16 = jnp.pad(four[:, 192:576].reshape(1, HIDDEN), ((0, 15), (0, 0)))
    table_rows = table_w.shape[0]
    table_t = four[:, 576:].reshape(12, table_rows)
    pairs = jnp.asarray(pair_onehot(table_rows), BF)
    bias_t = jnp.einsum("ht,tkq->hkq", table_t, pairs, preferred_element_type=F32) * LOG2E
    bias_t = bias_t.reshape(GROUPS, PACK, SLOT, SLOT).transpose(0, 2, 1, 3)
    bias_t = bias_t.reshape(GROUPS, SLOT, PACK * SLOT)

    crop_rows = lax.dynamic_slice_in_dim(crop_ids, head * rows_all, rows_all, 0)
    quads = (crop_rows & 3).astype(BF)
    quads = jnp.stack(
        [quads[(c // 4) * QUAD_ROWS + 192 * (c % 4) :][:SPAN] for c in range(canvases)]
    )
    quads = jnp.broadcast_to(quads[:, None, :], (canvases, 8, SPAN))
    to_slots, from_slots = permutations()
    to_slots, from_slots = jnp.asarray(to_slots, BF), jnp.asarray(from_slots, BF)
    codes = region_codes()
    reg_row = jnp.asarray(np.broadcast_to(codes[None, :], (8, 4 * SLOT)).copy())
    reg_col = jnp.asarray(np.broadcast_to(codes[:, None], (4 * SLOT, 8)).copy())
    par = jnp.pad(norm_p, ((0, 2), (0, 0)))

    slots = 4 * SLOT
    fm = (canvases, WIDTH, slots)
    tm = (canvases, slots, WIDTH)
    big = (canvases, 12, SLOT, slots)
    nt = (canvases, 400, slots)
    shapes = [
        ((rows_all, WIDTH), BF), (fm, BF), (fm, BF), (tm, BF), (big, BF), (fm, BF), (nt, BF),
        ((WIDTH, 3 * WIDTH), BF), ((WIDTH, WIDTH), BF), ((WIDTH, WIDTH), BF),
    ]
    merged, qt, kt, vv, pt, mt, n1t, wnat, outt, wout = pl.pallas_call(
        attention_forward,
        grid=(canvases,),
        in_specs=[SMEM]
        + [whole((192, WIDTH))] * 8
        + [
            whole((rows_all, WIDTH)), slab(quads.shape), turn(to_slots.shape),
            turn(from_slots.shape), whole(reg_row.shape), whole(reg_col.shape),
            whole(bias16.shape), whole(bias_t.shape), whole(par.shape),
        ],
        out_specs=[whole(shapes[0][0])]
        + [slab(s) for s, _ in shapes[1:7]]
        + [whole(s) for s, _ in shapes[7:]],
        out_shape=[jax.ShapeDtypeStruct(s, d) for s, d in shapes],
        scratch_shapes=[
            pltpu.VMEM((4, WIDTH, WIDTH), BF), pltpu.VMEM((512, 3 * WIDTH), BF),
            pltpu.VMEM((3 * WIDTH, 512), BF), pltpu.VMEM((slots, 512), BF),
            pltpu.VMEM((WIDTH, slots), BF),
        ],
        compiler_params=pltpu.CompilerParams(vmem_limit_bytes=50 * 2**20),
        name="attention_forward",
    )(idx, *firsts, tokens, quads, to_slots, from_slots, reg_row, reg_col, bias16, bias_t, par)

    wide = (rows_all, WIDTH)
    block_out, grad_mid, keep_r, send_r, sums, eb_grad = pl.pallas_call(
        mlp,
        grid=(HIDDEN // CHUNK,),
        in_specs=[SMEM]
        + [whole((192, 2 * WIDTH))] * 8
        + [
            whole(wide), whole(wide), whole(wide), whole((WIDTH, WIDTH)), whole(eb16.shape),
            whole(par.shape),
        ],
        out_specs=[
            whole(wide), whole(wide), whole((768, 2 * WIDTH)), whole((768, 2 * WIDTH)),
            whole((8, WIDTH)), whole((8, HIDDEN)),
        ],
        out_shape=[
            jax.ShapeDtypeStruct(wide, BF), jax.ShapeDtypeStruct(wide, F32),
            jax.ShapeDtypeStruct((768, 2 * WIDTH), BF), jax.ShapeDtypeStruct((768, 2 * WIDTH), BF),
            jax.ShapeDtypeStruct((8, WIDTH), F32), jax.ShapeDtypeStruct((8, HIDDEN), F32),
        ],
        scratch_shapes=[
            pltpu.VMEM((512, HIDDEN), BF), pltpu.VMEM((WIDTH, HIDDEN), BF),
            pltpu.VMEM((rows_all, 512), BF), pltpu.VMEM(wide, F32),
            pltpu.VMEM((400, rows_all), BF), pltpu.VMEM((WIDTH, rows_all), BF),
            pltpu.VMEM((rows_all, CHUNK), BF), pltpu.VMEM((rows_all, CHUNK), BF),
            pltpu.VMEM(wide, F32), pltpu.VMEM(wide, F32),
            pltpu.VMEM((WIDTH, HIDDEN), BF), pltpu.VMEM((WIDTH, HIDDEN), BF),
        ],
        compiler_params=pltpu.CompilerParams(vmem_limit_bytes=58 * 2**20),
        name="mlp",
    )(idx, *seconds, tokens, grad_out, merged, outt, eb16, par)

    grad_tokens, keep_q, send_q, table_sum = pl.pallas_call(
        attention_backward,
        grid=(canvases,),
        in_specs=[SMEM]
        + [
            whole(wide), whole(wide), slab(fm), slab(fm), slab(tm), slab(big), slab(fm), slab(nt),
            whole((WIDTH, 3 * WIDTH)), whole((WIDTH, WIDTH)), turn(to_slots.shape),
            turn(from_slots.shape), whole(par.shape), whole((8, WIDTH)),
        ],
        out_specs=[
            whole(wide), whole((784, WIDTH)), whole((784, WIDTH)), whole((GROUPS, SLOT, slots)),
        ],
        out_shape=[
            jax.ShapeDtypeStruct(wide, F32), jax.ShapeDtypeStruct((784, WIDTH), BF),
            jax.ShapeDtypeStruct((784, WIDTH), BF),
            jax.ShapeDtypeStruct((GROUPS, SLOT, slots), F32),
        ],
        scratch_shapes=[
            pltpu.VMEM((8, 128), BF), pltpu.VMEM((4, WIDTH, WIDTH), BF),
            pltpu.VMEM((400, 3 * WIDTH), F32), pltpu.VMEM((WIDTH, WIDTH), F32),
            pltpu.VMEM((8, WIDTH), F32), pltpu.VMEM((3 * WIDTH, slots), BF),
        ],
        compiler_params=pltpu.CompilerParams(vmem_limit_bytes=50 * 2**20),
        name="attention_backward",
    )(
        idx, tokens, grad_mid, qt, kt, vv, pt, mt, n1t, wnat, wout, to_slots, from_slots, par, sums
    )

    table_part = table_sum.reshape(GROUPS, SLOT, PACK, SLOT).transpose(0, 2, 1, 3)
    table_part = table_part.reshape(12, SLOT * SLOT)
    table_grad = jnp.dot(
        table_part, pairs.reshape(table_rows, -1).astype(F32).T, precision=lax.Precision.HIGHEST
    )
    extra = jnp.concatenate([eb_grad[0], table_grad.reshape(-1)])
    extra_rows = -(-extra.shape[0] // (16 * WIDTH)) * 16
    extra = jnp.pad(extra, (0, extra_rows * WIDTH - extra.shape[0])).reshape(extra_rows, WIDTH)

    def reduced(keep, send, small, small_sent):
        columns = keep.shape[1]
        total = keep.astype(F32) + links.send(send, c=1).astype(F32)
        if small is not None:
            small = small.astype(F32) + links.send(small_sent, c=1).astype(F32)
        total = total.reshape(4, 192, columns)
        got = []
        for k in range(1, 4):
            out = total[k].astype(BF)
            if small is not None:
                out = jnp.concatenate([out, small.astype(BF)], axis=0)
            got.append(links.send(out, x=k & 1, y=k >> 1).astype(F32))
        total = total[0] + got[0][:192] + got[1][:192] + got[2][:192]
        if small is not None:
            small = small + got[0][192:] + got[1][192:] + got[2][192:]
        total = total.reshape(4, 48, columns)
        got = []
        for s in range(1, 4):
            out = total[s].astype(BF)
            if small is not None:
                out = jnp.concatenate([out, small.astype(BF)], axis=0)
            got.append(links.send(out, z=s).astype(F32))
        total = total[0] + got[0][:48] + got[1][:48] + got[2][:48]
        if small is not None:
            small = small + got[0][48:] + got[1][48:] + got[2][48:]
        if links.outer > 1 and small is not None:
            small = lax.psum(small, "dp", axis_index_groups=links.groups())
        return links.outer_sum(total), small

    total_r, _ = reduced(keep_r, send_r, None, None)
    total_q, _ = reduced(keep_q[:768], send_q[:768], None, None)
    small_own = jnp.concatenate([keep_q[768:].astype(F32), extra], axis=0)
    small_own = small_own.astype(BF)
    small = small_own.astype(F32)
    small = small + links.send(small.astype(BF), c=1).astype(F32)
    send_now = small.astype(BF)
    for k in range(1, 4):
        small = small + links.send(send_now, x=k & 1, y=k >> 1).astype(F32)
    send_now = small.astype(BF)
    for s in range(1, 4):
        small = small + links.send(send_now, z=s).astype(F32)
    if links.outer > 1:
        small = lax.psum(small, "dp", axis_index_groups=links.groups())

    qkv_grad = total_q[:, 0:288].reshape(-1, 3, 96).transpose(1, 0, 2)
    out_grad = total_q[:, 288:].T
    exp_grad = total_r[:, 0:WIDTH]
    con_grad = total_r[:, WIDTH:].T
    norm_grad = small[0:6]
    qv_grad = lax.dynamic_slice_in_dim(small[6:8], head * 96, 96, 1)
    flat = small[16:].reshape(-1)
    eb_grad = lax.dynamic_slice_in_dim(flat[:HIDDEN], head * WIDTH, WIDTH, 0)
    tab_grad = flat[HIDDEN : HIDDEN + 12 * table_rows].reshape(12, table_rows)
    tab_grad = lax.dynamic_slice_in_dim(tab_grad, head * 3, 3, 0).T

    news = (
        adamw_step(qkv_w, qkv_grad, qkv_m, qkv_s, RATE_MATRIX, DECAY_MATRIX)
        + adamw_step(out_w, out_grad, out_m, out_s, RATE_MATRIX, DECAY_MATRIX)
        + adamw_step(exp_w, exp_grad, exp_m, exp_s, RATE_MATRIX, DECAY_MATRIX)
        + adamw_step(con_w, con_grad, con_m, con_s, RATE_MATRIX, DECAY_MATRIX)
        + adamw_step(qv_b, qv_grad, qv_m, qv_s, RATE_SMALL, 0.0)
        + adamw_step(exp_b, eb_grad, eb_m, eb_s, RATE_SMALL, 0.0)
        + adamw_step(table_w, tab_grad, tab_m, tab_s, RATE_SMALL, 0.0)
        + adamw_step(norm_p, norm_grad, norm_m, norm_s, RATE_SMALL, 0.0)
    )
    return (block_out, grad_tokens, *news)


def solution(mesh):
    tokens = P(("dp", "head"), None)
    qkv, rows_head, rows_dp = P(None, "dp", "head"), P("head", "dp"), P("dp", "head")
    pair, unit, none = P(None, "head"), P("head"), P()
    matrices = (qkv, rows_head, rows_dp, rows_head)
    small = (pair, unit, pair, none)
    in_specs = (tokens, P("dp"), tokens, *matrices, *small)
    in_specs += tuple(s for spec in (*matrices, *small) for s in (spec, spec))
    out_specs = (tokens, tokens) + tuple(
        s for spec in (*matrices, *small) for s in (spec, spec, spec)
    )
    return jax.shard_map(
        functools.partial(per_device, Links(dict(mesh.shape))),
        mesh=mesh, in_specs=in_specs, out_specs=out_specs, check_vma=False,
    )
```

time: 862 us -> 218 us (0.25)
  waiting for transfers between devices: 267 us -> 35.5 us
  blocking collectives: 231 us -> 0 us
  local copies, waits for them, and re-layouts: 179 us -> 8.17 us
  matrix products: 116 us -> 5.09 us
  Pallas kernels: 0 us -> 104 us
  starting transfers between devices: 0.46 us -> 46.4 us
  other arithmetic: 44.8 us -> 16.8 us
  between operations: 17.4 us -> 1.38 us
    unnamed x16 -> x0, waiting for transfers between devices: 162 us -> none
    all_gather x9 -> x0, blocking collectives: 160 us -> none  [the longest x1 34.6 us: per_device(): lax.all_gather(expand_weight.astype(jnp.bfloat16), 'dp', axis=0, tiled=True)]
    dot_general x22 -> x2, matrix products: 116 us -> 5.09 us  [the longest x1 2.59 us: per_device(): jnp.dot(table_part, pairs.reshape(table_rows, -1).astype(F32).T, precisio...]
    pallas_call x0 -> x3, Pallas kernels: none -> 104 us  [the longest x1 42 us: per_device(): pl.pallas_call(attention_backward, grid=(canvases,), in_specs=[SMEM] + [w...]
    reduce_scatter x4 -> x0, waiting for transfers between devices: 88.6 us -> none  [the longest x1 62.9 us: per_device(): lax.psum_scatter(expand_grad, 'dp', scatter_dimension=0, tiled=True)]
    psum x2 -> x0, blocking collectives: 60.8 us -> none  [the longest x1 39.8 us: per_device(): norm_grad = lax.psum(norm_grad, ('dp', 'head'))]
    ppermute x0 -> x43, starting transfers between devices: none -> 46.4 us  [send(): return lax.ppermute(value, ('dp', 'head'), self.perm(**flips))]
    reshape x9 -> x11, local copies, waits for them, and re-layouts: 43.3 us -> 1.11 us  [the longest x1 0.27 us: per_device(): bias_t = bias_t.reshape(GROUPS, SLOT, PACK * SLOT)]
  transfers between devices with their start and end apart: 11 -> 43, of which waited for: 6 -> 17; matrix products, arithmetic and copies ran while one was open for 19% -> 9% of each run, Pallas kernels for 0% -> 13%
where the time goes in v1:
time: 218 us; the launch traced here: 217 us
  Pallas kernels  104 us (48%)
  starting transfers between devices  46.4 us (21%)
  waiting for transfers between devices  35.5 us (16%)
  other arithmetic  16.8 us (8%)
  local copies, waits for them, and re-layouts  8.17 us (4%)
  matrix products  5.09 us (2%)
    ppermute x43, starting transfers between devices, send(): return lax.ppermute(value, ('dp', 'head'), self.perm(**flips))  46.4 us
    pallas_call x1, Pallas kernels, per_device(): pl.pallas_call(attention_backward, grid=(canvases,), in_specs=[SMEM] + [w...  42 us
    ppermute x43, waiting for transfers between devices, send(): return lax.ppermute(value, ('dp', 'head'), self.perm(**flips))  35.5 us
    pallas_call x1, Pallas kernels, per_device(): pl.pallas_call(mlp, grid=(HIDDEN // CHUNK,), in_specs=[SMEM] + [whole((19...  33 us
    pallas_call x1, Pallas kernels, per_device(): pl.pallas_call(attention_forward, grid=(canvases,), in_specs=[SMEM] + [wh...  28.6 us
    sub x8, other arithmetic, adamw_step(): master - step_rate * (moment_hat / (jnp.sqrt(square_hat) + ADAM_EPS) + de...  8.47 us
  transfers between devices with their start and end apart: 43, of which 17 were waited for; matrix products, arithmetic and copies ran while one was open for 9% of the time, Pallas kernels for 13%

profile of v1, /device:TPU:0, one launch (start us, length us, event | category | flops | bytes accessed | tf_op | source)
XLA Modules:
  0.0 216.9 jit_solution(11939864718081783257)
XLA Ops:
  0.7 0.9 convert.71
  1.6 0.7 convert_bitcast_fusion.1
  2.4 3.1 %collective-permute-start.10 = (bf16[48,384]{1,0:T(8,128)(2,1)S(1)}, bf16[48,384]{1,0:T(8,128)(2,1)S(1)}, u32[]{:S(2)}, u32[]{:S(2)}) collective-permute-start(bf16[48,384]{1,0:T(8,128)(2,1)S(1)} %pad_maximum_fusion.3), channel_id=1, source_target_pairs={{0,8},{1,9},{2,10},{3,11},{4,12},{5,13},{6,14},{7,15},{8,0},{9,1},... | collective-permute-start | bytes 110600 | tf_op jit(solution)/shard_map/ppermute | solution.py:387
  5.5 2.6 %collective-permute-start.11 = (bf16[48,384]{1,0:T(8,128)(2,1)S(1)}, bf16[48,384]{1,0:T(8,128)(2,1)S(1)}, u32[]{:S(2)}, u32[]{:S(2)}) collective-permute-start(bf16[48,384]{1,0:T(8,128)(2,1)S(1)} %pad_maximum_fusion.3), channel_id=1, source_target_pairs={{0,16},{1,17},{2,18},{3,19},{4,20},{5,21},{6,22},{7,23},{8,24},{9,... | collective-permute-start | bytes 110600 | tf_op jit(solution)/shard_map/ppermute | solution.py:387
  8.1 0.7 convert_bitcast_fusion.2
  8.9 0.7 convert.74
  9.6 0.7 convert.73
  10.5 0.9 convert.69
  11.4 0.9 convert_bitcast_fusion
  12.3 1.0 collective-permute-start
  13.3 0.8 and_convert_fusion
  14.3 0.7 pad.18.par
  15.0 3.6 %collective-permute-start.1 = (bf16[48,768]{1,0:T(8,128)(2,1)S(1)}, bf16[48,768]{1,0:T(8,128)(2,1)S(1)}, u32[]{:S(2)}, u32[]{:S(2)}) collective-permute-start(bf16[48,768]{1,0:T(8,128)(2,1)S(1)} %pad_maximum_fusion.2), channel_id=1, source_target_pairs={{0,16},{1,17},{2,18},{3,19},{4,20},{5,21},{6,22},{7,23},{8,24},{9,... | collective-permute-start | bytes 221192 | tf_op jit(solution)/shard_map/ppermute | solution.py:387
  18.7 1.7 collective-permute-start.21
  21.0 1.4 collective-permute-done.21
  22.4 1.7 collective-permute-start.14
  24.1 1.4 collective-permute-start.15
  25.8 0.7 collective-permute-start.3
  26.5 1.5 collective-permute-start.4
  28.0 3.2 %collective-permute-done.14.p2 = bf16[192,384]{1,0:T(8,128)(2,1)S(1)} collective-permute-done((bf16[192,384]{1,0:T(8,128)(2,1)S(1)}, bf16[192,384]{1,0:T(8,128)(2,1)S(1)}, u32[]{:S(2)}, u32[]{:S(2)}) %collective-permute-start.14) | collective-permute-done | bytes 147488 | tf_op jit(solution)/shard_map/ppermute | solution.py:387
  31.2 2.2 collective-permute-start.5
  33.4 2.5 %convolution_multiply_fusion = f32[12,64,64]{2,0,1:T(8,128)S(1)} fusion(bf16[12,169,1]{1,0,2:T(8,128)(2,1)S(1)} %reshape.199, bf16[169,64,64]{0,2,1:T(8,128)(2,1)} %constant.87.clone), kind=kOutput, calls=%fused_computation.1 | convolution fusion | flops 16662528 | bytes 1585112 | tf_op jit(solution)/shard_map/ht,tkq->hkq/dot_general | solution.py:459
  38.0 5.5 %collective-permute-done.4.p2 = bf16[192,768]{1,0:T(8,128)(2,1)} collective-permute-done((bf16[192,768]{1,0:T(8,128)(2,1)S(1)}, bf16[192,768]{1,0:T(8,128)(2,1)}, u32[]{:S(2)}, u32[]{:S(2)}) %collective-permute-start.4) | collective-permute-done | bytes 294944 | tf_op jit(solution)/shard_map/ppermute | solution.py:387
  44.8 0.9 collective-permute-done.19.p7
  45.7 28.6 %attention_forward.1 = (bf16[1568,384]{1,0:T(8,128)(2,1)}, bf16[8,384,256]{2,1,0:T(8,128)(2,1)}, bf16[8,384,256]{2,1,0:T(8,128)(2,1)}, bf16[8,256,384]{2,1,0:T(8...) custom-call(s32[4]{0:T(128)S(1)} %pad_add_fusion.idx, ...), custom_call_target="tpu_custom_call" | custom-call | tf_op jit(solution)/shard_map/attention_forward/pallas_call | solution.py:485
  74.3 0.7 copy-done.2
  76.1 33.0 %mlp.1 = (bf16[1568,384]{1,0:T(8,128)(2,1)}, f32[1568,384]{1,0:T(8,128)}, bf16[768,768]{1,0:T(8,128)(2,1)}, bf16[768,768]{1,0:T(8,128)(2,1)}, f32[8,384]{1,0:T(8,128)}, /*index=5*/f32[8,1536]{1,0:T(8,128)}) custom-call(s32[4]{0:T(128)} %copy-done.7, bf16[192,768]{1,0:T(8,128)(2,1)} %copy-done.10, bf16[192,768]{1,0:T(8,128)(2,1)} %copy-done.12, ...), custom_call_target="tpu_custom_call" | custom-call | tf_op jit(solution)/shard_map/mlp/pallas_call | solution.py:509
  109.1 0.7 copy-done.6
  109.8 42.0 %attention_backward.1 = (f32[1568,384]{1,0:T(8,128)}, bf16[784,384]{1,0:T(8,128)(2,1)S(1)}, bf16[784,384]{1,0:T(8,128)(2,1)S(1)}, f32[3,64,256]{2,1,0:T(8,128)S(1)}) custom-call(s32[4]{0:T(128)S(1)} %copy-done.8, bf16[1568,384]{1,0:T(8,128)(2,1)} %tok.5, f32[1568,384]{1,0:T(8,128)} %get-tuple-element.49.gmid, bf16[8,384,256]{2,1,0:T(8,128)(2,1)} %get-tuple-element.50.qt, ...), custom_call_target="tpu_custom_call" | custom-call | tf_op jit(solution)/shard_map/attention_backward/pallas_call | solution.py:539
  152.2 2.6 %convolution_convert_fusion = bf16[12,169]{1,0:T(8,128)(2,1)S(1)} fusion(f32[12,4096]{1,0:T(8,128)S(1)} %reshape.193, bf16[169,4096]{1,0:T(8,128)(2,1)} %constant.196), kind=kOutput, calls=%fused_computation.3 | convolution fusion | flops 99682288 | bytes 1585112 | tf_op jit(solution)/shard_map/dot_general | solution.py:569
  154.9 0.8 fusion.18
  156.0 1.1 collective-permute-done.36
  157.1 1.7 collective-permute-start.37
  158.8 1.1 collective-permute-start.38
  159.8 0.8 collective-permute-start.39
  161.0 1.6 collective-permute-done.38
  162.6 2.0 collective-permute-done.39
  165.0 3.6 %collective-permute-start.41 = (bf16[32,384]{1,0:T(8,128)(2,1)S(1)}, bf16[32,384]{1,0:T(8,128)(2,1)}, u32[]{:S(2)}, u32[]{:S(2)}) collective-permute-start(bf16[32,384]{1,0:T(8,128)(2,1)S(1)} %fusion.23), channel_id=1, source_target_pairs={{0,16},{1,17},{2,18},{3,19},{4,20},{5,21},{6,22},{7,23},{8,24},{9,... | collective-permute-start | bytes 73736 | tf_op jit(solution)/shard_map/ppermute | solution.py:387
  169.7 0.9 collective-permute-done.41
  170.6 3.8 %collective-permute-done.42 = bf16[32,384]{1,0:T(8,128)(2,1)} collective-permute-done((bf16[32,384]{1,0:T(8,128)(2,1)S(1)}, bf16[32,384]{1,0:T(8,128)(2,1)}, u32[]{:S(2)}, u32[]{:S(2)}) %collective-permute-start.42) | collective-permute-done | bytes 24608 | tf_op jit(solution)/shard_map/ppermute | solution.py:387
  174.4 0.8 convert_add_fusion.2
  175.4 1.4 multiply_subtract_fusion.6
  176.8 1.3 multiply_subtract_fusion.5
  178.1 1.3 multiply_subtract_fusion.4
  179.7 0.7 collective-permute-start.23
  180.4 1.0 collective-permute-start.24
  181.4 1.8 collective-permute-start.25
  183.9 1.0 collective-permute-done.23
  185.5 1.9 collective-permute-done.25
  187.6 1.7 collective-permute-start.27
  189.4 2.7 %collective-permute-start.28 = (bf16[48,384]{1,0:T(8,128)(2,1)S(1)}, bf16[48,384]{1,0:T(8,128)(2,1)S(1)}, u32[]{:S(2)}, u32[]{:S(2)}) collective-permute-start(bf16[48,384]{1,0:T(8,128)(2,1)S(1)} %get-tuple-element.162), channel_id=1, source_target_pairs={{0,24},{1,25},{2,26},{3,27},{4,28},{5,29},{6,30},{7,31},{8,16},{9,... | collective-permute-start | bytes 110600 | tf_op jit(solution)/shard_map/ppermute | solution.py:387
  192.4 0.9 fusion.40
  193.4 1.5 collective-permute-start.30
  194.8 0.9 collective-permute-start.31
  195.8 1.1 collective-permute-start.32
  197.0 1.6 multiply_subtract_fusion.2
  198.6 1.7 collective-permute-done.30
  200.3 4.6 %collective-permute-done.31 = bf16[192,768]{1,0:T(8,128)(2,1)S(1)} collective-permute-done((bf16[192,768]{1,0:T(8,128)(2,1)}, bf16[192,768]{1,0:T(8,128)(2,1)S(1)}, u32[]{:S(2)}, u32[]{:S(2)}) %collective-permute-start.31) | collective-permute-done | bytes 294944 | tf_op jit(solution)/shard_map/ppermute | solution.py:387
  205.7 3.5 %collective-permute-start.34 = (bf16[48,768]{1,0:T(8,128)(2,1)S(1)}, bf16[48,768]{1,0:T(8,128)(2,1)S(1)}, u32[]{:S(2)}, u32[]{:S(2)}) collective-permute-start(bf16[48,768]{1,0:T(8,128)(2,1)S(1)} %get-tuple-element.160), channel_id=1, source_target_pairs={{0,16},{1,17},{2,18},{3,19},{4,20},{5,21},{6,22},{7,23},{8,24},{9,... | collective-permute-start | bytes 221192 | tf_op jit(solution)/shard_map/ppermute | solution.py:387
  209.6 0.7 multiply_subtract_fusion.3
  210.3 2.0 collective-permute-done.34
  212.3 3.0 %collective-permute-done.35 = bf16[48,768]{1,0:T(8,128)(2,1)S(1)} collective-permute-done((bf16[48,768]{1,0:T(8,128)(2,1)S(1)}, bf16[48,768]{1,0:T(8,128)(2,1)S(1)}, u32[]{:S(2)}, u32[]{:S(2)}) %collective-permute-start.35) | collective-permute-done | bytes 73760 | tf_op jit(solution)/shard_map/ppermute | solution.py:387
  215.4 0.7 multiply_subtract_fusion
  216.1 0.7 multiply_subtract_fusion.1
  (185 shorter events, 12.1 us)
Async XLA Ops:
  2.4 16.2 %collective-permute-start.10 = (bf16[48,384]{1,0:T(8,128)(2,1)S(1)}, bf16[48,384]{1,0:T(8,128)(2,1)S(1)}, u32[]{:S(2)}, u32[]{:S(2)}) collective-permute-start(bf16[48,384]{1,0:T(8,128)(2,1)S(1)} %pad_maximum_fusion.3), channel_id=1, source_target_pairs={{0,8},{1,9},{2,10},{3,11},{4,12},{5,13},{6,14},{7,15},{8,0},{9,1},... | collective-permute-start | bytes 110600 | tf_op jit(solution)/shard_map/ppermute | solution.py:387
  5.5 13.2 %collective-permute-start.11 = (bf16[48,384]{1,0:T(8,128)(2,1)S(1)}, bf16[48,384]{1,0:T(8,128)(2,1)S(1)}, u32[]{:S(2)}, u32[]{:S(2)}) collective-permute-start(bf16[48,384]{1,0:T(8,128)(2,1)S(1)} %pad_maximum_fusion.3), channel_id=1, source_target_pairs={{0,16},{1,17},{2,18},{3,19},{4,20},{5,21},{6,22},{7,23},{8,24},{9,... | collective-permute-start | bytes 110600 | tf_op jit(solution)/shard_map/ppermute | solution.py:387
  8.1 12.3 %collective-permute-start.12 = (bf16[48,384]{1,0:T(8,128)(2,1)S(1)}, bf16[48,384]{1,0:T(8,128)(2,1)S(1)}, u32[]{:S(2)}, u32[]{:S(2)}) collective-permute-start(bf16[48,384]{1,0:T(8,128)(2,1)S(1)} %pad_maximum_fusion.3), channel_id=1, source_target_pairs={{0,24},{1,25},{2,26},{3,27},{4,28},{5,29},{6,30},{7,31},{8,16},{9,... | collective-permute-start | bytes 110600 | tf_op jit(solution)/shard_map/ppermute | solution.py:387
  10.4 4.6 %collective-permute-start.20 = (bf16[1,1083]{1,0:T(2,128)(2,1)S(1)}, bf16[1,1083]{1,0:T(2,128)(2,1)S(1)}, u32[]{:S(2)}, u32[]{:S(2)}) collective-permute-start(bf16[1,1083]{1,0:T(2,128)(2,1)S(1)} %concatenate.61), channel_id=1, source_target_pairs={{0,1},{1,0},{2,3},{3,2},{4,5},{5,4},{6,7},{7,6},{8,9},{9,8},{10,11... | collective-permute-start | bytes 6506 | tf_op jit(solution)/shard_map/ppermute | solution.py:387
  12.3 11.8 %collective-permute-start = (bf16[48,768]{1,0:T(8,128)(2,1)S(1)}, bf16[48,768]{1,0:T(8,128)(2,1)S(1)}, u32[]{:S(2)}, u32[]{:S(2)}) collective-permute-start(bf16[48,768]{1,0:T(8,128)(2,1)S(1)} %pad_maximum_fusion.2), channel_id=1, source_target_pairs={{0,8},{1,9},{2,10},{3,11},{4,12},{5,13},{6,14},{7,15},{8,0},{9,1},... | collective-permute-start | bytes 221192 | tf_op jit(solution)/shard_map/ppermute | solution.py:387
  14.2 31.5 %copy-start.7 = (s32[4]{0:T(128)}, s32[4]{0:T(128)S(1)}, u32[]{:S(2)}) copy-start(s32[4]{0:T(128)S(1)} %pad_add_fusion.idx) | copy-start | bytes 52
  15.0 30.7 %copy-start.3 = (f32[8,384]{1,0:T(8,128)}, f32[8,384]{1,0:T(8,128)S(1)}, u32[]{:S(2)}) copy-start(f32[8,384]{1,0:T(8,128)S(1)} %pad.18.par) | copy-start | bytes 36868
  15.0 10.7 %collective-permute-start.1 = (bf16[48,768]{1,0:T(8,128)(2,1)S(1)}, bf16[48,768]{1,0:T(8,128)(2,1)S(1)}, u32[]{:S(2)}, u32[]{:S(2)}) collective-permute-start(bf16[48,768]{1,0:T(8,128)(2,1)S(1)} %pad_maximum_fusion.2), channel_id=1, source_target_pairs={{0,16},{1,17},{2,18},{3,19},{4,20},{5,21},{6,22},{7,23},{8,24},{9,... | collective-permute-start | bytes 221192 | tf_op jit(solution)/shard_map/ppermute | solution.py:387
  18.6 7.1 %collective-permute-start.2 = (bf16[48,768]{1,0:T(8,128)(2,1)S(1)}, bf16[48,768]{1,0:T(8,128)(2,1)S(1)}, u32[]{:S(2)}, u32[]{:S(2)}) collective-permute-start(bf16[48,768]{1,0:T(8,128)(2,1)S(1)} %pad_maximum_fusion.2), channel_id=1, source_target_pairs={{0,24},{1,25},{2,26},{3,27},{4,28},{5,29},{6,30},{7,31},{8,16},{9,... | collective-permute-start | bytes 221192 | tf_op jit(solution)/shard_map/ppermute | solution.py:387
  18.7 3.7 %collective-permute-start.21 = (bf16[2,1083]{1,0:T(2,128)(2,1)S(1)}, bf16[2,1083]{1,0:T(2,128)(2,1)S(1)}, u32[]{:S(2)}, u32[]{:S(2)}) collective-permute-start(bf16[2,1083]{1,0:T(2,128)(2,1)S(1)} %broadcast_select_fusion), channel_id=1, source_target_pairs={{0,2},{1,3},{2,0},{3,1},{4,6},{5,7},{6,4},{7,5},{8,10},{9,11},{10,... | collective-permute-start | bytes 13004 | tf_op jit(solution)/shard_map/ppermute | solution.py:387
  20.5 6.0 %collective-permute-start.13 = (bf16[192,384]{1,0:T(8,128)(2,1)S(1)}, bf16[192,384]{1,0:T(8,128)(2,1)S(1)}, u32[]{:S(2)}, u32[]{:S(2)}) collective-permute-start(bf16[192,384]{1,0:T(8,128)(2,1)S(1)} %pad_maximum_fusion.1.p0), channel_id=1, source_target_pairs={{0,2},{1,3},{2,0},{3,1},{4,6},{5,7},{6,4},{7,5},{8,10},{9,11},{10,... | collective-permute-start | bytes 442376 | tf_op jit(solution)/shard_map/ppermute | solution.py:387
  22.4 8.8 %collective-permute-start.14 = (bf16[192,384]{1,0:T(8,128)(2,1)S(1)}, bf16[192,384]{1,0:T(8,128)(2,1)S(1)}, u32[]{:S(2)}, u32[]{:S(2)}) collective-permute-start(bf16[192,384]{1,0:T(8,128)(2,1)S(1)} %pad_maximum_fusion.1.p0), channel_id=1, source_target_pairs={{0,4},{1,5},{2,6},{3,7},{4,0},{5,1},{6,2},{7,3},{8,12},{9,13},{10,... | collective-permute-start | bytes 442376 | tf_op jit(solution)/shard_map/ppermute | solution.py:387
  24.1 9.3 %collective-permute-start.15 = (bf16[192,384]{1,0:T(8,128)(2,1)S(1)}, bf16[192,384]{1,0:T(8,128)(2,1)S(1)}, u32[]{:S(2)}, u32[]{:S(2)}) collective-permute-start(bf16[192,384]{1,0:T(8,128)(2,1)S(1)} %pad_maximum_fusion.1.p0), channel_id=1, source_target_pairs={{0,6},{1,7},{2,4},{3,5},{4,2},{5,3},{6,0},{7,1},{8,14},{9,15},{10,... | collective-permute-start | bytes 442376 | tf_op jit(solution)/shard_map/ppermute | solution.py:387
  25.7 10.3 %collective-permute-start.16 = (bf16[192,384]{1,0:T(8,128)(2,1)S(1)}, bf16[192,384]{1,0:T(8,128)(2,1)S(1)}, u32[]{:S(2)}, u32[]{:S(2)}) collective-permute-start(bf16[192,384]{1,0:T(8,128)(2,1)S(1)} %pad_maximum_fusion.1.p0), channel_id=1, source_target_pairs={{0,1},{1,0},{2,3},{3,2},{4,5},{5,4},{6,7},{7,6},{8,9},{9,8},{10,11... | collective-permute-start | bytes 442376 | tf_op jit(solution)/shard_map/ppermute | solution.py:387
  25.8 11.6 %copy-start.10 = (bf16[192,768]{1,0:T(8,128)(2,1)}, bf16[192,768]{1,0:T(8,128)(2,1)S(1)}, u32[]{:S(2)}) copy-start(bf16[192,768]{1,0:T(8,128)(2,1)S(1)} %pad_maximum_fusion.p0) | copy-start | bytes 884740
  25.8 11.7 %collective-permute-start.3 = (bf16[192,768]{1,0:T(8,128)(2,1)S(1)}, bf16[192,768]{1,0:T(8,128)(2,1)S(1)}, u32[]{:S(2)}, u32[]{:S(2)}) collective-permute-start(bf16[192,768]{1,0:T(8,128)(2,1)S(1)} %pad_maximum_fusion.p0), channel_id=1, source_target_pairs={{0,2},{1,3},{2,0},{3,1},{4,6},{5,7},{6,4},{7,5},{8,10},{9,11},{10,... | collective-permute-start | bytes 884744 | tf_op jit(solution)/shard_map/ppermute | solution.py:387
  26.5 16.9 %collective-permute-start.4 = (bf16[192,768]{1,0:T(8,128)(2,1)S(1)}, bf16[192,768]{1,0:T(8,128)(2,1)}, u32[]{:S(2)}, u32[]{:S(2)}) collective-permute-start(bf16[192,768]{1,0:T(8,128)(2,1)S(1)} %pad_maximum_fusion.p0), channel_id=1, source_target_pairs={{0,4},{1,5},{2,6},{3,7},{4,0},{5,1},{6,2},{7,3},{8,12},{9,13},{10,... | collective-permute-start | bytes 884744 | tf_op jit(solution)/shard_map/ppermute | solution.py:387
  31.2 12.3 %collective-permute-start.5 = (bf16[192,768]{1,0:T(8,128)(2,1)S(1)}, bf16[192,768]{1,0:T(8,128)(2,1)}, u32[]{:S(2)}, u32[]{:S(2)}) collective-permute-start(bf16[192,768]{1,0:T(8,128)(2,1)S(1)} %pad_maximum_fusion.p0), channel_id=1, source_target_pairs={{0,6},{1,7},{2,4},{3,5},{4,2},{5,3},{6,0},{7,1},{8,14},{9,15},{10,... | collective-permute-start | bytes 884744 | tf_op jit(solution)/shard_map/ppermute | solution.py:387
  33.4 4.0 %collective-permute-start.17 = (bf16[192,384]{1,0:T(8,128)(2,1)S(1)}, bf16[192,384]{1,0:T(8,128)(2,1)S(1)}, u32[]{:S(2)}, u32[]{:S(2)}) collective-permute-start(bf16[192,384]{1,0:T(8,128)(2,1)S(1)} %collective-permute-done.13.p1), channel_id=1, source_target_pairs={{0,1},{1,0},{2,3},{3,2},{4,5},{5,4},{6,7},{7,6},{8,9},{9,8},{10,11... | collective-permute-start | bytes 442376 | tf_op jit(solution)/shard_map/ppermute | solution.py:387
  35.9 9.8 %copy-start.1 = (bf16[4,208,256]{2,1,0:T(8,128)(2,1)S(1)}, bf16[4,208,256]{2,1,0:T(8,128)(2,1)}, u32[]{:S(2)}) copy-start(bf16[4,208,256]{2,1,0:T(8,128)(2,1)} %constant.89.clone.u) | copy-start | bytes 1277956
  36.0 8.0 %collective-permute-start.18 = (bf16[192,384]{1,0:T(8,128)(2,1)S(1)}, bf16[192,384]{1,0:T(8,128)(2,1)S(1)}, u32[]{:S(2)}, u32[]{:S(2)}) collective-permute-start(bf16[192,384]{1,0:T(8,128)(2,1)S(1)} %collective-permute-done.14.p2), channel_id=1, source_target_pairs={{0,1},{1,0},{2,3},{3,2},{4,5},{5,4},{6,7},{7,6},{8,9},{9,8},{10,11... | collective-permute-start | bytes 442376 | tf_op jit(solution)/shard_map/ppermute | solution.py:387
  37.4 37.7 %collective-permute-start.6 = (bf16[192,768]{1,0:T(8,128)(2,1)S(1)}, bf16[192,768]{1,0:T(8,128)(2,1)S(1)}, u32[]{:S(2)}, u32[]{:S(2)}) collective-permute-start(bf16[192,768]{1,0:T(8,128)(2,1)S(1)} %pad_maximum_fusion.p0), channel_id=1, source_target_pairs={{0,1},{1,0},{2,3},{3,2},{4,5},{5,4},{6,7},{7,6},{8,9},{9,8},{10,11... | collective-permute-start | bytes 884744 | tf_op jit(solution)/shard_map/ppermute | solution.py:387
  37.5 36.8 %copy-start.12 = (bf16[192,768]{1,0:T(8,128)(2,1)}, bf16[192,768]{1,0:T(8,128)(2,1)S(1)}, u32[]{:S(2)}) copy-start(bf16[192,768]{1,0:T(8,128)(2,1)S(1)} %collective-permute-done.3.p1) | copy-start | bytes 884740
  37.5 37.6 %collective-permute-start.7 = (bf16[192,768]{1,0:T(8,128)(2,1)S(1)}, bf16[192,768]{1,0:T(8,128)(2,1)S(1)}, u32[]{:S(2)}, u32[]{:S(2)}) collective-permute-start(bf16[192,768]{1,0:T(8,128)(2,1)S(1)} %collective-permute-done.3.p1), channel_id=1, source_target_pairs={{0,1},{1,0},{2,3},{3,2},{4,5},{5,4},{6,7},{7,6},{8,9},{9,8},{10,11... | collective-permute-start | bytes 884744 | tf_op jit(solution)/shard_map/ppermute | solution.py:387
  43.5 31.6 %collective-permute-start.8 = (bf16[192,768]{1,0:T(8,128)(2,1)}, bf16[192,768]{1,0:T(8,128)(2,1)S(1)}, u32[]{:S(2)}, u32[]{:S(2)}) collective-permute-start(bf16[192,768]{1,0:T(8,128)(2,1)} %collective-permute-done.4.p2), channel_id=1, source_target_pairs={{0,1},{1,0},{2,3},{3,2},{4,5},{5,4},{6,7},{7,6},{8,9},{9,8},{10,11... | collective-permute-start | bytes 884744 | tf_op jit(solution)/shard_map/ppermute | solution.py:387
  43.5 31.6 %collective-permute-start.9 = (bf16[192,768]{1,0:T(8,128)(2,1)}, bf16[192,768]{1,0:T(8,128)(2,1)S(1)}, u32[]{:S(2)}, u32[]{:S(2)}) collective-permute-start(bf16[192,768]{1,0:T(8,128)(2,1)} %collective-permute-done.5.p3), channel_id=1, source_target_pairs={{0,1},{1,0},{2,3},{3,2},{4,5},{5,4},{6,7},{7,6},{8,9},{9,8},{10,11... | collective-permute-start | bytes 884744 | tf_op jit(solution)/shard_map/ppermute | solution.py:387
  44.0 1.6 collective-permute-start.19
  76.1 33.0 %copy-start.4 = (f32[8,384]{1,0:T(8,128)S(1)}, f32[8,384]{1,0:T(8,128)}, u32[]{:S(2)}) copy-start(f32[8,384]{1,0:T(8,128)} %copy-done.3) | copy-start | bytes 36868
  76.1 33.0 %copy-start.8 = (s32[4]{0:T(128)S(1)}, s32[4]{0:T(128)}, u32[]{:S(2)}) copy-start(s32[4]{0:T(128)} %copy-done.7) | copy-start | bytes 52
  152.2 23.2 %copy-start.31 = (f32[384]{0:T(512)S(1)}, f32[384]{0:T(512)}, u32[]{:S(2)}) copy-start(f32[384]{0:T(512)} %param.40) | copy-start | bytes 4612
  152.2 24.6 %copy-start.29 = (f32[169,3]{0,1:T(4,128)S(1)}, f32[169,3]{0,1:T(4,128)}, u32[]{:S(2)}) copy-start(f32[169,3]{0,1:T(4,128)} %param.41) | copy-start | bytes 6088
  154.8 23.3 %copy-start.25 = (f32[6,384]{1,0:T(8,128)S(1)}, f32[6,384]{1,0:T(8,128)}, u32[]{:S(2)}) copy-start(f32[6,384]{1,0:T(8,128)} %param.42) | copy-start | bytes 27652
  154.8 23.3 %copy-start.30 = (f32[6,384]{1,0:T(8,128)S(1)}, f32[6,384]{1,0:T(8,128)}, u32[]{:S(2)}) copy-start(f32[6,384]{1,0:T(8,128)} %param.57) | copy-start | bytes 27652
  155.8 1.3 collective-permute-start.36
  157.1 3.9 %collective-permute-start.37 = (bf16[32,384]{1,0:T(8,128)(2,1)S(1)}, bf16[32,384]{1,0:T(8,128)(2,1)S(1)}, u32[]{:S(2)}, u32[]{:S(2)}) collective-permute-start(bf16[32,384]{1,0:T(8,128)(2,1)S(1)} %fusion.12), channel_id=1, source_target_pairs={{0,2},{1,3},{2,0},{3,1},{4,6},{5,7},{6,4},{7,5},{8,10},{9,11},{10,... | collective-permute-start | bytes 73736 | tf_op jit(solution)/shard_map/ppermute | solution.py:387
  158.8 3.8 %collective-permute-start.38 = (bf16[32,384]{1,0:T(8,128)(2,1)S(1)}, bf16[32,384]{1,0:T(8,128)(2,1)S(1)}, u32[]{:S(2)}, u32[]{:S(2)}) collective-permute-start(bf16[32,384]{1,0:T(8,128)(2,1)S(1)} %fusion.12), channel_id=1, source_target_pairs={{0,4},{1,5},{2,6},{3,7},{4,0},{5,1},{6,2},{7,3},{8,12},{9,13},{10,... | collective-permute-start | bytes 73736 | tf_op jit(solution)/shard_map/ppermute | solution.py:387
  159.8 4.7 %collective-permute-start.39 = (bf16[32,384]{1,0:T(8,128)(2,1)S(1)}, bf16[32,384]{1,0:T(8,128)(2,1)S(1)}, u32[]{:S(2)}, u32[]{:S(2)}) collective-permute-start(bf16[32,384]{1,0:T(8,128)(2,1)S(1)} %fusion.12), channel_id=1, source_target_pairs={{0,6},{1,7},{2,4},{3,5},{4,2},{5,3},{6,0},{7,1},{8,14},{9,15},{10,... | collective-permute-start | bytes 73736 | tf_op jit(solution)/shard_map/ppermute | solution.py:387
  164.6 5.1 %collective-permute-start.40 = (bf16[32,384]{1,0:T(8,128)(2,1)S(1)}, bf16[32,384]{1,0:T(8,128)(2,1)S(1)}, u32[]{:S(2)}, u32[]{:S(2)}) collective-permute-start(bf16[32,384]{1,0:T(8,128)(2,1)S(1)} %fusion.23), channel_id=1, source_target_pairs={{0,8},{1,9},{2,10},{3,11},{4,12},{5,13},{6,14},{7,15},{8,0},{9,1},... | collective-permute-start | bytes 73736 | tf_op jit(solution)/shard_map/ppermute | solution.py:387
  165.0 5.6 %collective-permute-start.41 = (bf16[32,384]{1,0:T(8,128)(2,1)S(1)}, bf16[32,384]{1,0:T(8,128)(2,1)}, u32[]{:S(2)}, u32[]{:S(2)}) collective-permute-start(bf16[32,384]{1,0:T(8,128)(2,1)S(1)} %fusion.23), channel_id=1, source_target_pairs={{0,16},{1,17},{2,18},{3,19},{4,20},{5,21},{6,22},{7,23},{8,24},{9,... | collective-permute-start | bytes 73736 | tf_op jit(solution)/shard_map/ppermute | solution.py:387
  168.7 5.7 %collective-permute-start.42 = (bf16[32,384]{1,0:T(8,128)(2,1)S(1)}, bf16[32,384]{1,0:T(8,128)(2,1)}, u32[]{:S(2)}, u32[]{:S(2)}) collective-permute-start(bf16[32,384]{1,0:T(8,128)(2,1)S(1)} %fusion.23), channel_id=1, source_target_pairs={{0,24},{1,25},{2,26},{3,27},{4,28},{5,29},{6,30},{7,31},{8,16},{9,... | collective-permute-start | bytes 73736 | tf_op jit(solution)/shard_map/ppermute | solution.py:387
  169.0 23.0 %collective-permute-start.29 = (bf16[768,768]{1,0:T(8,128)(2,1)}, bf16[768,768]{1,0:T(8,128)(2,1)S(1)}, u32[]{:S(2)}, u32[]{:S(2)}) collective-permute-start(bf16[768,768]{1,0:T(8,128)(2,1)} %get-tuple-element.63), channel_id=1, source_target_pairs={{0,1},{1,0},{2,3},{3,2},{4,5},{5,4},{6,7},{7,6},{8,9},{9,8},{10,11... | collective-permute-start | bytes 3538952 | tf_op jit(solution)/shard_map/ppermute | solution.py:387
  169.1 10.3 %collective-permute-start.22 = (bf16[768,384]{1,0:T(8,128)(2,1)S(1)}, bf16[768,384]{1,0:T(8,128)(2,1)S(1)}, u32[]{:S(2)}, u32[]{:S(2)}) collective-permute-start(bf16[768,384]{1,0:T(8,128)(2,1)S(1)} %slice.202), channel_id=1, source_target_pairs={{0,1},{1,0},{2,3},{3,2},{4,5},{5,4},{6,7},{7,6},{8,9},{9,8},{10,11... | collective-permute-start | bytes 1769480 | tf_op jit(solution)/shard_map/ppermute | solution.py:387
  179.6 12.4 %copy-start.11 = (bf16[768,768]{1,0:T(8,128)(2,1)S(1)}, bf16[768,768]{1,0:T(8,128)(2,1)}, u32[]{:S(2)}) copy-start(bf16[768,768]{1,0:T(8,128)(2,1)} %get-tuple-element.62) | copy-start | bytes 3538948
  179.7 5.2 %collective-permute-start.23 = (bf16[192,384]{1,0:T(8,128)(2,1)S(1)}, bf16[192,384]{1,0:T(8,128)(2,1)S(1)}, u32[]{:S(2)}, u32[]{:S(2)}) collective-permute-start(bf16[192,384]{1,0:T(8,128)(2,1)S(1)} %get-tuple-element.155), channel_id=1, source_target_pairs={{0,2},{1,3},{2,0},{3,1},{4,6},{5,7},{6,4},{7,5},{8,10},{9,11},{10,... | collective-permute-start | bytes 442376 | tf_op jit(solution)/shard_map/ppermute | solution.py:387
  180.4 5.1 %collective-permute-start.24 = (bf16[192,384]{1,0:T(8,128)(2,1)S(1)}, bf16[192,384]{1,0:T(8,128)(2,1)S(1)}, u32[]{:S(2)}, u32[]{:S(2)}) collective-permute-start(bf16[192,384]{1,0:T(8,128)(2,1)S(1)} %get-tuple-element.157), channel_id=1, source_target_pairs={{0,4},{1,5},{2,6},{3,7},{4,0},{5,1},{6,2},{7,3},{8,12},{9,13},{10,... | collective-permute-start | bytes 442376 | tf_op jit(solution)/shard_map/ppermute | solution.py:387
  181.4 6.0 %collective-permute-start.25 = (bf16[192,384]{1,0:T(8,128)(2,1)S(1)}, bf16[192,384]{1,0:T(8,128)(2,1)S(1)}, u32[]{:S(2)}, u32[]{:S(2)}) collective-permute-start(bf16[192,384]{1,0:T(8,128)(2,1)S(1)} %get-tuple-element.156), channel_id=1, source_target_pairs={{0,6},{1,7},{2,4},{3,5},{4,2},{5,3},{6,0},{7,1},{8,14},{9,15},{10,... | collective-permute-start | bytes 442376 | tf_op jit(solution)/shard_map/ppermute | solution.py:387
  187.6 8.2 %collective-permute-start.26 = (bf16[48,384]{1,0:T(8,128)(2,1)S(1)}, bf16[48,384]{1,0:T(8,128)(2,1)S(1)}, u32[]{:S(2)}, u32[]{:S(2)}) collective-permute-start(bf16[48,384]{1,0:T(8,128)(2,1)S(1)} %get-tuple-element.161), channel_id=1, source_target_pairs={{0,8},{1,9},{2,10},{3,11},{4,12},{5,13},{6,14},{7,15},{8,0},{9,1},... | collective-permute-start | bytes 110600 | tf_op jit(solution)/shard_map/ppermute | solution.py:387
  187.6 9.2 %collective-permute-start.27 = (bf16[48,384]{1,0:T(8,128)(2,1)S(1)}, bf16[48,384]{1,0:T(8,128)(2,1)S(1)}, u32[]{:S(2)}, u32[]{:S(2)}) collective-permute-start(bf16[48,384]{1,0:T(8,128)(2,1)S(1)} %get-tuple-element.163), channel_id=1, source_target_pairs={{0,16},{1,17},{2,18},{3,19},{4,20},{5,21},{6,22},{7,23},{8,24},{9,... | collective-permute-start | bytes 110600 | tf_op jit(solution)/shard_map/ppermute | solution.py:387
  189.4 7.5 %collective-permute-start.28 = (bf16[48,384]{1,0:T(8,128)(2,1)S(1)}, bf16[48,384]{1,0:T(8,128)(2,1)S(1)}, u32[]{:S(2)}, u32[]{:S(2)}) collective-permute-start(bf16[48,384]{1,0:T(8,128)(2,1)S(1)} %get-tuple-element.162), channel_id=1, source_target_pairs={{0,24},{1,25},{2,26},{3,27},{4,28},{5,29},{6,30},{7,31},{8,16},{9,... | collective-permute-start | bytes 110600 | tf_op jit(solution)/shard_map/ppermute | solution.py:387
  193.4 7.0 %collective-permute-start.30 = (bf16[192,768]{1,0:T(8,128)(2,1)}, bf16[192,768]{1,0:T(8,128)(2,1)S(1)}, u32[]{:S(2)}, u32[]{:S(2)}) collective-permute-start(bf16[192,768]{1,0:T(8,128)(2,1)} %get-tuple-element.152), channel_id=1, source_target_pairs={{0,2},{1,3},{2,0},{3,1},{4,6},{5,7},{6,4},{7,5},{8,10},{9,11},{10,... | collective-permute-start | bytes 884744 | tf_op jit(solution)/shard_map/ppermute | solution.py:387
  194.8 10.1 %collective-permute-start.31 = (bf16[192,768]{1,0:T(8,128)(2,1)}, bf16[192,768]{1,0:T(8,128)(2,1)S(1)}, u32[]{:S(2)}, u32[]{:S(2)}) collective-permute-start(bf16[192,768]{1,0:T(8,128)(2,1)} %get-tuple-element.154), channel_id=1, source_target_pairs={{0,4},{1,5},{2,6},{3,7},{4,0},{5,1},{6,2},{7,3},{8,12},{9,13},{10,... | collective-permute-start | bytes 884744 | tf_op jit(solution)/shard_map/ppermute | solution.py:387
  195.8 9.2 %collective-permute-start.32 = (bf16[192,768]{1,0:T(8,128)(2,1)}, bf16[192,768]{1,0:T(8,128)(2,1)S(1)}, u32[]{:S(2)}, u32[]{:S(2)}) collective-permute-start(bf16[192,768]{1,0:T(8,128)(2,1)} %get-tuple-element.153), channel_id=1, source_target_pairs={{0,6},{1,7},{2,4},{3,5},{4,2},{5,3},{6,0},{7,1},{8,14},{9,15},{10,... | collective-permute-start | bytes 884744 | tf_op jit(solution)/shard_map/ppermute | solution.py:387
  198.6 11.0 %copy-start.20 = (f32[96,48]{0,1:T(8,128)S(1)}, f32[96,48]{0,1:T(8,128)}, u32[]{:S(2)}) copy-start(f32[96,48]{0,1:T(8,128)} %param.36) | copy-start | bytes 55300
  198.6 11.0 %copy-start.26 = (f32[96,48]{0,1:T(8,128)S(1)}, f32[96,48]{0,1:T(8,128)}, u32[]{:S(2)}) copy-start(f32[96,48]{0,1:T(8,128)} %param.45) | copy-start | bytes 55300
  198.6 11.0 %copy-start.27 = (f32[96,48]{0,1:T(8,128)S(1)}, f32[96,48]{0,1:T(8,128)}, u32[]{:S(2)}) copy-start(f32[96,48]{0,1:T(8,128)} %param.46) | copy-start | bytes 55300
  204.9 10.5 %copy-start.18 = (f32[384,48]{0,1:T(8,128)S(1)}, f32[384,48]{0,1:T(8,128)}, u32[]{:S(2)}) copy-start(f32[384,48]{0,1:T(8,128)} %param.38) | copy-start | bytes 221188
  204.9 10.5 %copy-start.21 = (f32[384,48]{0,1:T(8,128)S(1)}, f32[384,48]{0,1:T(8,128)}, u32[]{:S(2)}) copy-start(f32[384,48]{0,1:T(8,128)} %param.49) | copy-start | bytes 221188
  204.9 10.5 %copy-start.22 = (f32[384,48]{0,1:T(8,128)S(1)}, f32[384,48]{0,1:T(8,128)}, u32[]{:S(2)}) copy-start(f32[384,48]{0,1:T(8,128)} %param.50) | copy-start | bytes 221188
  204.9 11.2 %copy-start.19 = (f32[48,384]{1,0:T(8,128)S(1)}, f32[48,384]{1,0:T(8,128)}, u32[]{:S(2)}) copy-start(f32[48,384]{1,0:T(8,128)} %param.37) | copy-start | bytes 221188
  205.0 11.2 %copy-start.23 = (f32[48,384]{1,0:T(8,128)S(1)}, f32[48,384]{1,0:T(8,128)}, u32[]{:S(2)}) copy-start(f32[48,384]{1,0:T(8,128)} %param.47) | copy-start | bytes 221188
  205.0 11.2 %copy-start.24 = (f32[48,384]{1,0:T(8,128)S(1)}, f32[48,384]{1,0:T(8,128)}, u32[]{:S(2)}) copy-start(f32[48,384]{1,0:T(8,128)} %param.48) | copy-start | bytes 221188
  205.2 5.2 %collective-permute-start.33 = (bf16[48,768]{1,0:T(8,128)(2,1)S(1)}, bf16[48,768]{1,0:T(8,128)(2,1)S(1)}, u32[]{:S(2)}, u32[]{:S(2)}) collective-permute-start(bf16[48,768]{1,0:T(8,128)(2,1)S(1)} %get-tuple-element.158), channel_id=1, source_target_pairs={{0,8},{1,9},{2,10},{3,11},{4,12},{5,13},{6,14},{7,15},{8,0},{9,1},... | collective-permute-start | bytes 221192 | tf_op jit(solution)/shard_map/ppermute | solution.py:387
  205.7 6.7 %collective-permute-start.34 = (bf16[48,768]{1,0:T(8,128)(2,1)S(1)}, bf16[48,768]{1,0:T(8,128)(2,1)S(1)}, u32[]{:S(2)}, u32[]{:S(2)}) collective-permute-start(bf16[48,768]{1,0:T(8,128)(2,1)S(1)} %get-tuple-element.160), channel_id=1, source_target_pairs={{0,16},{1,17},{2,18},{3,19},{4,20},{5,21},{6,22},{7,23},{8,24},{9,... | collective-permute-start | bytes 221192 | tf_op jit(solution)/shard_map/ppermute | solution.py:387
  209.2 6.2 %collective-permute-start.35 = (bf16[48,768]{1,0:T(8,128)(2,1)S(1)}, bf16[48,768]{1,0:T(8,128)(2,1)S(1)}, u32[]{:S(2)}, u32[]{:S(2)}) collective-permute-start(bf16[48,768]{1,0:T(8,128)(2,1)S(1)} %get-tuple-element.159), channel_id=1, source_target_pairs={{0,24},{1,25},{2,26},{3,27},{4,28},{5,29},{6,30},{7,31},{8,16},{9,... | collective-permute-start | bytes 221192 | tf_op jit(solution)/shard_map/ppermute | solution.py:387
  (14 other events, 51.3 us)

commit v2 on v1

v2 whole, which is shorter than its diff:
```python
import functools
import math

import jax
import jax.numpy as jnp
import numpy as np
from jax import lax
from jax.experimental import pallas as pl
from jax.experimental.pallas import tpu as pltpu
from jax.sharding import PartitionSpec as P

HEAD_DIM = 32
WINDOW = 7
SIDE = 14
SHIFT = 3
STEP = 10
CANVAS = SIDE * SIDE
PLACES = WINDOW * WINDOW
SLOT = 64
QUAD_ROWS = 4 * CANVAS
SPAN = 208
WIDTH = 384
GROUPS = 3
PACK = 4
HIDDEN = 1536
CHUNK = 512

NORM_EPS = 1e-05
BETA_ONE = 0.9
BETA_TWO = 0.999
ADAM_EPS = 1e-08
RATE_MATRIX = 0.1
RATE_SMALL = 0.5
DECAY_MATRIX = 0.05
MASKED = -1e30
LOG2E = math.log2(math.e)
SCALE = HEAD_DIM**-0.5
ROOT_HALF = 0.7071067811865476
INV_ROOT_TWO_PI = 1.0 / 2.5066282746310002
BF = jnp.bfloat16
F32 = jnp.float32


def slot_rows():
    rows = -np.ones((4, SLOT), np.int64)
    for win in range(4):
        for place in range(PLACES):
            row = (win // 2) * WINDOW + place // WINDOW
            col = (win % 2) * WINDOW + place % WINDOW
            rows[win, place] = ((row + SHIFT) % SIDE) * SIDE + (col + SHIFT) % SIDE
    return rows.reshape(-1)


def region_codes():
    def band(v):
        return 0 if v < SIDE - WINDOW else (1 if v < SIDE - SHIFT else 2)

    codes = np.full((4, SLOT), 999.0, np.float32)
    for win in range(4):
        for place in range(PLACES):
            row = (win // 2) * WINDOW + place // WINDOW
            col = (win % 2) * WINDOW + place % WINDOW
            codes[win, place] = 4 * (3 * band(row) + band(col))
    return codes.reshape(-1)


def tables():
    line = np.array([13 * (p // WINDOW) + p % WINDOW for p in range(PLACES)], np.float32)
    out = np.full((8, 4 * SLOT), -1000.0, np.float32)
    out[0] = slot_rows()
    out[0][out[0] < 0] = -1000.0
    out[1] = region_codes()
    out[2, :PLACES] = 43 + line
    out[3, :PLACES] = out[3, SLOT : SLOT + PLACES] = 84 - line
    out[4, :PLACES] = line
    return out, out.T.copy()


def onehot(shape, axis, places):
    index = lax.broadcasted_iota(jnp.int32, shape, axis).astype(F32)
    return jnp.where(index == places, 1.0, 0.0).astype(BF)


def dot_nn(a, b):
    return jnp.dot(a, b, preferred_element_type=F32)


def dot_nt(a, b):
    return lax.dot_general(a, b, (((1,), (1,)), ((), ())), preferred_element_type=F32)


def stats(values):
    centred = values - jnp.mean(values, axis=-1, keepdims=True)
    inv_std = lax.rsqrt(jnp.mean(centred * centred, axis=-1, keepdims=True) + NORM_EPS)
    return centred * inv_std, inv_std


def norm_back(grad_norm, hat, inv_std, gain_row):
    grad_hat = grad_norm * gain_row
    inner = grad_hat - jnp.mean(grad_hat, axis=-1, keepdims=True)
    return inv_std * (inner - hat * jnp.mean(grad_hat * hat, axis=-1, keepdims=True))


def owners(idx):
    z, y, x, c = idx[0], idx[1], idx[2], idx[3]
    for e in range(2):
        for k in range(4):
            for s in range(4):
                row = ((z ^ s) * 2 + (y ^ (k >> 1))) * 48
                yield e, k, s, pl.multiple_of(row, 16), (x ^ (k & 1)) * 2 + (c ^ e)


def spread(block):
    four = jnp.concatenate([block] * PACK, axis=1)
    rows = lax.broadcasted_iota(jnp.int32, four.shape, 0) // HEAD_DIM
    lanes = lax.broadcasted_iota(jnp.int32, four.shape, 1) // SLOT
    return jnp.where(rows == lanes, four, jnp.zeros_like(four))


def assemble(idx, refs, put):
    for e, k, s, row, head in owners(idx):
        put(row, head, refs[e * 4 + k][s * 48 : (s + 1) * 48, :])


UNITS = [(win, g) for win in range(4) for g in range(GROUPS)]


def window(win):
    return slice(win * SLOT, (win + 1) * SLOT)


def feats(g):
    return slice(g * 128, (g + 1) * 128)


def own_blocks(parts):
    rows = []
    for g in range(GROUPS):
        for h in range(PACK):
            rows.append(
                jnp.concatenate(
                    [
                        parts[win, g][
                            h * HEAD_DIM : (h + 1) * HEAD_DIM, h * SLOT : (h + 1) * SLOT
                        ]
                        for win in range(4)
                    ],
                    axis=1,
                )
            )
    return jnp.concatenate(rows, axis=0)


def canvas_start(step):
    return pl.multiple_of((step // 4) * QUAD_ROWS + (step % 4) * 192, 16)


def pack_attention(qkv, out_t, first):
    first[...] = jnp.concatenate([qkv[0], qkv[1], qkv[2], out_t[...]], axis=1).astype(BF)


def pack_mlp(expand, contract_t, qv, eb, table_t, second, own):
    second[:, 0:WIDTH] = expand[...].astype(BF)
    second[:, WIDTH:] = contract_t[...].astype(BF)
    own[...] = jnp.zeros(own.shape, BF)
    own[0:2, 0:96] = qv[...].astype(BF)
    own[2:3, :] = eb[...].reshape(1, -1).astype(BF)
    own[3:6, 0 : table_t.shape[1]] = table_t[...].astype(BF)


def prepare(
    idx, own, by_c, by_x, by_xc, tok, gout, crop, rows_c, cols_c, par_h,
    na, xt, ut, u, tokv, goutv, got, tb, bias, eb, code_row, code_col, par, down, across,
    sbuf,
):
    x, c = idx[2], idx[3]
    for ref, dx, dc in ((own, 0, 0), (by_c, 0, 1), (by_x, 1, 0), (by_xc, 1, 1)):
        sbuf[(x ^ dx) * 2 + (c ^ dc)] = ref[...].astype(F32)
    pad = jnp.zeros((1, WIDTH), F32)
    qv = [jnp.concatenate([sbuf[h, r : r + 1, 0:96] for h in range(4)], axis=1) for r in (0, 1)]
    bias[0:16, :] = jnp.concatenate(
        [jnp.concatenate([qv[0], pad, qv[1]], axis=1), jnp.zeros((15, 3 * WIDTH), F32)], axis=0
    ).astype(BF)
    eb[...] = jnp.concatenate(
        [
            jnp.concatenate([sbuf[h, 2:3, :] for h in range(4)], axis=1),
            jnp.zeros((15, HIDDEN), F32),
        ],
        axis=0,
    ).astype(BF)
    up = onehot((SLOT, 128), 1, cols_c[0:SLOT, 2:3])
    down[...] = onehot((128, 2 * SLOT), 0, rows_c[3:4, 0 : 2 * SLOT])
    over = onehot((256, SLOT), 0, rows_c[4:5, 0:SLOT])
    across[...] = over
    for g in range(GROUPS):
        blocks = []
        for h in range(g * PACK, (g + 1) * PACK):
            row = sbuf[h // 3, 3 + h % 3 : 4 + h % 3, 0:256]
            lines = pltpu.roll(
                jnp.broadcast_to(row, (128, 256)), 129, axis=1, stride=1, stride_axis=0
            )
            keyed = dot_nn(up, lines.astype(BF)).astype(BF)
            blocks.append(dot_nn(keyed, over))
        tb[g] = jnp.concatenate(blocks, axis=1) * LOG2E
    tokv[...] = tok[...]
    goutv[...] = gout[...]
    par[...] = jnp.concatenate([par_h[...], jnp.zeros((2, WIDTH), F32)], axis=0)
    lane = lax.broadcasted_iota(jnp.int32, (4 * SLOT, 128), 1)
    ones = jnp.where(lane == 0, 1.0, 0.0).astype(BF)
    to_slots = []
    for turn in range(4):
        ut[turn] = onehot((4 * SLOT, SPAN), 1, cols_c[:, 0:1] + 4.0 * turn)
        u[turn] = onehot((SPAN, 4 * SLOT), 0, rows_c[0:1, :] + 4.0 * turn)
        to_slots.append(ut[turn])
    head = idx[2] * 2 + idx[3]
    for block in range(na.shape[0] // 4):
        hat, _ = stats(tok[block * QUAD_ROWS : (block + 1) * QUAD_ROWS, :].astype(F32))
        n1 = (hat * par_h[0:1, :] + par_h[1:2, :]).astype(BF)
        sides = jnp.concatenate([n1, hat.astype(BF)], axis=1)
        crops = crop[pl.ds(head * (na.shape[0] // 4) + block, 1), :] & 3
        for turn in range(4):
            step, start = 4 * block + turn, 192 * turn
            both = dot_nn(to_slots[turn], sides[start : start + SPAN]).astype(BF)
            na[step] = jnp.concatenate([both[:, 0:WIDTH], ones], axis=1)
            xt[step] = jnp.concatenate([both[:, WIDTH:], ones], axis=1).T[0:400, :]
            quad = crops[:, start : start + SPAN]
            quad = jnp.broadcast_to(quad.astype(F32), (8, SPAN)).astype(BF)
            code_row[step] = dot_nt(quad, to_slots[turn]) + rows_c[1:2, :]
            code_col[step] = dot_nt(to_slots[turn], quad) + cols_c[:, 1:2]
    got[...] = gout[...].T


def attention_forward(
    idx, p0, p1, p2, p3, p4, p5, p6, p7, nas, codes_row, codes_col, u, bias, tb,
    mrg, qt, kt, vv, pt, mt, wnat, outt, wout,
    wbuf, waug, wt,
):
    def put(row, head, value):
        wbuf[head, pl.ds(row, 48), :] = value

    assemble(idx, (p0, p1, p2, p3, p4, p5, p6, p7), put)
    for j in range(3):
        waug[0:WIDTH, j * WIDTH : (j + 1) * WIDTH] = jnp.concatenate(
            [wbuf[h, :, 96 * j : 96 * (j + 1)] for h in range(4)], axis=1
        )
    out_t = jnp.concatenate([wbuf[h, :, 288:384] for h in range(4)], axis=1)
    outt[...] = out_t
    wout[...] = out_t.T
    waug[WIDTH : WIDTH + 16, :] = bias[...]
    waug[WIDTH + 16 : 512, :] = jnp.zeros((112, 3 * WIDTH), BF)
    wnat[...] = waug[0:WIDTH, :]
    wt[...] = waug[...].T

    def canvas(step, carry):
        turn = step % 4
        start = canvas_start(step)
        na = nas[step]
        all_t = dot_nt(wt[...], na).astype(BF)
        kv = dot_nt(na, wt[WIDTH:, :]).astype(BF)
        q_t, v_t = all_t[0:WIDTH], all_t[2 * WIDTH :]
        code_row, code_col = codes_row[step], codes_col[step]
        masks = []
        for win in range(4):
            row = jnp.concatenate([code_row[0:1, window(win)]] * PACK, axis=1)
            masks.append(jnp.where(code_col[window(win), 0:1] == row, 0.0, MASKED))
        scores = {
            (w, g): dot_nn(kv[window(w), feats(g)], spread(q_t[feats(g), window(w)]))
            for w, g in UNITS
        }
        probs = {}
        for w, g in UNITS:
            sc = scores[w, g] * (SCALE * LOG2E) + (tb[g] + masks[w])
            grown = jnp.exp2(sc - jnp.max(sc, axis=0, keepdims=True))
            probs[w, g] = (grown * (1.0 / jnp.sum(grown, axis=0, keepdims=True))).astype(BF)
        mixed = {(w, g): dot_nn(v_t[feats(g), window(w)], probs[w, g]) for w, g in UNITS}
        merged_t = own_blocks(mixed).astype(BF)
        back = dot_nt(u[turn], merged_t).astype(BF)
        for w, g in UNITS:
            pt[step, w * GROUPS + g] = probs[w, g]
        mt[step] = merged_t
        qt[step] = q_t
        kt[step] = all_t[WIDTH : 2 * WIDTH]
        vv[step] = kv[:, WIDTH:]
        begin = pl.ds(start, 16)
        mrg[begin, :] = back[0:16] + jnp.where(turn == 0, jnp.zeros((16, WIDTH), BF), mrg[begin, :])
        mrg[pl.ds(pl.multiple_of(start + 16, 16), SPAN - 16), :] = back[16:]
        return carry

    lax.fori_loop(0, nas.shape[0], canvas, 0)


TILE = 784


def mlp_begin(mrg, tok, outt, par, mid, n2, n2t):
    lane = lax.broadcasted_iota(jnp.int32, (TILE, 128), 1)
    ones = jnp.where(lane == 0, 1.0, 0.0).astype(BF)

    def head_rows(t, carry):
        rows = pl.ds(pl.multiple_of(t * TILE, 16), TILE)
        middle = tok[rows, :].astype(F32) + dot_nt(mrg[rows, :], outt[...]) + par[4:5, :]
        mid[rows, :] = middle
        hat, _ = stats(middle)
        n2[rows, 0:WIDTH] = (hat * par[2:3, :] + par[3:4, :]).astype(BF)
        n2[rows, WIDTH:512] = ones
        return carry

    lax.fori_loop(0, tok.shape[0] // TILE, head_rows, 0)
    n2t[...] = n2[...].T[0:400, :]


def mlp(
    idx, p0, p1, p2, p3, p4, p5, p6, p7, n2, n2t, got, gout, eb,
    acc_m, acc_g, keep, send, ebg,
    eaug, ct, hid, gpr, cg, eg,
):
    tiles = gout.shape[0] // TILE

    def put(row, head, value):
        lanes = pl.ds(pl.multiple_of(head * WIDTH, 128), WIDTH)
        eaug[pl.ds(row, 48), lanes] = value[:, 0:WIDTH]
        ct[pl.ds(row, 48), lanes] = value[:, WIDTH:]

    assemble(idx, (p0, p1, p2, p3, p4, p5, p6, p7), put)
    eaug[WIDTH : WIDTH + 16, :] = eb[...]
    eaug[WIDTH + 16 : 512, :] = jnp.zeros((112, HIDDEN), BF)
    acc_m[...] = jnp.zeros(acc_m.shape, F32)
    acc_g[...] = jnp.zeros(acc_g.shape, F32)

    def chunk(step, carry):
        cols = pl.ds(pl.multiple_of(step * CHUNK, 128), CHUNK)

        def unit_rows(t, carry):
            rows = pl.ds(pl.multiple_of(t * TILE, 16), TILE)
            pre = dot_nn(n2[rows, :], eaug[:, cols])
            grad_hidden = dot_nn(gout[rows, :], ct[:, cols])
            phi = 0.5 + 0.5 * lax.erf(pre * ROOT_HALF)
            bell = jnp.exp2(pre * pre * (-0.5 * LOG2E)) * INV_ROOT_TWO_PI
            hidden = (pre * phi).astype(BF)
            grad_pre = (grad_hidden * (phi + pre * bell)).astype(BF)
            hid[rows, :] = hidden
            gpr[rows, :] = grad_pre
            acc_m[rows, :] += dot_nt(hidden, ct[:, cols])
            acc_g[rows, :] += dot_nt(grad_pre, eaug[0:WIDTH, cols])
            return carry

        lax.fori_loop(0, tiles, unit_rows, 0)
        cg[:, cols] = dot_nn(got[...], hid[...]).astype(BF)
        grads = dot_nn(n2t[...], gpr[...])
        eg[:, cols] = grads[0:WIDTH].astype(BF)
        ebg[:, cols] = grads[WIDTH : WIDTH + 8]
        return carry

    lax.fori_loop(0, HIDDEN // CHUNK, chunk, 0)
    for e, k, s, row, head in owners(idx):
        dst = (keep, send)[e]
        lanes = pl.ds(pl.multiple_of(head * WIDTH, 128), WIDTH)
        base = (k * 4 + s) * 48
        dst[base : base + 48, 0:WIDTH] = eg[pl.ds(row, 48), lanes]
        dst[base : base + 48, WIDTH:] = cg[pl.ds(row, 48), lanes]


def mlp_end(mid, acc_m, acc_g, gout, par, blk, gmid, sums):
    def tail_rows(t, carry):
        rows = pl.ds(pl.multiple_of(t * TILE, 16), TILE)
        middle = mid[rows, :]
        blk[rows, :] = (middle + acc_m[rows, :] + par[5:6, :]).astype(BF)
        hat, inv = stats(middle)
        g = acc_g[rows, :]
        top = gout[rows, :].astype(F32)
        grad_mid = top + norm_back(g, hat, inv, par[2:3, :])
        gmid[rows, :] = grad_mid
        parts = (g * hat, g, grad_mid, top)
        return tuple(c + jnp.sum(p, axis=0, keepdims=True) for c, p in zip(carry, parts))

    zero = jnp.zeros((1, WIDTH), F32)
    totals = lax.fori_loop(0, mid.shape[0] // TILE, tail_rows, (zero,) * 4)
    sums[...] = jnp.concatenate([zero, zero, *totals, zero, zero], axis=0)


def attention_backward(
    idx, gmid, qt, kt, vv, pt, mt, xt, wout, ut, wnat, par, sums, ebg, down, across,
    keep, send, gta,
    ntall, wacc, oacc, table,
):
    table[...] = jnp.zeros(table.shape, F32)
    oacc[...] = jnp.zeros(oacc.shape, F32)
    wacc[...] = jnp.zeros(wacc.shape, F32)

    def canvas(step, carry):
        turn = step % 4
        rows = pl.ds(canvas_start(step), SPAN)
        gmw = dot_nn(ut[turn], gmid[rows, :].astype(BF)).astype(BF)
        gmt = dot_nt(wout[...], gmw).astype(BF)
        q_t, k_t, v_w = qt[step], kt[step], vv[step]
        gm_s = {(w, g): spread(gmt[feats(g), window(w)]) for w, g in UNITS}
        q_s = {(w, g): spread(q_t[feats(g), window(w)]) for w, g in UNITS}
        gp = {(w, g): dot_nn(v_w[window(w), feats(g)], gm_s[w, g]) for w, g in UNITS}
        probs_b = {(w, g): pt[step, w * GROUPS + g] for w, g in UNITS}
        gs = {}
        for w, g in UNITS:
            probs = probs_b[w, g].astype(F32)
            delta = jnp.sum(probs * gp[w, g], axis=0, keepdims=True)
            gs[w, g] = (probs * (gp[w, g] - delta)).astype(BF)
        gq = {(w, g): dot_nn(k_t[feats(g), window(w)], gs[w, g]) for w, g in UNITS}
        gk = {(w, g): dot_nt(q_s[w, g], gs[w, g]) for w, g in UNITS}
        gv = {(w, g): dot_nt(gm_s[w, g], probs_b[w, g]) for w, g in UNITS}

        def rows_of(parts):
            return jnp.concatenate(
                [
                    jnp.concatenate([parts[w, g] for w in range(4)], axis=1)
                    for g in range(GROUPS)
                ],
                axis=0,
            )

        g_all = jnp.concatenate(
            [
                (own_blocks(gq) * SCALE).astype(BF),
                (rows_of(gk) * SCALE).astype(BF),
                rows_of(gv).astype(BF),
            ],
            axis=0,
        )
        gta[step] = g_all
        wacc[...] += dot_nt(xt[step], g_all)
        oacc[...] += dot_nn(mt[step], gmw)
        for g in range(GROUPS):
            table[g] += sum(gs[w, g].astype(F32) for w in range(4))
        return carry

    lax.fori_loop(0, qt.shape[0], canvas, 0)
    columns = par[...].T
    gain, offset = columns[:, 0:1], columns[:, 1:2]
    totals = wacc[WIDTH : WIDTH + 1, :]
    weights = wnat[...].astype(F32)
    gain_sum = jnp.sum(weights * wacc[0:WIDTH, :], axis=1, keepdims=True)
    offset_sum = jnp.sum(weights * totals, axis=1, keepdims=True)
    norm_rows = jnp.concatenate([gain_sum, offset_sum, jnp.zeros((WIDTH, 6), F32)], axis=1).T
    grads = wacc[0:WIDTH, :] * gain + offset * totals
    out_t = oacc[...].T
    for h in range(4):
        pieces = [grads[:, j * WIDTH + 96 * h : j * WIDTH + 96 * (h + 1)] for j in range(3)]
        pieces.append(out_t[:, 96 * h : 96 * (h + 1)])
        ntall[h] = jnp.concatenate(pieces, axis=1).astype(BF)
    for e, k, s, row, head in owners(idx):
        base = (k * 4 + s) * 48
        (keep, send)[e][base : base + 48, :] = ntall[head, pl.ds(row, 48), :]
    rows = [norm_rows[0:2, :], sums[2:6, :], totals[:, 0:WIDTH], totals[:, 2 * WIDTH :]]
    rows += [ebg[0:1, j * WIDTH : (j + 1) * WIDTH] for j in range(4)]
    for g in range(GROUPS):
        high = table[g].astype(BF)
        low = (table[g] - high.astype(F32)).astype(BF)
        both = jnp.concatenate([high, low], axis=0)
        for h in range(PACK):
            spaced = dot_nt(both[:, h * SLOT : (h + 1) * SLOT], across[...]).astype(BF)
            lines = dot_nn(down[...], spaced)
            lines = pltpu.roll(lines, 0, axis=1, stride=1, stride_axis=0)
            row = jnp.sum(lines, axis=0, keepdims=True)
            rows.append(jnp.concatenate([row, jnp.zeros((1, 128), F32)], axis=1))
    rows.append(jnp.zeros((8, WIDTH), F32))
    small = jnp.concatenate(rows, axis=0).astype(BF)
    keep[768:800, :] = small
    send[768:800, :] = small


def tokens_end(tok, gmid, gta, wnat, u, par, gtok):
    def block_rows(block, carry):
        ends = []
        for turn in range(4):
            g1t = dot_nn(wnat[...], gta[4 * block + turn])
            high = g1t.astype(BF)
            low = (g1t - high.astype(F32)).astype(BF)
            ends.append(dot_nt(u[turn], high) + dot_nt(u[turn], low))
        pieces = [ends[0][0:192]]
        for turn in range(1, 4):
            pieces += [ends[turn - 1][192:] + ends[turn][0:16], ends[turn][16:192]]
        g1 = jnp.concatenate([*pieces, ends[3][192:]], axis=0)
        rows = pl.ds(pl.multiple_of(block * QUAD_ROWS, 16), QUAD_ROWS)
        hat, inv = stats(tok[rows, :].astype(F32))
        gtok[rows, :] = gmid[rows, :] + norm_back(g1, hat, inv, par[0:1, :])
        return carry

    lax.fori_loop(0, gta.shape[0] // 4, block_rows, 0)


def plane_sum(keep, got, *refs):
    small = None
    if len(refs) > 4:
        small = keep[768:, :].astype(F32) + got[768:, :].astype(F32)
        refs[4][...] = small
    for k in range(4):
        block = slice(k * 192, (k + 1) * 192)
        value = keep[block, :].astype(F32) + got[block, :].astype(F32)
        if k == 0:
            refs[0][...] = value
        else:
            refs[k][0:192, :] = value.astype(BF)
            if small is not None:
                refs[k][192:, :] = small.astype(BF)


def line_sum(own, r1, r2, r3, *refs):
    small = None
    parts = (r1, r2, r3)
    if len(refs) > 4:
        mine, *refs = refs
        small = mine[...] + sum(r[192:, :].astype(F32) for r in parts)
        refs[4][...] = small
    for s in range(4):
        block = slice(s * 48, (s + 1) * 48)
        value = own[block, :] + sum(r[block, :].astype(F32) for r in parts)
        if s == 0:
            refs[0][...] = value
        else:
            refs[s][0:48, :] = value.astype(BF)
            if small is not None:
                refs[s][48:, :] = small.astype(BF)


def adamw(master, grad, moment, square, step_rate, decay_rate):
    moment_new = BETA_ONE * moment + (1.0 - BETA_ONE) * grad
    square_new = BETA_TWO * square + (1.0 - BETA_TWO) * grad * grad
    moment_hat = moment_new * (1.0 / (1.0 - BETA_ONE**STEP))
    square_hat = square_new * (1.0 / (1.0 - BETA_TWO**STEP))
    step = moment_hat / (jnp.sqrt(square_hat) + ADAM_EPS)
    if decay_rate:
        step = step + decay_rate * master
    return master - step_rate * step, moment_new, square_new


def update(refs, grad, outs, step_rate, decay_rate, at=...):
    master, moment, square = (r[at] for r in refs)
    news = adamw(master, grad, moment, square, step_rate, decay_rate)
    for out, new in zip(outs, news):
        out[at] = new


def step_mlp(n_parts, *refs):
    parts, refs = refs[:n_parts], refs[n_parts:]
    total = sum(r[...].astype(F32) for r in parts)
    update(refs[0:3], total[:, 0:WIDTH], refs[6:9], RATE_MATRIX, DECAY_MATRIX)
    update(refs[3:6], total[:, WIDTH:], refs[9:12], RATE_MATRIX, DECAY_MATRIX)


def step_attention(n_parts, rows, idx, *refs):
    parts, refs = refs[:n_parts], refs[n_parts:]
    total = sum(r[0:rows, :].astype(F32) for r in parts)
    small, refs = refs[0], refs[1:]
    small = small[...] + sum(r[rows:, :].astype(F32) for r in parts[1:])
    head = idx[2] * 2 + idx[3]

    def pick(blocks):
        return sum(jnp.where(head == h, block, 0.0) for h, block in enumerate(blocks))

    ins, outs = refs[:18], refs[18:]
    for j in range(3):
        update(
            ins[0:3], total[:, 96 * j : 96 * (j + 1)], outs[0:3], RATE_MATRIX, DECAY_MATRIX, at=j
        )
    update(ins[3:6], total[:, 288:384], outs[3:6], RATE_MATRIX, DECAY_MATRIX)
    qv = pick([small[6:8, 96 * h : 96 * (h + 1)] for h in range(4)])
    update(ins[6:9], qv, outs[6:9], RATE_SMALL, 0.0)
    eb = pick([small[8 + h : 9 + h, :] for h in range(4)])
    update(ins[9:12], eb.reshape(ins[9].shape), outs[9:12], RATE_SMALL, 0.0)
    table_rows = ins[12].shape[1]
    table = pick([small[12 + 3 * h : 15 + 3 * h, 0:table_rows] for h in range(4)])
    update(ins[12:15], table, outs[12:15], RATE_SMALL, 0.0)
    update(ins[15:18], small[0:6, :], outs[15:18], RATE_SMALL, 0.0)


class Links:
    def __init__(self, sizes):
        self.sizes = sizes
        self.outer = sizes["dp"] // 8

    def perm(self, z=0, y=0, x=0, c=0):
        pairs = []
        for flat in range(self.sizes["dp"] * self.sizes["head"]):
            head, dp = flat % 4, flat // 4
            inner, place = dp // self.outer, dp % self.outer
            inner ^= z * 2 + y
            pairs.append((flat, (inner * self.outer + place) * 4 + (head ^ (x * 2 + c))))
        return pairs

    def send(self, value, **flips):
        return lax.ppermute(value, ("dp", "head"), self.perm(**flips))

    def groups(self):
        return [[i * self.outer + j for j in range(self.outer)] for i in range(8)]

    def gather_line(self, shard):
        if self.outer > 1:
            shard = lax.all_gather(
                shard, "dp", axis=0, tiled=True, axis_index_groups=self.groups()
            )
        return jnp.concatenate([shard] + [self.send(shard, z=s) for s in range(1, 4)], axis=0)

    def gather_plane(self, line):
        return [line] + [self.send(line, x=k & 1, y=k >> 1) for k in range(1, 4)]

    def gather_core(self, plane):
        return list(plane) + [self.send(part, c=1) for part in plane]

    def to_plane(self, blocks):
        return [self.send(b, x=k & 1, y=k >> 1) for k, b in enumerate(blocks, 1)]

    def to_line(self, blocks):
        return [self.send(b, z=s) for s, b in enumerate(blocks, 1)]

    def outer_sum(self, value):
        if self.outer > 1:
            value = lax.psum_scatter(
                value, "dp", scatter_dimension=0, tiled=True, axis_index_groups=self.groups()
            )
        return value


SMEM = pl.BlockSpec(memory_space=pltpu.SMEM)
VMEM = pl.BlockSpec(memory_space=pltpu.VMEM)


class Far:
    def __init__(self, value):
        self.value = value


def placed(arg):
    if isinstance(arg, Far):
        return pltpu.with_memory_space_constraint(arg.value, pltpu.HBM)
    return pltpu.with_memory_space_constraint(arg, pltpu.VMEM)


def call(kernel, outs, *args, scratch=(), limit=16, scalars=None, far=(), time=1):
    lead = [] if scalars is None else [scalars]
    name = getattr(kernel, "__name__", None) or kernel.func.__name__
    return pl.pallas_call(
        kernel,
        in_specs=[SMEM] * len(lead) + [VMEM] * len(args),
        out_specs=[VMEM] * len(outs),
        out_shape=[(pltpu.HBM if i in far else pltpu.VMEM)(s, d) for i, (s, d) in enumerate(outs)],
        scratch_shapes=[pltpu.VMEM(s, d) for s, d in scratch],
        compiler_params=pltpu.CompilerParams(vmem_limit_bytes=limit * 2**20),
        cost_estimate=pl.CostEstimate(
            flops=int(time * 1.15e9), bytes_accessed=0, transcendentals=0
        ),
        name=name,
    )(*lead, *(placed(a) for a in args))


def per_device(links, *args):
    (
        tokens, crop_ids, grad_out, qkv_w, out_w, exp_w, con_w, qv_b, exp_b, table_w, norm_p,
        qkv_m, qkv_s, out_m, out_s, exp_m, exp_s, con_m, con_s,
        qv_m, qv_s, eb_m, eb_s, tab_m, tab_s, norm_m, norm_s,
    ) = args
    rows_all = tokens.shape[0]
    canvases = rows_all // CANVAS
    head = lax.axis_index("head")
    dp = lax.axis_index("dp") // links.outer
    idx = jnp.stack([dp // 2, dp % 2, head // 2, head % 2]).astype(jnp.int32)
    slots = 4 * SLOT
    wide = (rows_all, WIDTH)
    square = (WIDTH, WIDTH)
    fm = (canvases, WIDTH, slots)
    tm = (canvases, slots, WIDTH)

    rows_own = exp_w.shape[0]
    (first,) = call(pack_attention, [((rows_own, WIDTH), BF)], Far(qkv_w), Far(out_w.T))
    line = links.gather_line(first)
    firsts = links.gather_plane(line)
    second, own = call(
        pack_mlp, [((rows_own, 2 * WIDTH), BF), ((16, WIDTH), BF)],
        Far(exp_w), Far(con_w.T), Far(qv_b), Far(exp_b), Far(table_w.T),
    )
    by_c, by_x, by_xc = links.send(own, c=1), links.send(own, x=1), links.send(own, x=1, c=1)

    crop_rows = crop_ids.reshape(-1, QUAD_ROWS)
    rows_c, cols_c = (jnp.asarray(t) for t in tables())
    line, own = lax.optimization_barrier((line, own))
    to_slots = (4, slots, SPAN)
    prepared = call(
        prepare,
        [
            ((canvases, slots, 512), BF), ((canvases, 400, slots), BF), (to_slots, BF),
            ((4, SPAN, slots), BF), (wide, BF), (wide, BF), ((WIDTH, rows_all), BF),
            ((GROUPS, SLOT, slots), F32), ((16, 3 * WIDTH), BF), ((16, HIDDEN), BF),
            ((canvases, 8, slots), F32), ((canvases, slots, 8), F32), ((8, WIDTH), F32),
            ((128, 2 * SLOT), BF), ((256, SLOT), BF),
        ],
        own, by_c, by_x, by_xc, Far(tokens), Far(grad_out), Far(crop_rows), Far(rows_c),
        Far(cols_c), Far(norm_p),
        scratch=[((4, 16, WIDTH), F32)], limit=16, scalars=idx, time=5,
    )
    (second, *prepared) = lax.optimization_barrier((second, *prepared))
    nas, xt, ut, u, tok, gout, got, bias_t, bias16, eb16, code_row, code_col, par = prepared[:13]
    down, across = prepared[13:]
    line_s = links.gather_line(second)
    plane_s = links.gather_plane(line_s)
    firsts = list(lax.optimization_barrier((*firsts, nas))[:4])
    firsts = links.gather_core(firsts)
    firsts[0], line_s = lax.optimization_barrier((firsts[0], line_s))
    merged, qt, kt, vv, pt, mt, wnat, outt, wout = call(
        attention_forward,
        [
            (wide, BF), (fm, BF), (fm, BF), (tm, BF), ((canvases, 12, SLOT, slots), BF), (fm, BF),
            ((WIDTH, 3 * WIDTH), BF), (square, BF), (square, BF),
        ],
        *firsts, nas, code_row, code_col, u, bias16, bias_t,
        scratch=[
            ((4, WIDTH, WIDTH), BF), ((512, 3 * WIDTH), BF), ((3 * WIDTH, 512), BF),
        ],
        limit=10, scalars=idx, time=14,
    )
    merged, *plane_s = lax.optimization_barrier((merged, *plane_s))
    seconds = links.gather_core(plane_s)
    middle, n2, n2t = call(
        mlp_begin, [(wide, F32), ((rows_all, 512), BF), ((400, rows_all), BF)],
        merged, tok, outt, par, time=3,
    )
    acc_m, acc_g, keep_r, send_r, eb_grad = call(
        mlp,
        [
            (wide, F32), (wide, F32), ((768, 2 * WIDTH), BF), ((768, 2 * WIDTH), BF),
            ((8, HIDDEN), F32),
        ],
        *seconds, n2, n2t, got, gout, eb16,
        scratch=[
            ((512, HIDDEN), BF), ((WIDTH, HIDDEN), BF), ((rows_all, CHUNK), BF),
            ((rows_all, CHUNK), BF), ((WIDTH, HIDDEN), BF), ((WIDTH, HIDDEN), BF),
        ],
        limit=24, scalars=idx, time=18,
    )
    got_r = links.send(send_r, c=1)
    block_out, grad_mid, sums = call(
        mlp_end, [(wide, BF), (wide, F32), ((8, WIDTH), F32)], middle, acc_m, acc_g, gout, par,
        limit=16, far=(0,), time=3,
    )
    block_r = [((192, 2 * WIDTH), F32)] + [((192, 2 * WIDTH), BF)] * 3
    got_r, grad_mid = lax.optimization_barrier((got_r, grad_mid))
    own_r, *blocks_r = call(plane_sum, block_r, keep_r, got_r)
    grad_mid, *blocks_r = lax.optimization_barrier((grad_mid, *blocks_r))
    plane_r = links.to_plane(blocks_r)
    keep_q, send_q, g_all = call(
        attention_backward,
        [((800, WIDTH), BF), ((800, WIDTH), BF), ((canvases, 3 * WIDTH, slots), BF)],
        grad_mid, qt, kt, vv, pt, mt, xt, wout, ut, wnat, par, sums, eb_grad, down, across,
        scratch=[
            ((4, WIDTH, WIDTH), BF), ((400, 3 * WIDTH), F32), (square, F32),
            ((GROUPS, SLOT, slots), F32),
        ],
        limit=16, scalars=idx, time=20,
    )
    *plane_r, send_q = lax.optimization_barrier((*plane_r, send_q))
    got_q = links.send(send_q, c=1)
    block_q = [((192, WIDTH), F32)] + [((224, WIDTH), BF)] * 3 + [((32, WIDTH), F32)]
    own_q, *blocks_q, small = call(plane_sum, block_q, keep_q, got_q)
    plane_q = links.to_plane(blocks_q)
    plane_r = lax.optimization_barrier((*plane_r, *blocks_q))[:3]
    line_r = [((48, 2 * WIDTH), F32)] + [((48, 2 * WIDTH), BF)] * 3
    own_r, *blocks_r = call(line_sum, line_r, own_r, *plane_r)
    parts_r = links.to_line(blocks_r)
    g_all = lax.optimization_barrier((g_all, *blocks_r))[0]
    (grad_tokens,) = call(
        tokens_end, [(wide, F32)], tok, grad_mid, g_all, wnat, u, par, far=(0,), time=5,
    )
    *plane_q, grad_tokens = lax.optimization_barrier((*plane_q, grad_tokens))
    line_q = [((48, WIDTH), F32)] + [((80, WIDTH), BF)] * 3 + [((32, WIDTH), F32)]
    own_q, *blocks_q, small = call(line_sum, line_q, own_q, *plane_q, small)
    parts_q = links.to_line(blocks_q)
    parts_q, parts_r = [own_q, *parts_q], [own_r, *parts_r]
    rows = 48
    if links.outer > 1:
        small = small + sum(p[48:].astype(F32) for p in parts_q[1:])
        small = lax.psum(small, "dp", axis_index_groups=links.groups())
        parts_q = [links.outer_sum(sum(p[:48].astype(F32) for p in parts_q))]
        parts_r = [links.outer_sum(sum(p.astype(F32) for p in parts_r))]
        rows = parts_q[0].shape[0]

    mlp_state = [exp_w, exp_m, exp_s, con_w.T, con_m.T, con_s.T]
    third = call(
        functools.partial(step_mlp, len(parts_r)), [(a.shape, F32) for a in mlp_state],
        *parts_r, *(Far(a) for a in mlp_state), far=range(6), time=2,
    )
    state = [
        qkv_w, qkv_m, qkv_s, out_w.T, out_m.T, out_s.T, qv_b, qv_m, qv_s, exp_b, eb_m, eb_s,
        table_w.T, tab_m.T, tab_s.T, norm_p, norm_m, norm_s,
    ]
    fourth = call(
        functools.partial(step_attention, len(parts_q), rows), [(a.shape, F32) for a in state],
        *parts_q, small, *(Far(a) for a in state), scalars=idx, far=range(18), time=2,
    )
    return (
        block_out, grad_tokens, *fourth[0:3], *(a.T for a in fourth[3:6]), *third[0:3],
        *(a.T for a in third[3:6]), *fourth[6:12], *(a.T for a in fourth[12:15]), *fourth[15:],
    )


def solution(mesh):
    tokens = P(("dp", "head"), None)
    qkv, rows_head, rows_dp = P(None, "dp", "head"), P("head", "dp"), P("dp", "head")
    pair, unit, none = P(None, "head"), P("head"), P()
    matrices = (qkv, rows_head, rows_dp, rows_head)
    small = (pair, unit, pair, none)
    in_specs = (tokens, P("dp"), tokens, *matrices, *small)
    in_specs += tuple(s for spec in (*matrices, *small) for s in (spec, spec))
    out_specs = (tokens, tokens) + tuple(
        s for spec in (*matrices, *small) for s in (spec, spec, spec)
    )
    return jax.shard_map(
        functools.partial(per_device, Links(dict(mesh.shape))),
        mesh=mesh, in_specs=in_specs, out_specs=out_specs, check_vma=False,
    )
```

time: 218 us -> 127 us (0.58)
  Pallas kernels: 104 us -> 75.4 us
  waiting for transfers between devices: 35.5 us -> 13.6 us
  other arithmetic: 16.8 us -> 0.09 us
  starting transfers between devices: 46.4 us -> 36 us
  local copies, waits for them, and re-layouts: 8.17 us -> 0.72 us
  matrix products: 5.09 us -> 0 us
    pallas_call x3 -> x15, Pallas kernels: 104 us -> 75.4 us  [call(): pl.pallas_call(kernel, in_specs=[SMEM] * len(lead) + [VMEM] * len(args),...]
    ppermute x43 -> x37, waiting for transfers between devices: 35.5 us -> 13.6 us  [send(): return lax.ppermute(value, ('dp', 'head'), self.perm(**flips))]
    ppermute x43 -> x37, starting transfers between devices: 46.4 us -> 36 us  [send(): return lax.ppermute(value, ('dp', 'head'), self.perm(**flips))]
    sub x8 -> x0, other arithmetic: 8.47 us -> none  [adamw_step(): master - step_rate * (moment_hat / (jnp.sqrt(square_hat) + ADAM_EPS) + de...]
    dot_general x2 -> x0, matrix products: 5.09 us -> none  [the longest x1 2.59 us: per_device(): jnp.dot(table_part, pairs.reshape(table_rows, -1).astype(F32).T, precisio...]
    another operation x6 -> x0, other arithmetic: 3.4 us -> none
    unnamed x72 -> x5, local copies, waits for them, and re-layouts: 2.65 us -> 0.02 us
    transpose x3 -> x0, other arithmetic: 2.32 us -> none  [the longest x1 0.89 us: per_device(): second = jnp.concatenate([exp_w, con_w.T], axis=1).astype(BF)]
  transfers between devices with their start and end apart: 43 -> 37, of which waited for: 17 -> 6; matrix products, arithmetic and copies ran while one was open for 9% -> 1% of each run, Pallas kernels for 13% -> 42%
where the time goes in v2:
time: 127 us
  Pallas kernels  75.4 us (59%)
  starting transfers between devices  36 us (28%)
  waiting for transfers between devices  13.6 us (11%)
    pallas_call x15, Pallas kernels, call(): pl.pallas_call(kernel, in_specs=[SMEM] * len(lead) + [VMEM] * len(args),...  75.4 us
    ppermute x37, starting transfers between devices, send(): return lax.ppermute(value, ('dp', 'head'), self.perm(**flips))  36 us
    ppermute x37, waiting for transfers between devices, send(): return lax.ppermute(value, ('dp', 'head'), self.perm(**flips))  13.6 us
  transfers between devices with their start and end apart: 37, of which 6 were waited for; matrix products, arithmetic and copies ran while one was open for 1% of the time, Pallas kernels for 42%

profile of v2, /device:TPU:0, one launch (start us, length us, event | category | flops | bytes accessed | tf_op | source)
XLA Modules:
  0.0 126.9 jit_solution(7320683524030008712)
XLA Ops:
  0.7 1.0 pack_attention.1
  1.6 5.1 %collective-permute-start.2 = (bf16[48,384]{1,0:T(8,128)(2,1)S(1)}, bf16[48,384]{1,0:T(8,128)(2,1)S(1)}, u32[]{:S(2)}, u32[]{:S(2)}) collective-permute-start(bf16[48,384]{1,0:T(8,128)(2,1)S(1)} %pack_attention.1), channel_id=1, source_target_pairs={{0,24},{1,25},{2,26},{3,27},{4,28},{5,29},{6,30},{7,31},{8,16},{9,... | collective-permute-start | bytes 110600 | tf_op jit(solution)/shard_map/ppermute | solution.py:588
  6.8 0.0 collective-permute-start.1
  6.8 0.6 collective-permute-start
  7.4 1.0 pack_mlp.1
  8.4 0.4 collective-permute-start.8
  8.8 1.3 %collective-permute-start.7 = (bf16[16,384]{1,0:T(8,128)(2,1)S(1)}, bf16[16,384]{1,0:T(8,128)(2,1)S(1)}, u32[]{:S(2)}, u32[]{:S(2)}) collective-permute-start(bf16[16,384]{1,0:T(8,128)(2,1)S(1)} %get-tuple-element.155.own), channel_id=1, source_target_pairs={{0,2},{1,3},{2,0},{3,1},{4,6},{5,7},{6,4},{7,5},{8,10},{9,11},{10,... | collective-permute-start | bytes 36872 | tf_op jit(solution)/shard_map/ppermute | solution.py:588
  10.1 0.1 pad_add_fusion.idx
  10.2 0.7 reshape.55.crop
  10.9 0.2 collective-permute-start.6
  11.1 0.5 collective-permute-done.1
  11.6 2.5 %collective-permute-start.5 = (bf16[192,384]{1,0:T(8,128)(2,1)S(1)}, bf16[192,384]{1,0:T(8,128)(2,1)S(1)}, u32[]{:S(2)}, u32[]{:S(2)}) collective-permute-start(bf16[192,384]{1,0:T(8,128)(2,1)S(1)} %pad_maximum_fusion.p0), channel_id=1, source_target_pairs={{0,6},{1,7},{2,4},{3,5},{4,2},{5,3},{6,0},{7,1},{8,14},{9,15},{10,... | collective-permute-start | bytes 442376 | tf_op jit(solution)/shard_map/ppermute | solution.py:588
  14.1 0.5 collective-permute-start.4
  14.7 0.5 collective-permute-start.3
  15.2 0.0 collective-permute-done.7.by_x
  15.2 0.0 collective-permute-done.6.by_c
  15.2 4.7 %prepare.1 = (bf16[8,256,512]{2,1,0:T(8,128)(2,1)S(1)}, bf16[8,400,256]{2,1,0:T(8,128)(2,1)S(1)}, bf16[4,256,208]{2,1,0:T(8,128)(2,1)S(1)}, bf16[4,208,256]{2,1,...) custom-call(s32[4]{0:T(128)S(1)} %pad_add_fusion.idx, ...), custom_call_target="tpu_custom_call" | custom-call | flops 5750000128 | tf_op jit(solution)/shard_map/prepare/pallas_call | solution.py:638
  19.9 3.3 %collective-permute-start.11 = (bf16[48,768]{1,0:T(8,128)(2,1)S(1)}, bf16[48,768]{1,0:T(8,128)(2,1)S(1)}, u32[]{:S(2)}, u32[]{:S(2)}) collective-permute-start(bf16[48,768]{1,0:T(8,128)(2,1)S(1)} %get-tuple-element.173), channel_id=1, source_target_pairs={{0,24},{1,25},{2,26},{3,27},{4,28},{5,29},{6,30},{7,31},{8,16},{9,... | collective-permute-start | bytes 221192 | tf_op jit(solution)/shard_map/ppermute | solution.py:588
  23.1 0.0 collective-permute-start.9
  23.2 4.3 %collective-permute-done.9 = bf16[48,768]{1,0:T(8,128)(2,1)S(1)} collective-permute-done((bf16[48,768]{1,0:T(8,128)(2,1)S(1)}, bf16[48,768]{1,0:T(8,128)(2,1)S(1)}, u32[]{:S(2)}, u32[]{:S(2)}) %collective-permute-start.9) | collective-permute-done | bytes 73760 | tf_op jit(solution)/shard_map/ppermute | solution.py:588
  27.5 0.0 collective-permute-start.10
  27.5 0.0 collective-permute-done.5.p3
  27.5 0.0 collective-permute-done.4.p2
  27.5 0.1 collective-permute-start.12
  27.6 0.5 collective-permute-start.13
  28.1 0.1 collective-permute-start.14
  28.2 5.3 %collective-permute-done.10 = bf16[48,768]{1,0:T(8,128)(2,1)S(1)} collective-permute-done((bf16[48,768]{1,0:T(8,128)(2,1)S(1)}, bf16[48,768]{1,0:T(8,128)(2,1)S(1)}, u32[]{:S(2)}, u32[]{:S(2)}) %collective-permute-start.10) | collective-permute-done | bytes 73760 | tf_op jit(solution)/shard_map/ppermute | solution.py:588
  33.5 0.0 collective-permute-start.15
  33.6 2.5 %collective-permute-start.18 = (bf16[192,768]{1,0:T(8,128)(2,1)S(1)}, bf16[192,768]{1,0:T(8,128)(2,1)S(1)}, u32[]{:S(2)}, u32[]{:S(2)}) collective-permute-start(bf16[192,768]{1,0:T(8,128)(2,1)S(1)} %constant_dynamic-update-slice_fusion.p0), channel_id=1, source_target_pairs={{0,6},{1,7},{2,4},{3,5},{4,2},{5,3},{6,0},{7,1},{8,14},{9,15},{10,... | collective-permute-start | bytes 884744 | tf_op jit(solution)/shard_map/ppermute | solution.py:588
  36.1 0.5 collective-permute-start.17
  36.6 0.5 collective-permute-start.16
  37.1 14.1 %attention_forward.1 = (bf16[1568,384]{1,0:T(8,128)(2,1)S(1)}, bf16[8,384,256]{2,1,0:T(8,128)(2,1)S(1)}, bf16[8,384,256]{2,1,0:T(8,128)(2,1)S(1)}, bf16[8,256,38...) custom-call(s32[4]{0:T(128)S(1)} %pad_add_fusion.idx, ...), custom_call_target="tpu_custom_call" | custom-call | flops 16099999744 | tf_op jit(solution)/shard_map/attention_forward/pallas_call | solution.py:638
  51.3 0.1 collective-permute-start.19
  51.3 0.5 collective-permute-start.20
  51.8 0.1 collective-permute-start.21
  51.9 0.4 collective-permute-start.22
  52.4 2.3 %mlp_begin.1 = (f32[1568,384]{1,0:T(8,128)S(1)}, bf16[1568,512]{1,0:T(8,128)(2,1)S(1)}, bf16[400,1568]{1,0:T(8,128)(2,1)S(1)}) custom-call(bf16[1568,384]{1,0:T(8,128)(2,1)S(1)} %get-tuple-element.184.mrg, bf16[1568,384]{1,0:T(8,128)(2,1)S(1)} %get-tuple-element.185.tok, bf16[384,384]{1,0:T(8,128)(2,1)S(1)} %get-tuple-element.186.outt, ...), custom_call_target="tpu_custom_call" | custom-call | flops 3449999872 | tf_op jit(solution)/shard_map/mlp_begin/pallas_call | solution.py:638
  54.8 18.4 %mlp.1 = (f32[1568,384]{1,0:T(8,128)S(1)}, f32[1568,384]{1,0:T(8,128)S(1)}, bf16[768,768]{1,0:T(8,128)(2,1)S(1)}, bf16[768,768]{1,0:T(8,128)(2,1)S(1)}, f32[8,1536]{1,0:T(8,128)S(1)}) custom-call(s32[4]{0:T(128)S(1)} %pad_add_fusion.idx, bf16[192,768]{1,0:T(8,128)(2,1)S(1)} %constant_dynamic-update-slice_fusion.p0, ...), custom_call_target="tpu_custom_call" | custom-call | flops 20700000256 | tf_op jit(solution)/shard_map/mlp/pallas_call | solution.py:638
  73.1 0.1 collective-permute-start.23
  73.2 3.1 %mlp_end.1 = (bf16[1568,384]{1,0:T(8,128)(2,1)}, f32[1568,384]{1,0:T(8,128)S(1)}, f32[8,384]{1,0:T(8,128)S(1)}) custom-call(f32[1568,384]{1,0:T(8,128)S(1)} %get-tuple-element.188.mid, f32[1568,384]{1,0:T(8,128)S(1)} %get-tuple-element.198.acc_m, f32[1568,384]{1,0:T(8,128)S(1)} %get-tuple-element.199.acc_g, bf16[1568,384]{1,0:T(8,128)(2,1)S(1)} %get-tuple-element.196.gout, ...), custom_call_target="tpu_custom_call" | custom-call | flops 3449999872 | tf_op jit(solution)/shard_map/mlp_end/pallas_call | solution.py:638
  76.3 0.3 plane_sum.2
  76.6 1.6 %collective-permute-start.24 = (bf16[192,768]{1,0:T(8,128)(2,1)S(1)}, bf16[192,768]{1,0:T(8,128)(2,1)S(1)}, u32[]{:S(2)}, u32[]{:S(2)}) collective-permute-start(bf16[192,768]{1,0:T(8,128)(2,1)S(1)} %get-tuple-element.224), channel_id=1, source_target_pairs={{0,2},{1,3},{2,0},{3,1},{4,6},{5,7},{6,4},{7,5},{8,10},{9,11},{10,... | collective-permute-start | bytes 884744 | tf_op jit(solution)/shard_map/ppermute | solution.py:588
  78.1 1.5 %collective-permute-start.25 = (bf16[192,768]{1,0:T(8,128)(2,1)S(1)}, bf16[192,768]{1,0:T(8,128)(2,1)S(1)}, u32[]{:S(2)}, u32[]{:S(2)}) collective-permute-start(bf16[192,768]{1,0:T(8,128)(2,1)S(1)} %get-tuple-element.225), channel_id=1, source_target_pairs={{0,4},{1,5},{2,6},{3,7},{4,0},{5,1},{6,2},{7,3},{8,12},{9,13},{10,... | collective-permute-start | bytes 884744 | tf_op jit(solution)/shard_map/ppermute | solution.py:588
  79.7 0.5 collective-permute-start.26
  80.1 19.9 %attention_backward.1 = (bf16[800,384]{1,0:T(8,128)(2,1)S(1)}, bf16[800,384]{1,0:T(8,128)(2,1)S(1)}, bf16[8,1152,256]{2,1,0:T(8,128)(2,1)S(1)}) custom-call(s32[4]{0:T(128)S(1)} %pad_add_fusion.idx, f32[1568,384]{1,0:T(8,128)S(1)} %get-tuple-element.209.gmid, bf16[8,384,256]{2,1,0:T(8,128)(2,1)S(1)} %get-tuple-element.210.qt, ...), custom_call_target="tpu_custom_call" | custom-call | flops 23000000512 | tf_op jit(solution)/shard_map/attention_backward/pallas_call | solution.py:638
  100.1 0.1 collective-permute-start.27
  100.2 2.0 %collective-permute-done.27.got = bf16[800,384]{1,0:T(8,128)(2,1)S(1)} collective-permute-done((bf16[800,384]{1,0:T(8,128)(2,1)S(1)}, bf16[800,384]{1,0:T(8,128)(2,1)S(1)}, u32[]{:S(2)}, u32[]{:S(2)}) %collective-permute-start.27) | collective-permute-done | bytes 614432 | tf_op jit(solution)/shard_map/ppermute | solution.py:588
  102.2 0.2 plane_sum.3
  102.4 1.6 %collective-permute-start.28 = (bf16[224,384]{1,0:T(8,128)(2,1)S(1)}, bf16[224,384]{1,0:T(8,128)(2,1)S(1)}, u32[]{:S(2)}, u32[]{:S(2)}) collective-permute-start(bf16[224,384]{1,0:T(8,128)(2,1)S(1)} %get-tuple-element.229), channel_id=1, source_target_pairs={{0,2},{1,3},{2,0},{3,1},{4,6},{5,7},{6,4},{7,5},{8,10},{9,11},{10,... | collective-permute-start | bytes 516104 | tf_op jit(solution)/shard_map/ppermute | solution.py:588
  103.9 1.5 %collective-permute-start.29 = (bf16[224,384]{1,0:T(8,128)(2,1)S(1)}, bf16[224,384]{1,0:T(8,128)(2,1)S(1)}, u32[]{:S(2)}, u32[]{:S(2)}) collective-permute-start(bf16[224,384]{1,0:T(8,128)(2,1)S(1)} %get-tuple-element.230), channel_id=1, source_target_pairs={{0,4},{1,5},{2,6},{3,7},{4,0},{5,1},{6,2},{7,3},{8,12},{9,13},{10,... | collective-permute-start | bytes 516104 | tf_op jit(solution)/shard_map/ppermute | solution.py:588
  105.5 0.5 collective-permute-start.30
  105.9 0.1 line_sum.2
  106.1 0.2 collective-permute-start.34
  106.2 1.4 %collective-permute-start.35 = (bf16[48,768]{1,0:T(8,128)(2,1)S(1)}, bf16[48,768]{1,0:T(8,128)(2,1)S(1)}, u32[]{:S(2)}, u32[]{:S(2)}) collective-permute-start(bf16[48,768]{1,0:T(8,128)(2,1)S(1)} %get-tuple-element.241), channel_id=1, source_target_pairs={{0,16},{1,17},{2,18},{3,19},{4,20},{5,21},{6,22},{7,23},{8,24},{9,... | collective-permute-start | bytes 221192 | tf_op jit(solution)/shard_map/ppermute | solution.py:588
  107.6 6.5 %tokens_end.1 = f32[1568,384]{1,0:T(8,128)} custom-call(bf16[1568,384]{1,0:T(8,128)(2,1)S(1)} %get-tuple-element.185.tok, f32[1568,384]{1,0:T(8,128)S(1)} %get-tuple-element.209.gmid, bf16[8,1152,256]{2,1,0:T(8,128)(2,1)S(1)} %get-tuple-element.243.gta, bf16[384,1152]{1,0:T(8,128)(2,1)S(1)} %get-tuple-element.218.wnat, ...), custom_call_target="tpu_custom_call" | custom-call | flops 5750000128 | tf_op jit(solution)/shard_map/tokens_end/pallas_call | solution.py:638
  114.1 2.9 %collective-permute-start.36 = (bf16[48,768]{1,0:T(8,128)(2,1)S(1)}, bf16[48,768]{1,0:T(8,128)(2,1)S(1)}, u32[]{:S(2)}, u32[]{:S(2)}) collective-permute-start(bf16[48,768]{1,0:T(8,128)(2,1)S(1)} %get-tuple-element.242), channel_id=1, source_target_pairs={{0,24},{1,25},{2,26},{3,27},{4,28},{5,29},{6,30},{7,31},{8,16},{9,... | collective-permute-start | bytes 221192 | tf_op jit(solution)/shard_map/ppermute | solution.py:588
  117.0 0.1 line_sum.3
  117.1 0.1 collective-permute-start.31
  117.2 1.5 %collective-permute-start.32 = (bf16[80,384]{1,0:T(8,128)(2,1)S(1)}, bf16[80,384]{1,0:T(8,128)(2,1)S(1)}, u32[]{:S(2)}, u32[]{:S(2)}) collective-permute-start(bf16[80,384]{1,0:T(8,128)(2,1)S(1)} %get-tuple-element.252), channel_id=1, source_target_pairs={{0,16},{1,17},{2,18},{3,19},{4,20},{5,21},{6,22},{7,23},{8,24},{9,... | collective-permute-start | bytes 184328 | tf_op jit(solution)/shard_map/ppermute | solution.py:588
  118.7 2.9 %collective-permute-start.33 = (bf16[80,384]{1,0:T(8,128)(2,1)S(1)}, bf16[80,384]{1,0:T(8,128)(2,1)S(1)}, u32[]{:S(2)}, u32[]{:S(2)}) collective-permute-start(bf16[80,384]{1,0:T(8,128)(2,1)S(1)} %get-tuple-element.253), channel_id=1, source_target_pairs={{0,24},{1,25},{2,26},{3,27},{4,28},{5,29},{6,30},{7,31},{8,16},{9,... | collective-permute-start | bytes 184328 | tf_op jit(solution)/shard_map/ppermute | solution.py:588
  121.6 1.9 %step_mlp.1 = (f32[48,384]{1,0:T(8,128)}, f32[48,384]{1,0:T(8,128)}, f32[48,384]{1,0:T(8,128)}, f32[48,384]{1,0:T(8,128)}, f32[48,384]{1,0:T(8,128)}, /*index=5*/f32[48,384]{1,0:T(8,128)}) custom-call(f32[48,768]{1,0:T(8,128)S(1)} %get-tuple-element.261.refs_0_, bf16[48,768]{1,0:T(8,128)(2,1)S(1)} %collective-permute-done.34.refs_1_, ...), custom_call_target="tpu_custom_call" | custom-call | flops 2300000000 | tf_op jit(solution)/shard_map/step_mlp/pallas_call | solution.py:638
  123.5 0.5 collective-permute-done.32.refs_2_
  124.0 0.8 collective-permute-done.33.refs_3_
  124.8 2.0 %step_attention.1 = (f32[3,48,96]{2,1,0:T(8,128)}, f32[3,48,96]{2,1,0:T(8,128)}, f32[3,48,96]{2,1,0:T(8,128)}, f32[48,96]{1,0:T(8,128)}, f32[48,96]{1,0:T(8,128)...) custom-call(s32[4]{0:T(128)S(1)} %pad_add_fusion.idx, ...), custom_call_target="tpu_custom_call" | custom-call | flops 2300000000 | tf_op jit(solution)/shard_map/step_attention/pallas_call | solution.py:638
  (34 shorter events, 0.1 us)
Async XLA Ops:
  1.6 9.3 %collective-permute-start.2 = (bf16[48,384]{1,0:T(8,128)(2,1)S(1)}, bf16[48,384]{1,0:T(8,128)(2,1)S(1)}, u32[]{:S(2)}, u32[]{:S(2)}) collective-permute-start(bf16[48,384]{1,0:T(8,128)(2,1)S(1)} %pack_attention.1), channel_id=1, source_target_pairs={{0,24},{1,25},{2,26},{3,27},{4,28},{5,29},{6,30},{7,31},{8,16},{9,... | collective-permute-start | bytes 110600 | tf_op jit(solution)/shard_map/ppermute | solution.py:588
  6.8 4.9 %collective-permute-start.1 = (bf16[48,384]{1,0:T(8,128)(2,1)S(1)}, bf16[48,384]{1,0:T(8,128)(2,1)S(1)}, u32[]{:S(2)}, u32[]{:S(2)}) collective-permute-start(bf16[48,384]{1,0:T(8,128)(2,1)S(1)} %pack_attention.1), channel_id=1, source_target_pairs={{0,16},{1,17},{2,18},{3,19},{4,20},{5,21},{6,22},{7,23},{8,24},{9,... | collective-permute-start | bytes 110600 | tf_op jit(solution)/shard_map/ppermute | solution.py:588
  6.8 4.9 %collective-permute-start = (bf16[48,384]{1,0:T(8,128)(2,1)S(1)}, bf16[48,384]{1,0:T(8,128)(2,1)S(1)}, u32[]{:S(2)}, u32[]{:S(2)}) collective-permute-start(bf16[48,384]{1,0:T(8,128)(2,1)S(1)} %pack_attention.1), channel_id=1, source_target_pairs={{0,8},{1,9},{2,10},{3,11},{4,12},{5,13},{6,14},{7,15},{8,0},{9,1},... | collective-permute-start | bytes 110600 | tf_op jit(solution)/shard_map/ppermute | solution.py:588
  7.4 2.8 %copy-start = (s32[6272]{0:T(1024)S(1)}, s32[6272]{0:T(1024)}, u32[]{:S(2)}) copy-start(s32[6272]{0:T(1024)} %param.30) | copy-start | bytes 75268
  8.4 6.3 %collective-permute-start.8 = (bf16[16,384]{1,0:T(8,128)(2,1)S(1)}, bf16[16,384]{1,0:T(8,128)(2,1)S(1)}, u32[]{:S(2)}, u32[]{:S(2)}) collective-permute-start(bf16[16,384]{1,0:T(8,128)(2,1)S(1)} %get-tuple-element.155.own), channel_id=1, source_target_pairs={{0,3},{1,2},{2,1},{3,0},{4,7},{5,6},{6,5},{7,4},{8,11},{9,10},{10,... | collective-permute-start | bytes 36872 | tf_op jit(solution)/shard_map/ppermute | solution.py:588
  8.8 6.4 %collective-permute-start.7 = (bf16[16,384]{1,0:T(8,128)(2,1)S(1)}, bf16[16,384]{1,0:T(8,128)(2,1)S(1)}, u32[]{:S(2)}, u32[]{:S(2)}) collective-permute-start(bf16[16,384]{1,0:T(8,128)(2,1)S(1)} %get-tuple-element.155.own), channel_id=1, source_target_pairs={{0,2},{1,3},{2,0},{3,1},{4,6},{5,7},{6,4},{7,5},{8,10},{9,11},{10,... | collective-permute-start | bytes 36872 | tf_op jit(solution)/shard_map/ppermute | solution.py:588
  10.9 4.3 %collective-permute-start.6 = (bf16[16,384]{1,0:T(8,128)(2,1)S(1)}, bf16[16,384]{1,0:T(8,128)(2,1)S(1)}, u32[]{:S(2)}, u32[]{:S(2)}) collective-permute-start(bf16[16,384]{1,0:T(8,128)(2,1)S(1)} %get-tuple-element.155.own), channel_id=1, source_target_pairs={{0,1},{1,0},{2,3},{3,2},{4,5},{5,4},{6,7},{7,6},{8,9},{9,8},{10,11... | collective-permute-start | bytes 36872 | tf_op jit(solution)/shard_map/ppermute | solution.py:588
  11.6 15.9 %collective-permute-start.5 = (bf16[192,384]{1,0:T(8,128)(2,1)S(1)}, bf16[192,384]{1,0:T(8,128)(2,1)S(1)}, u32[]{:S(2)}, u32[]{:S(2)}) collective-permute-start(bf16[192,384]{1,0:T(8,128)(2,1)S(1)} %pad_maximum_fusion.p0), channel_id=1, source_target_pairs={{0,6},{1,7},{2,4},{3,5},{4,2},{5,3},{6,0},{7,1},{8,14},{9,15},{10,... | collective-permute-start | bytes 442376 | tf_op jit(solution)/shard_map/ppermute | solution.py:588
  14.1 13.4 %collective-permute-start.4 = (bf16[192,384]{1,0:T(8,128)(2,1)S(1)}, bf16[192,384]{1,0:T(8,128)(2,1)S(1)}, u32[]{:S(2)}, u32[]{:S(2)}) collective-permute-start(bf16[192,384]{1,0:T(8,128)(2,1)S(1)} %pad_maximum_fusion.p0), channel_id=1, source_target_pairs={{0,4},{1,5},{2,6},{3,7},{4,0},{5,1},{6,2},{7,3},{8,12},{9,13},{10,... | collective-permute-start | bytes 442376 | tf_op jit(solution)/shard_map/ppermute | solution.py:588
  14.7 12.9 %collective-permute-start.3 = (bf16[192,384]{1,0:T(8,128)(2,1)S(1)}, bf16[192,384]{1,0:T(8,128)(2,1)S(1)}, u32[]{:S(2)}, u32[]{:S(2)}) collective-permute-start(bf16[192,384]{1,0:T(8,128)(2,1)S(1)} %pad_maximum_fusion.p0), channel_id=1, source_target_pairs={{0,2},{1,3},{2,0},{3,1},{4,6},{5,7},{6,4},{7,5},{8,10},{9,11},{10,... | collective-permute-start | bytes 442376 | tf_op jit(solution)/shard_map/ppermute | solution.py:588
  19.9 13.7 %collective-permute-start.11 = (bf16[48,768]{1,0:T(8,128)(2,1)S(1)}, bf16[48,768]{1,0:T(8,128)(2,1)S(1)}, u32[]{:S(2)}, u32[]{:S(2)}) collective-permute-start(bf16[48,768]{1,0:T(8,128)(2,1)S(1)} %get-tuple-element.173), channel_id=1, source_target_pairs={{0,24},{1,25},{2,26},{3,27},{4,28},{5,29},{6,30},{7,31},{8,16},{9,... | collective-permute-start | bytes 221192 | tf_op jit(solution)/shard_map/ppermute | solution.py:588
  23.1 4.4 %collective-permute-start.9 = (bf16[48,768]{1,0:T(8,128)(2,1)S(1)}, bf16[48,768]{1,0:T(8,128)(2,1)S(1)}, u32[]{:S(2)}, u32[]{:S(2)}) collective-permute-start(bf16[48,768]{1,0:T(8,128)(2,1)S(1)} %get-tuple-element.173), channel_id=1, source_target_pairs={{0,8},{1,9},{2,10},{3,11},{4,12},{5,13},{6,14},{7,15},{8,0},{9,1},... | collective-permute-start | bytes 221192 | tf_op jit(solution)/shard_map/ppermute | solution.py:588
  27.5 6.0 %collective-permute-start.10 = (bf16[48,768]{1,0:T(8,128)(2,1)S(1)}, bf16[48,768]{1,0:T(8,128)(2,1)S(1)}, u32[]{:S(2)}, u32[]{:S(2)}) collective-permute-start(bf16[48,768]{1,0:T(8,128)(2,1)S(1)} %get-tuple-element.173), channel_id=1, source_target_pairs={{0,16},{1,17},{2,18},{3,19},{4,20},{5,21},{6,22},{7,23},{8,24},{9,... | collective-permute-start | bytes 221192 | tf_op jit(solution)/shard_map/ppermute | solution.py:588
  27.5 8.6 %collective-permute-start.12 = (bf16[192,384]{1,0:T(8,128)(2,1)S(1)}, bf16[192,384]{1,0:T(8,128)(2,1)S(1)}, u32[]{:S(2)}, u32[]{:S(2)}) collective-permute-start(bf16[192,384]{1,0:T(8,128)(2,1)S(1)} %pad_maximum_fusion.p0), channel_id=1, source_target_pairs={{0,1},{1,0},{2,3},{3,2},{4,5},{5,4},{6,7},{7,6},{8,9},{9,8},{10,11... | collective-permute-start | bytes 442376 | tf_op jit(solution)/shard_map/ppermute | solution.py:588
  27.6 9.0 %collective-permute-start.13 = (bf16[192,384]{1,0:T(8,128)(2,1)S(1)}, bf16[192,384]{1,0:T(8,128)(2,1)S(1)}, u32[]{:S(2)}, u32[]{:S(2)}) collective-permute-start(bf16[192,384]{1,0:T(8,128)(2,1)S(1)} %collective-permute-done.3.p1), channel_id=1, source_target_pairs={{0,1},{1,0},{2,3},{3,2},{4,5},{5,4},{6,7},{7,6},{8,9},{9,8},{10,11... | collective-permute-start | bytes 442376 | tf_op jit(solution)/shard_map/ppermute | solution.py:588
  28.1 9.0 %collective-permute-start.14 = (bf16[192,384]{1,0:T(8,128)(2,1)S(1)}, bf16[192,384]{1,0:T(8,128)(2,1)S(1)}, u32[]{:S(2)}, u32[]{:S(2)}) collective-permute-start(bf16[192,384]{1,0:T(8,128)(2,1)S(1)} %collective-permute-done.4.p2), channel_id=1, source_target_pairs={{0,1},{1,0},{2,3},{3,2},{4,5},{5,4},{6,7},{7,6},{8,9},{9,8},{10,11... | collective-permute-start | bytes 442376 | tf_op jit(solution)/shard_map/ppermute | solution.py:588
  33.5 3.6 %collective-permute-start.15 = (bf16[192,384]{1,0:T(8,128)(2,1)S(1)}, bf16[192,384]{1,0:T(8,128)(2,1)S(1)}, u32[]{:S(2)}, u32[]{:S(2)}) collective-permute-start(bf16[192,384]{1,0:T(8,128)(2,1)S(1)} %collective-permute-done.5.p3), channel_id=1, source_target_pairs={{0,1},{1,0},{2,3},{3,2},{4,5},{5,4},{6,7},{7,6},{8,9},{9,8},{10,11... | collective-permute-start | bytes 442376 | tf_op jit(solution)/shard_map/ppermute | solution.py:588
  33.6 17.7 %collective-permute-start.18 = (bf16[192,768]{1,0:T(8,128)(2,1)S(1)}, bf16[192,768]{1,0:T(8,128)(2,1)S(1)}, u32[]{:S(2)}, u32[]{:S(2)}) collective-permute-start(bf16[192,768]{1,0:T(8,128)(2,1)S(1)} %constant_dynamic-update-slice_fusion.p0), channel_id=1, source_target_pairs={{0,6},{1,7},{2,4},{3,5},{4,2},{5,3},{6,0},{7,1},{8,14},{9,15},{10,... | collective-permute-start | bytes 884744 | tf_op jit(solution)/shard_map/ppermute | solution.py:588
  36.1 15.2 %collective-permute-start.17 = (bf16[192,768]{1,0:T(8,128)(2,1)S(1)}, bf16[192,768]{1,0:T(8,128)(2,1)S(1)}, u32[]{:S(2)}, u32[]{:S(2)}) collective-permute-start(bf16[192,768]{1,0:T(8,128)(2,1)S(1)} %constant_dynamic-update-slice_fusion.p0), channel_id=1, source_target_pairs={{0,4},{1,5},{2,6},{3,7},{4,0},{5,1},{6,2},{7,3},{8,12},{9,13},{10,... | collective-permute-start | bytes 884744 | tf_op jit(solution)/shard_map/ppermute | solution.py:588
  36.6 14.7 %collective-permute-start.16 = (bf16[192,768]{1,0:T(8,128)(2,1)S(1)}, bf16[192,768]{1,0:T(8,128)(2,1)S(1)}, u32[]{:S(2)}, u32[]{:S(2)}) collective-permute-start(bf16[192,768]{1,0:T(8,128)(2,1)S(1)} %constant_dynamic-update-slice_fusion.p0), channel_id=1, source_target_pairs={{0,2},{1,3},{2,0},{3,1},{4,6},{5,7},{6,4},{7,5},{8,10},{9,11},{10,... | collective-permute-start | bytes 884744 | tf_op jit(solution)/shard_map/ppermute | solution.py:588
  51.3 3.4 %collective-permute-start.19 = (bf16[192,768]{1,0:T(8,128)(2,1)S(1)}, bf16[192,768]{1,0:T(8,128)(2,1)S(1)}, u32[]{:S(2)}, u32[]{:S(2)}) collective-permute-start(bf16[192,768]{1,0:T(8,128)(2,1)S(1)} %constant_dynamic-update-slice_fusion.p0), channel_id=1, source_target_pairs={{0,1},{1,0},{2,3},{3,2},{4,5},{5,4},{6,7},{7,6},{8,9},{9,8},{10,11... | collective-permute-start | bytes 884744 | tf_op jit(solution)/shard_map/ppermute | solution.py:588
  51.3 3.4 %collective-permute-start.20 = (bf16[192,768]{1,0:T(8,128)(2,1)S(1)}, bf16[192,768]{1,0:T(8,128)(2,1)S(1)}, u32[]{:S(2)}, u32[]{:S(2)}) collective-permute-start(bf16[192,768]{1,0:T(8,128)(2,1)S(1)} %collective-permute-done.16.p1), channel_id=1, source_target_pairs={{0,1},{1,0},{2,3},{3,2},{4,5},{5,4},{6,7},{7,6},{8,9},{9,8},{10,11... | collective-permute-start | bytes 884744 | tf_op jit(solution)/shard_map/ppermute | solution.py:588
  51.8 2.9 %collective-permute-start.21 = (bf16[192,768]{1,0:T(8,128)(2,1)S(1)}, bf16[192,768]{1,0:T(8,128)(2,1)S(1)}, u32[]{:S(2)}, u32[]{:S(2)}) collective-permute-start(bf16[192,768]{1,0:T(8,128)(2,1)S(1)} %collective-permute-done.17.p2), channel_id=1, source_target_pairs={{0,1},{1,0},{2,3},{3,2},{4,5},{5,4},{6,7},{7,6},{8,9},{9,8},{10,11... | collective-permute-start | bytes 884744 | tf_op jit(solution)/shard_map/ppermute | solution.py:588
  51.9 2.8 %collective-permute-start.22 = (bf16[192,768]{1,0:T(8,128)(2,1)S(1)}, bf16[192,768]{1,0:T(8,128)(2,1)S(1)}, u32[]{:S(2)}, u32[]{:S(2)}) collective-permute-start(bf16[192,768]{1,0:T(8,128)(2,1)S(1)} %collective-permute-done.18.p3), channel_id=1, source_target_pairs={{0,1},{1,0},{2,3},{3,2},{4,5},{5,4},{6,7},{7,6},{8,9},{9,8},{10,11... | collective-permute-start | bytes 884744 | tf_op jit(solution)/shard_map/ppermute | solution.py:588
  73.1 3.2 %collective-permute-start.23 = (bf16[768,768]{1,0:T(8,128)(2,1)S(1)}, bf16[768,768]{1,0:T(8,128)(2,1)S(1)}, u32[]{:S(2)}, u32[]{:S(2)}) collective-permute-start(bf16[768,768]{1,0:T(8,128)(2,1)S(1)} %get-tuple-element.201), channel_id=1, source_target_pairs={{0,1},{1,0},{2,3},{3,2},{4,5},{5,4},{6,7},{7,6},{8,9},{9,8},{10,11... | collective-permute-start | bytes 3538952 | tf_op jit(solution)/shard_map/ppermute | solution.py:588
  76.6 23.5 %collective-permute-start.24 = (bf16[192,768]{1,0:T(8,128)(2,1)S(1)}, bf16[192,768]{1,0:T(8,128)(2,1)S(1)}, u32[]{:S(2)}, u32[]{:S(2)}) collective-permute-start(bf16[192,768]{1,0:T(8,128)(2,1)S(1)} %get-tuple-element.224), channel_id=1, source_target_pairs={{0,2},{1,3},{2,0},{3,1},{4,6},{5,7},{6,4},{7,5},{8,10},{9,11},{10,... | collective-permute-start | bytes 884744 | tf_op jit(solution)/shard_map/ppermute | solution.py:588
  78.1 21.9 %collective-permute-start.25 = (bf16[192,768]{1,0:T(8,128)(2,1)S(1)}, bf16[192,768]{1,0:T(8,128)(2,1)S(1)}, u32[]{:S(2)}, u32[]{:S(2)}) collective-permute-start(bf16[192,768]{1,0:T(8,128)(2,1)S(1)} %get-tuple-element.225), channel_id=1, source_target_pairs={{0,4},{1,5},{2,6},{3,7},{4,0},{5,1},{6,2},{7,3},{8,12},{9,13},{10,... | collective-permute-start | bytes 884744 | tf_op jit(solution)/shard_map/ppermute | solution.py:588
  79.7 20.4 %collective-permute-start.26 = (bf16[192,768]{1,0:T(8,128)(2,1)S(1)}, bf16[192,768]{1,0:T(8,128)(2,1)S(1)}, u32[]{:S(2)}, u32[]{:S(2)}) collective-permute-start(bf16[192,768]{1,0:T(8,128)(2,1)S(1)} %get-tuple-element.226), channel_id=1, source_target_pairs={{0,6},{1,7},{2,4},{3,5},{4,2},{5,3},{6,0},{7,1},{8,14},{9,15},{10,... | collective-permute-start | bytes 884744 | tf_op jit(solution)/shard_map/ppermute | solution.py:588
  100.1 2.1 %collective-permute-start.27 = (bf16[800,384]{1,0:T(8,128)(2,1)S(1)}, bf16[800,384]{1,0:T(8,128)(2,1)S(1)}, u32[]{:S(2)}, u32[]{:S(2)}) collective-permute-start(bf16[800,384]{1,0:T(8,128)(2,1)S(1)} %get-tuple-element.228), channel_id=1, source_target_pairs={{0,1},{1,0},{2,3},{3,2},{4,5},{5,4},{6,7},{7,6},{8,9},{9,8},{10,11... | collective-permute-start | bytes 1843208 | tf_op jit(solution)/shard_map/ppermute | solution.py:588
  102.4 11.7 %collective-permute-start.28 = (bf16[224,384]{1,0:T(8,128)(2,1)S(1)}, bf16[224,384]{1,0:T(8,128)(2,1)S(1)}, u32[]{:S(2)}, u32[]{:S(2)}) collective-permute-start(bf16[224,384]{1,0:T(8,128)(2,1)S(1)} %get-tuple-element.229), channel_id=1, source_target_pairs={{0,2},{1,3},{2,0},{3,1},{4,6},{5,7},{6,4},{7,5},{8,10},{9,11},{10,... | collective-permute-start | bytes 516104 | tf_op jit(solution)/shard_map/ppermute | solution.py:588
  103.9 13.1 %collective-permute-start.29 = (bf16[224,384]{1,0:T(8,128)(2,1)S(1)}, bf16[224,384]{1,0:T(8,128)(2,1)S(1)}, u32[]{:S(2)}, u32[]{:S(2)}) collective-permute-start(bf16[224,384]{1,0:T(8,128)(2,1)S(1)} %get-tuple-element.230), channel_id=1, source_target_pairs={{0,4},{1,5},{2,6},{3,7},{4,0},{5,1},{6,2},{7,3},{8,12},{9,13},{10,... | collective-permute-start | bytes 516104 | tf_op jit(solution)/shard_map/ppermute | solution.py:588
  105.5 11.6 %collective-permute-start.30 = (bf16[224,384]{1,0:T(8,128)(2,1)S(1)}, bf16[224,384]{1,0:T(8,128)(2,1)S(1)}, u32[]{:S(2)}, u32[]{:S(2)}) collective-permute-start(bf16[224,384]{1,0:T(8,128)(2,1)S(1)} %get-tuple-element.231), channel_id=1, source_target_pairs={{0,6},{1,7},{2,4},{3,5},{4,2},{5,3},{6,0},{7,1},{8,14},{9,15},{10,... | collective-permute-start | bytes 516104 | tf_op jit(solution)/shard_map/ppermute | solution.py:588
  106.1 12.6 %collective-permute-start.34 = (bf16[48,768]{1,0:T(8,128)(2,1)S(1)}, bf16[48,768]{1,0:T(8,128)(2,1)S(1)}, u32[]{:S(2)}, u32[]{:S(2)}) collective-permute-start(bf16[48,768]{1,0:T(8,128)(2,1)S(1)} %get-tuple-element.240), channel_id=1, source_target_pairs={{0,8},{1,9},{2,10},{3,11},{4,12},{5,13},{6,14},{7,15},{8,0},{9,1},... | collective-permute-start | bytes 221192 | tf_op jit(solution)/shard_map/ppermute | solution.py:588
  106.2 15.4 %collective-permute-start.35 = (bf16[48,768]{1,0:T(8,128)(2,1)S(1)}, bf16[48,768]{1,0:T(8,128)(2,1)S(1)}, u32[]{:S(2)}, u32[]{:S(2)}) collective-permute-start(bf16[48,768]{1,0:T(8,128)(2,1)S(1)} %get-tuple-element.241), channel_id=1, source_target_pairs={{0,16},{1,17},{2,18},{3,19},{4,20},{5,21},{6,22},{7,23},{8,24},{9,... | collective-permute-start | bytes 221192 | tf_op jit(solution)/shard_map/ppermute | solution.py:588
  114.1 7.5 %collective-permute-start.36 = (bf16[48,768]{1,0:T(8,128)(2,1)S(1)}, bf16[48,768]{1,0:T(8,128)(2,1)S(1)}, u32[]{:S(2)}, u32[]{:S(2)}) collective-permute-start(bf16[48,768]{1,0:T(8,128)(2,1)S(1)} %get-tuple-element.242), channel_id=1, source_target_pairs={{0,24},{1,25},{2,26},{3,27},{4,28},{5,29},{6,30},{7,31},{8,16},{9,... | collective-permute-start | bytes 221192 | tf_op jit(solution)/shard_map/ppermute | solution.py:588
  117.1 6.4 %collective-permute-start.31 = (bf16[80,384]{1,0:T(8,128)(2,1)S(1)}, bf16[80,384]{1,0:T(8,128)(2,1)S(1)}, u32[]{:S(2)}, u32[]{:S(2)}) collective-permute-start(bf16[80,384]{1,0:T(8,128)(2,1)S(1)} %get-tuple-element.251), channel_id=1, source_target_pairs={{0,8},{1,9},{2,10},{3,11},{4,12},{5,13},{6,14},{7,15},{8,0},{9,1},... | collective-permute-start | bytes 184328 | tf_op jit(solution)/shard_map/ppermute | solution.py:588
  117.2 6.8 %collective-permute-start.32 = (bf16[80,384]{1,0:T(8,128)(2,1)S(1)}, bf16[80,384]{1,0:T(8,128)(2,1)S(1)}, u32[]{:S(2)}, u32[]{:S(2)}) collective-permute-start(bf16[80,384]{1,0:T(8,128)(2,1)S(1)} %get-tuple-element.252), channel_id=1, source_target_pairs={{0,16},{1,17},{2,18},{3,19},{4,20},{5,21},{6,22},{7,23},{8,24},{9,... | collective-permute-start | bytes 184328 | tf_op jit(solution)/shard_map/ppermute | solution.py:588
  118.7 6.1 %collective-permute-start.33 = (bf16[80,384]{1,0:T(8,128)(2,1)S(1)}, bf16[80,384]{1,0:T(8,128)(2,1)S(1)}, u32[]{:S(2)}, u32[]{:S(2)}) collective-permute-start(bf16[80,384]{1,0:T(8,128)(2,1)S(1)} %get-tuple-element.253), channel_id=1, source_target_pairs={{0,24},{1,25},{2,26},{3,27},{4,28},{5,29},{6,30},{7,31},{8,16},{9,... | collective-permute-start | bytes 184328 | tf_op jit(solution)/shard_map/ppermute | solution.py:588

commit v3 on v2

--- a/solution.py
+++ b/solution.py
@@ -117,9 +117,10 @@
     return jnp.where(rows == lanes, four, jnp.zeros_like(four))
 
 
-def assemble(idx, refs, put):
+def assemble(idx, refs, put, order=(0, 1, 2, 3)):
     for e, k, s, row, head in owners(idx):
-        put(row, head, refs[e * 4 + k][s * 48 : (s + 1) * 48, :])
+        start = (k * 4 + order.index(s)) * 48
+        put(row, head, refs[e][start : start + 48, :])
 
 
 UNITS = [(win, g) for win in range(4) for g in range(GROUPS)]
@@ -151,15 +152,11 @@
     return jnp.concatenate(rows, axis=0)
 
 
-def canvas_start(step):
-    return pl.multiple_of((step // 4) * QUAD_ROWS + (step % 4) * 192, 16)
-
-
 def pack_attention(qkv, out_t, first):
     first[...] = jnp.concatenate([qkv[0], qkv[1], qkv[2], out_t[...]], axis=1).astype(BF)
 
 
-def pack_mlp(expand, contract_t, qv, eb, table_t, second, own):
+def pack_mlp(after, expand, contract_t, qv, eb, table_t, second, own):
     second[:, 0:WIDTH] = expand[...].astype(BF)
     second[:, WIDTH:] = contract_t[...].astype(BF)
     own[...] = jnp.zeros(own.shape, BF)
@@ -169,39 +166,11 @@
 
 
 def prepare(
-    idx, own, by_c, by_x, by_xc, tok, gout, crop, rows_c, cols_c, par_h,
-    na, xt, ut, u, tokv, goutv, got, tb, bias, eb, code_row, code_col, par, down, across,
-    sbuf,
+    idx, after, tok, gout, crop, rows_c, cols_c, par_h,
+    na, xt, ut, u, tokv, goutv, got, code_row, code_col, par, down, across,
 ):
-    x, c = idx[2], idx[3]
-    for ref, dx, dc in ((own, 0, 0), (by_c, 0, 1), (by_x, 1, 0), (by_xc, 1, 1)):
-        sbuf[(x ^ dx) * 2 + (c ^ dc)] = ref[...].astype(F32)
-    pad = jnp.zeros((1, WIDTH), F32)
-    qv = [jnp.concatenate([sbuf[h, r : r + 1, 0:96] for h in range(4)], axis=1) for r in (0, 1)]
-    bias[0:16, :] = jnp.concatenate(
-        [jnp.concatenate([qv[0], pad, qv[1]], axis=1), jnp.zeros((15, 3 * WIDTH), F32)], axis=0
-    ).astype(BF)
-    eb[...] = jnp.concatenate(
-        [
-            jnp.concatenate([sbuf[h, 2:3, :] for h in range(4)], axis=1),
-            jnp.zeros((15, HIDDEN), F32),
-        ],
-        axis=0,
-    ).astype(BF)
-    up = onehot((SLOT, 128), 1, cols_c[0:SLOT, 2:3])
     down[...] = onehot((128, 2 * SLOT), 0, rows_c[3:4, 0 : 2 * SLOT])
-    over = onehot((256, SLOT), 0, rows_c[4:5, 0:SLOT])
-    across[...] = over
-    for g in range(GROUPS):
-        blocks = []
-        for h in range(g * PACK, (g + 1) * PACK):
-            row = sbuf[h // 3, 3 + h % 3 : 4 + h % 3, 0:256]
-            lines = pltpu.roll(
-                jnp.broadcast_to(row, (128, 256)), 129, axis=1, stride=1, stride_axis=0
-            )
-            keyed = dot_nn(up, lines.astype(BF)).astype(BF)
-            blocks.append(dot_nn(keyed, over))
-        tb[g] = jnp.concatenate(blocks, axis=1) * LOG2E
+    across[...] = onehot((256, SLOT), 0, rows_c[4:5, 0:SLOT])
     tokv[...] = tok[...]
     goutv[...] = gout[...]
     par[...] = jnp.concatenate([par_h[...], jnp.zeros((2, WIDTH), F32)], axis=0)
@@ -230,15 +199,52 @@
     got[...] = gout[...].T
 
 
+def spread_small(idx, own, by_c, cols_c, across, tb, bias, eb, sbuf):
+    x, c = idx[2], idx[3]
+    for ref, dc in ((own, 0), (by_c, 1)):
+        for dx in range(2):
+            sbuf[(x ^ dx) * 2 + (c ^ dc)] = ref[16 * dx : 16 * (dx + 1), :].astype(F32)
+    pad = jnp.zeros((1, WIDTH), F32)
+    qv = [jnp.concatenate([sbuf[h, r : r + 1, 0:96] for h in range(4)], axis=1) for r in (0, 1)]
+    bias[0:16, :] = jnp.concatenate(
+        [jnp.concatenate([qv[0], pad, qv[1]], axis=1), jnp.zeros((15, 3 * WIDTH), F32)], axis=0
+    ).astype(BF)
+    eb[...] = jnp.concatenate(
+        [
+            jnp.concatenate([sbuf[h, 2:3, :] for h in range(4)], axis=1),
+            jnp.zeros((15, HIDDEN), F32),
+        ],
+        axis=0,
+    ).astype(BF)
+    up = onehot((SLOT, 128), 1, cols_c[0:SLOT, 2:3])
+    for g in range(GROUPS):
+        blocks = []
+        for h in range(g * PACK, (g + 1) * PACK):
+            row = sbuf[h // 3, 3 + h % 3 : 4 + h % 3, 0:256]
+            lines = pltpu.roll(
+                jnp.broadcast_to(row, (128, 256)), 129, axis=1, stride=1, stride_axis=0
+            )
+            keyed = dot_nn(up, lines.astype(BF)).astype(BF)
+            blocks.append(dot_nn(keyed, across[...]))
+        tb[g] = jnp.concatenate(blocks, axis=1) * LOG2E
+
+
+BATCH = 4
+
+
+def canvas_start(step):
+    return pl.multiple_of((step // 4) * QUAD_ROWS + (step % 4) * 192, 16)
+
+
 def attention_forward(
-    idx, p0, p1, p2, p3, p4, p5, p6, p7, nas, codes_row, codes_col, u, bias, tb,
+    idx, mine, other, nas, codes_row, codes_col, u, bias, tb,
     mrg, qt, kt, vv, pt, mt, wnat, outt, wout,
     wbuf, waug, wt,
 ):
     def put(row, head, value):
         wbuf[head, pl.ds(row, 48), :] = value
 
-    assemble(idx, (p0, p1, p2, p3, p4, p5, p6, p7), put)
+    assemble(idx, (mine, other), put)
     for j in range(3):
         waug[0:WIDTH, j * WIDTH : (j + 1) * WIDTH] = jnp.concatenate(
             [wbuf[h, :, 96 * j : 96 * (j + 1)] for h in range(4)], axis=1
@@ -251,42 +257,47 @@
     wnat[...] = waug[0:WIDTH, :]
     wt[...] = waug[...].T
 
-    def canvas(step, carry):
-        turn = step % 4
-        start = canvas_start(step)
-        na = nas[step]
-        all_t = dot_nt(wt[...], na).astype(BF)
-        kv = dot_nt(na, wt[WIDTH:, :]).astype(BF)
-        q_t, v_t = all_t[0:WIDTH], all_t[2 * WIDTH :]
-        code_row, code_col = codes_row[step], codes_col[step]
-        masks = []
-        for win in range(4):
-            row = jnp.concatenate([code_row[0:1, window(win)]] * PACK, axis=1)
-            masks.append(jnp.where(code_col[window(win), 0:1] == row, 0.0, MASKED))
+    def canvases(batch, carry):
+        steps = [batch * BATCH + i for i in range(BATCH)]
+        units = [(i, w, g) for i in range(BATCH) for w, g in UNITS]
+        all_t = [dot_nt(wt[...], nas[s]).astype(BF) for s in steps]
+        kv = [dot_nt(nas[s], wt[WIDTH:, :]).astype(BF) for s in steps]
+        masks = {}
+        for i, s in enumerate(steps):
+            for win in range(4):
+                row = jnp.concatenate([codes_row[s, 0:1, window(win)]] * PACK, axis=1)
+                masks[i, win] = jnp.where(codes_col[s, window(win), 0:1] == row, 0.0, MASKED)
         scores = {
-            (w, g): dot_nn(kv[window(w), feats(g)], spread(q_t[feats(g), window(w)]))
-            for w, g in UNITS
+            (i, w, g): dot_nn(kv[i][window(w), feats(g)], spread(all_t[i][feats(g), window(w)]))
+            for i, w, g in units
         }
         probs = {}
-        for w, g in UNITS:
-            sc = scores[w, g] * (SCALE * LOG2E) + (tb[g] + masks[w])
+        for i, w, g in units:
+            sc = scores[i, w, g] * (SCALE * LOG2E) + (tb[g] + masks[i, w])
             grown = jnp.exp2(sc - jnp.max(sc, axis=0, keepdims=True))
-            probs[w, g] = (grown * (1.0 / jnp.sum(grown, axis=0, keepdims=True))).astype(BF)
-        mixed = {(w, g): dot_nn(v_t[feats(g), window(w)], probs[w, g]) for w, g in UNITS}
-        merged_t = own_blocks(mixed).astype(BF)
-        back = dot_nt(u[turn], merged_t).astype(BF)
-        for w, g in UNITS:
-            pt[step, w * GROUPS + g] = probs[w, g]
-        mt[step] = merged_t
-        qt[step] = q_t
-        kt[step] = all_t[WIDTH : 2 * WIDTH]
-        vv[step] = kv[:, WIDTH:]
-        begin = pl.ds(start, 16)
-        mrg[begin, :] = back[0:16] + jnp.where(turn == 0, jnp.zeros((16, WIDTH), BF), mrg[begin, :])
-        mrg[pl.ds(pl.multiple_of(start + 16, 16), SPAN - 16), :] = back[16:]
+            probs[i, w, g] = (grown * (1.0 / jnp.sum(grown, axis=0, keepdims=True))).astype(BF)
+        mixed = {
+            (i, w, g): dot_nn(all_t[i][2 * WIDTH :][feats(g), window(w)], probs[i, w, g])
+            for i, w, g in units
+        }
+        for i, s in enumerate(steps):
+            turn, start = s % 4, canvas_start(s)
+            merged_t = own_blocks({(w, g): mixed[i, w, g] for w, g in UNITS}).astype(BF)
+            back = dot_nt(u[turn], merged_t).astype(BF)
+            for w, g in UNITS:
+                pt[s, w * GROUPS + g] = probs[i, w, g]
+            mt[s] = merged_t
+            qt[s] = all_t[i][0:WIDTH]
+            kt[s] = all_t[i][WIDTH : 2 * WIDTH]
+            vv[s] = kv[i][:, WIDTH:]
+            begin = pl.ds(start, 16)
+            mrg[begin, :] = back[0:16] + jnp.where(
+                turn == 0, jnp.zeros((16, WIDTH), BF), mrg[begin, :]
+            )
+            mrg[pl.ds(pl.multiple_of(start + 16, 16), SPAN - 16), :] = back[16:]
         return carry
 
-    lax.fori_loop(0, nas.shape[0], canvas, 0)
+    lax.fori_loop(0, nas.shape[0] // BATCH, canvases, 0)
 
 
 TILE = 784
@@ -310,18 +321,17 @@
 
 
 def mlp(
-    idx, p0, p1, p2, p3, p4, p5, p6, p7, n2, n2t, got, gout, eb,
+    idx, mine, other, n2, n2t, got, gout, eb,
     acc_m, acc_g, keep, send, ebg,
     eaug, ct, hid, gpr, cg, eg,
 ):
-    tiles = gout.shape[0] // TILE
 
     def put(row, head, value):
         lanes = pl.ds(pl.multiple_of(head * WIDTH, 128), WIDTH)
         eaug[pl.ds(row, 48), lanes] = value[:, 0:WIDTH]
         ct[pl.ds(row, 48), lanes] = value[:, WIDTH:]
 
-    assemble(idx, (p0, p1, p2, p3, p4, p5, p6, p7), put)
+    assemble(idx, (mine, other), put, order=(0, 2, 1, 3))
     eaug[WIDTH : WIDTH + 16, :] = eb[...]
     eaug[WIDTH + 16 : 512, :] = jnp.zeros((112, HIDDEN), BF)
     acc_m[...] = jnp.zeros(acc_m.shape, F32)
@@ -330,21 +340,16 @@
     def chunk(step, carry):
         cols = pl.ds(pl.multiple_of(step * CHUNK, 128), CHUNK)
 
-        def unit_rows(t, carry):
-            rows = pl.ds(pl.multiple_of(t * TILE, 16), TILE)
-            pre = dot_nn(n2[rows, :], eaug[:, cols])
-            grad_hidden = dot_nn(gout[rows, :], ct[:, cols])
-            phi = 0.5 + 0.5 * lax.erf(pre * ROOT_HALF)
-            bell = jnp.exp2(pre * pre * (-0.5 * LOG2E)) * INV_ROOT_TWO_PI
-            hidden = (pre * phi).astype(BF)
-            grad_pre = (grad_hidden * (phi + pre * bell)).astype(BF)
-            hid[rows, :] = hidden
-            gpr[rows, :] = grad_pre
-            acc_m[rows, :] += dot_nt(hidden, ct[:, cols])
-            acc_g[rows, :] += dot_nt(grad_pre, eaug[0:WIDTH, cols])
-            return carry
-
-        lax.fori_loop(0, tiles, unit_rows, 0)
+        pre = dot_nn(n2[...], eaug[:, cols])
+        grad_hidden = dot_nn(gout[...], ct[:, cols])
+        phi = 0.5 + 0.5 * lax.erf(pre * ROOT_HALF)
+        bell = jnp.exp2(pre * pre * (-0.5 * LOG2E)) * INV_ROOT_TWO_PI
+        hidden = (pre * phi).astype(BF)
+        grad_pre = (grad_hidden * (phi + pre * bell)).astype(BF)
+        hid[...] = hidden
+        gpr[...] = grad_pre
+        acc_m[...] += dot_nt(hidden, ct[:, cols])
+        acc_g[...] += dot_nt(grad_pre, eaug[0:WIDTH, cols])
         cg[:, cols] = dot_nn(got[...], hid[...]).astype(BF)
         grads = dot_nn(n2t[...], gpr[...])
         eg[:, cols] = grads[0:WIDTH].astype(BF)
@@ -387,50 +392,64 @@
     oacc[...] = jnp.zeros(oacc.shape, F32)
     wacc[...] = jnp.zeros(wacc.shape, F32)
 
-    def canvas(step, carry):
-        turn = step % 4
-        rows = pl.ds(canvas_start(step), SPAN)
-        gmw = dot_nn(ut[turn], gmid[rows, :].astype(BF)).astype(BF)
-        gmt = dot_nt(wout[...], gmw).astype(BF)
-        q_t, k_t, v_w = qt[step], kt[step], vv[step]
-        gm_s = {(w, g): spread(gmt[feats(g), window(w)]) for w, g in UNITS}
-        q_s = {(w, g): spread(q_t[feats(g), window(w)]) for w, g in UNITS}
-        gp = {(w, g): dot_nn(v_w[window(w), feats(g)], gm_s[w, g]) for w, g in UNITS}
-        probs_b = {(w, g): pt[step, w * GROUPS + g] for w, g in UNITS}
-        gs = {}
-        for w, g in UNITS:
-            probs = probs_b[w, g].astype(F32)
-            delta = jnp.sum(probs * gp[w, g], axis=0, keepdims=True)
-            gs[w, g] = (probs * (gp[w, g] - delta)).astype(BF)
-        gq = {(w, g): dot_nn(k_t[feats(g), window(w)], gs[w, g]) for w, g in UNITS}
-        gk = {(w, g): dot_nt(q_s[w, g], gs[w, g]) for w, g in UNITS}
-        gv = {(w, g): dot_nt(gm_s[w, g], probs_b[w, g]) for w, g in UNITS}
-
-        def rows_of(parts):
-            return jnp.concatenate(
-                [
-                    jnp.concatenate([parts[w, g] for w in range(4)], axis=1)
-                    for g in range(GROUPS)
-                ],
-                axis=0,
-            )
-
-        g_all = jnp.concatenate(
-            [
-                (own_blocks(gq) * SCALE).astype(BF),
-                (rows_of(gk) * SCALE).astype(BF),
-                rows_of(gv).astype(BF),
-            ],
+    def rows_of(parts):
+        return jnp.concatenate(
+            [jnp.concatenate([parts[w, g] for w in range(4)], axis=1) for g in range(GROUPS)],
             axis=0,
         )
-        gta[step] = g_all
-        wacc[...] += dot_nt(xt[step], g_all)
-        oacc[...] += dot_nn(mt[step], gmw)
+
+    def canvases(batch, carry):
+        steps = [batch * BATCH + i for i in range(BATCH)]
+        units = [(i, w, g) for i in range(BATCH) for w, g in UNITS]
+        gmw = [
+            dot_nn(ut[s % 4], gmid[pl.ds(canvas_start(s), SPAN), :].astype(BF)).astype(BF)
+            for s in steps
+        ]
+        gmt = [dot_nt(wout[...], v).astype(BF) for v in gmw]
+        gm_s = {(i, w, g): spread(gmt[i][feats(g), window(w)]) for i, w, g in units}
+        gp = {
+            (i, w, g): dot_nn(vv[steps[i], window(w), feats(g)], gm_s[i, w, g])
+            for i, w, g in units
+        }
+        gs = {}
+        for i, w, g in units:
+            probs = pt[steps[i], w * GROUPS + g].astype(F32)
+            delta = jnp.sum(probs * gp[i, w, g], axis=0, keepdims=True)
+            gs[i, w, g] = (probs * (gp[i, w, g] - delta)).astype(BF)
+        q_s = {(i, w, g): spread(qt[steps[i], feats(g), window(w)]) for i, w, g in units}
+        gq = {
+            (i, w, g): dot_nn(kt[steps[i], feats(g), window(w)], gs[i, w, g])
+            for i, w, g in units
+        }
+        gk = {(i, w, g): dot_nt(q_s[i, w, g], gs[i, w, g]) for i, w, g in units}
+        gv = {
+            (i, w, g): dot_nt(gm_s[i, w, g], pt[steps[i], w * GROUPS + g]) for i, w, g in units
+        }
+        g_all = []
+        for i in range(BATCH):
+            parts = [{(w, g): v[i, w, g] for w, g in UNITS} for v in (gq, gk, gv)]
+            g_all.append(
+                jnp.concatenate(
+                    [
+                        (own_blocks(parts[0]) * SCALE).astype(BF),
+                        (rows_of(parts[1]) * SCALE).astype(BF),
+                        rows_of(parts[2]).astype(BF),
+                    ],
+                    axis=0,
+                )
+            )
+            gta[steps[i]] = g_all[i]
+        wacc[...] += dot_nt(
+            jnp.concatenate([xt[s] for s in steps], axis=1), jnp.concatenate(g_all, axis=1)
+        )
+        oacc[...] += dot_nn(
+            jnp.concatenate([mt[s] for s in steps], axis=1), jnp.concatenate(gmw, axis=0)
+        )
         for g in range(GROUPS):
-            table[g] += sum(gs[w, g].astype(F32) for w in range(4))
+            table[g] += sum(gs[i, w, g].astype(F32) for i in range(BATCH) for w in range(4))
         return carry
 
-    lax.fori_loop(0, qt.shape[0], canvas, 0)
+    lax.fori_loop(0, qt.shape[0] // BATCH, canvases, 0)
     columns = par[...].T
     gain, offset = columns[:, 0:1], columns[:, 1:2]
     totals = wacc[WIDTH : WIDTH + 1, :]
@@ -465,18 +484,19 @@
     send[768:800, :] = small
 
 
-def tokens_end(tok, gmid, gta, wnat, u, par, gtok):
+def tokens_end(tok, gmid, gta, wnat, u, par, *refs):
+    state, (gtok, *near) = refs[: len(refs) // 2], refs[len(refs) // 2 :]
+    for source, target in zip(state, near):
+        target[...] = source[...]
+
     def block_rows(block, carry):
-        ends = []
-        for turn in range(4):
-            g1t = dot_nn(wnat[...], gta[4 * block + turn])
-            high = g1t.astype(BF)
-            low = (g1t - high.astype(F32)).astype(BF)
-            ends.append(dot_nt(u[turn], high) + dot_nt(u[turn], low))
+        ends = [
+            dot_nt(u[turn], gta[4 * block + turn]).astype(BF) for turn in range(4)
+        ]
         pieces = [ends[0][0:192]]
         for turn in range(1, 4):
             pieces += [ends[turn - 1][192:] + ends[turn][0:16], ends[turn][16:192]]
-        g1 = jnp.concatenate([*pieces, ends[3][192:]], axis=0)
+        g1 = dot_nt(jnp.concatenate([*pieces, ends[3][192:]], axis=0), wnat[...])
         rows = pl.ds(pl.multiple_of(block * QUAD_ROWS, 16), QUAD_ROWS)
         hat, inv = stats(tok[rows, :].astype(F32))
         gtok[rows, :] = gmid[rows, :] + norm_back(g1, hat, inv, par[0:1, :])
@@ -501,13 +521,10 @@
                 refs[k][192:, :] = small.astype(BF)
 
 
-def line_sum(own, r1, r2, r3, *refs):
-    small = None
+def line_sum(own, r1, r2, r3, mine, *refs):
     parts = (r1, r2, r3)
-    if len(refs) > 4:
-        mine, *refs = refs
-        small = mine[...] + sum(r[192:, :].astype(F32) for r in parts)
-        refs[4][...] = small
+    small = mine[...] + sum(r[192:, :].astype(F32) for r in parts)
+    refs[4][...] = small
     for s in range(4):
         block = slice(s * 48, (s + 1) * 48)
         value = own[block, :] + sum(r[block, :].astype(F32) for r in parts)
@@ -515,8 +532,15 @@
             refs[0][...] = value
         else:
             refs[s][0:48, :] = value.astype(BF)
-            if small is not None:
-                refs[s][48:, :] = small.astype(BF)
+            refs[s][48:, :] = small.astype(BF)
+
+
+def half_sum(own, *refs):
+    parts, (keep, send) = refs[:-2], refs[-2:]
+    half = own.shape[0] // 2
+    total = own[...] + sum(r[...].astype(F32) for r in parts)
+    keep[...] = total[0:half]
+    send[...] = total[half:].astype(BF)
 
 
 def adamw(master, grad, moment, square, step_rate, decay_rate):
@@ -537,24 +561,22 @@
         out[at] = new
 
 
-def step_mlp(n_parts, *refs):
+def step_all(n_mlp, n_parts, rows, idx, *refs):
+    parts, refs = refs[:n_mlp], refs[n_mlp:]
+    total = sum(r[...].astype(F32) for r in parts)
     parts, refs = refs[:n_parts], refs[n_parts:]
-    total = sum(r[...].astype(F32) for r in parts)
-    update(refs[0:3], total[:, 0:WIDTH], refs[6:9], RATE_MATRIX, DECAY_MATRIX)
-    update(refs[3:6], total[:, WIDTH:], refs[9:12], RATE_MATRIX, DECAY_MATRIX)
-
-
-def step_attention(n_parts, rows, idx, *refs):
-    parts, refs = refs[:n_parts], refs[n_parts:]
+    half = (len(refs) - 1) // 2
+    small, ins, outs = refs[0], refs[1 : half + 1], refs[half + 1 :]
+    update(ins[0:3], total[:, 0:WIDTH], outs[0:3], RATE_MATRIX, DECAY_MATRIX)
+    update(ins[3:6], total[:, WIDTH:], outs[3:6], RATE_MATRIX, DECAY_MATRIX)
+    ins, outs = ins[6:], outs[6:]
     total = sum(r[0:rows, :].astype(F32) for r in parts)
-    small, refs = refs[0], refs[1:]
     small = small[...] + sum(r[rows:, :].astype(F32) for r in parts[1:])
     head = idx[2] * 2 + idx[3]
 
     def pick(blocks):
         return sum(jnp.where(head == h, block, 0.0) for h, block in enumerate(blocks))
 
-    ins, outs = refs[:18], refs[18:]
     for j in range(3):
         update(
             ins[0:3], total[:, 96 * j : 96 * (j + 1)], outs[0:3], RATE_MATRIX, DECAY_MATRIX, at=j
@@ -590,18 +612,22 @@
     def groups(self):
         return [[i * self.outer + j for j in range(self.outer)] for i in range(8)]
 
-    def gather_line(self, shard):
+    def outer_gather(self, shard):
         if self.outer > 1:
             shard = lax.all_gather(
                 shard, "dp", axis=0, tiled=True, axis_index_groups=self.groups()
             )
+        return shard
+
+    def gather_line(self, shard):
         return jnp.concatenate([shard] + [self.send(shard, z=s) for s in range(1, 4)], axis=0)
 
     def gather_plane(self, line):
         return [line] + [self.send(line, x=k & 1, y=k >> 1) for k in range(1, 4)]
 
     def gather_core(self, plane):
-        return list(plane) + [self.send(part, c=1) for part in plane]
+        plane = jnp.concatenate(plane, axis=0)
+        return plane, self.send(plane, c=1)
 
     def to_plane(self, blocks):
         return [self.send(b, x=k & 1, y=k >> 1) for k, b in enumerate(blocks, 1)]
@@ -667,40 +693,44 @@
     tm = (canvases, slots, WIDTH)
 
     rows_own = exp_w.shape[0]
-    (first,) = call(pack_attention, [((rows_own, WIDTH), BF)], Far(qkv_w), Far(out_w.T))
-    line = links.gather_line(first)
-    firsts = links.gather_plane(line)
+    (first,) = call(
+        pack_attention, [((rows_own, WIDTH), BF)], Far(qkv_w), Far(out_w.T),
+    )
     second, own = call(
         pack_mlp, [((rows_own, 2 * WIDTH), BF), ((16, WIDTH), BF)],
-        Far(exp_w), Far(con_w.T), Far(qv_b), Far(exp_b), Far(table_w.T),
-    )
-    by_c, by_x, by_xc = links.send(own, c=1), links.send(own, x=1), links.send(own, x=1, c=1)
-
+        first[0:1, 0:128], Far(exp_w), Far(con_w.T), Far(qv_b), Far(exp_b), Far(table_w.T),
+    )
+    first = links.outer_gather(first)
+    line = links.gather_line(first)
+    second = links.outer_gather(second)
+    pair_s = jnp.concatenate([second, links.send(second, z=2)], axis=0)
+    own = jnp.concatenate([own, links.send(own, x=1)], axis=0)
+    line, pair_s, own = lax.optimization_barrier((line, pair_s, own))
+    plane = links.gather_plane(line)
+    by_c = links.send(own, c=1)
+    by_c, pair_s = lax.optimization_barrier((by_c, pair_s))
+    line_s = jnp.concatenate([pair_s, links.send(pair_s, z=1)], axis=0)
     crop_rows = crop_ids.reshape(-1, QUAD_ROWS)
     rows_c, cols_c = (jnp.asarray(t) for t in tables())
-    line, own = lax.optimization_barrier((line, own))
     to_slots = (4, slots, SPAN)
-    prepared = call(
+    nas, xt, ut, u, tok, gout, got, code_row, code_col, par, down, across = call(
         prepare,
         [
             ((canvases, slots, 512), BF), ((canvases, 400, slots), BF), (to_slots, BF),
             ((4, SPAN, slots), BF), (wide, BF), (wide, BF), ((WIDTH, rows_all), BF),
-            ((GROUPS, SLOT, slots), F32), ((16, 3 * WIDTH), BF), ((16, HIDDEN), BF),
             ((canvases, 8, slots), F32), ((canvases, slots, 8), F32), ((8, WIDTH), F32),
             ((128, 2 * SLOT), BF), ((256, SLOT), BF),
         ],
-        own, by_c, by_x, by_xc, Far(tokens), Far(grad_out), Far(crop_rows), Far(rows_c),
-        Far(cols_c), Far(norm_p),
-        scratch=[((4, 16, WIDTH), F32)], limit=16, scalars=idx, time=5,
-    )
-    (second, *prepared) = lax.optimization_barrier((second, *prepared))
-    nas, xt, ut, u, tok, gout, got, bias_t, bias16, eb16, code_row, code_col, par = prepared[:13]
-    down, across = prepared[13:]
-    line_s = links.gather_line(second)
+        by_c, Far(tokens), Far(grad_out), Far(crop_rows), Far(rows_c), Far(cols_c),
+        Far(norm_p), limit=16, scalars=idx, time=4,
+    )
+    bias_t, bias16, eb16 = call(
+        spread_small, [((GROUPS, SLOT, slots), F32), ((16, 3 * WIDTH), BF), ((16, HIDDEN), BF)],
+        own, by_c, Far(cols_c), across, scratch=[((4, 16, WIDTH), F32)], scalars=idx,
+    )
+    *plane, line_s, bias_t = lax.optimization_barrier((*plane, line_s, bias_t))
     plane_s = links.gather_plane(line_s)
-    firsts = list(lax.optimization_barrier((*firsts, nas))[:4])
-    firsts = links.gather_core(firsts)
-    firsts[0], line_s = lax.optimization_barrier((firsts[0], line_s))
+    firsts = list(links.gather_core(plane))
     merged, qt, kt, vv, pt, mt, wnat, outt, wout = call(
         attention_forward,
         [
@@ -711,7 +741,7 @@
         scratch=[
             ((4, WIDTH, WIDTH), BF), ((512, 3 * WIDTH), BF), ((3 * WIDTH, 512), BF),
         ],
-        limit=10, scalars=idx, time=14,
+        limit=20, scalars=idx, time=11,
     )
     merged, *plane_s = lax.optimization_barrier((merged, *plane_s))
     seconds = links.gather_core(plane_s)
@@ -730,7 +760,7 @@
             ((512, HIDDEN), BF), ((WIDTH, HIDDEN), BF), ((rows_all, CHUNK), BF),
             ((rows_all, CHUNK), BF), ((WIDTH, HIDDEN), BF), ((WIDTH, HIDDEN), BF),
         ],
-        limit=24, scalars=idx, time=18,
+        limit=34, scalars=idx, time=17,
     )
     got_r = links.send(send_r, c=1)
     block_out, grad_mid, sums = call(
@@ -750,26 +780,36 @@
             ((4, WIDTH, WIDTH), BF), ((400, 3 * WIDTH), F32), (square, F32),
             ((GROUPS, SLOT, slots), F32),
         ],
-        limit=16, scalars=idx, time=20,
+        limit=24, scalars=idx, time=15,
     )
     *plane_r, send_q = lax.optimization_barrier((*plane_r, send_q))
     got_q = links.send(send_q, c=1)
+    own_r, block_r = call(
+        half_sum, [((96, 2 * WIDTH), F32), ((96, 2 * WIDTH), BF)], own_r, *plane_r,
+    )
+    got_q, block_r = lax.optimization_barrier((got_q, block_r))
     block_q = [((192, WIDTH), F32)] + [((224, WIDTH), BF)] * 3 + [((32, WIDTH), F32)]
     own_q, *blocks_q, small = call(plane_sum, block_q, keep_q, got_q)
     plane_q = links.to_plane(blocks_q)
-    plane_r = lax.optimization_barrier((*plane_r, *blocks_q))[:3]
-    line_r = [((48, 2 * WIDTH), F32)] + [((48, 2 * WIDTH), BF)] * 3
-    own_r, *blocks_r = call(line_sum, line_r, own_r, *plane_r)
-    parts_r = links.to_line(blocks_r)
-    g_all = lax.optimization_barrier((g_all, *blocks_r))[0]
-    (grad_tokens,) = call(
-        tokens_end, [(wide, F32)], tok, grad_mid, g_all, wnat, u, par, far=(0,), time=5,
-    )
-    *plane_q, grad_tokens = lax.optimization_barrier((*plane_q, grad_tokens))
+    got_r = links.send(block_r, z=2)
+    g_all = lax.optimization_barrier((g_all, *blocks_q))[0]
+    state = [
+        exp_w, exp_m, exp_s, con_w.T, con_m.T, con_s.T, qkv_w, qkv_m, qkv_s, out_w.T, out_m.T,
+        out_s.T, qv_b, qv_m, qv_s, exp_b, eb_m, eb_s, table_w.T, tab_m.T, tab_s.T, norm_p, norm_m,
+        norm_s,
+    ]
+    grad_tokens, *near = call(
+        tokens_end, [(wide, F32)] + [(a.shape, F32) for a in state],
+        tok, grad_mid, g_all, wnat, u, par, *(Far(a) for a in state), far=(0,), time=5,
+    )
+    *plane_q, got_r, grad_tokens = lax.optimization_barrier((*plane_q, got_r, grad_tokens))
     line_q = [((48, WIDTH), F32)] + [((80, WIDTH), BF)] * 3 + [((32, WIDTH), F32)]
     own_q, *blocks_q, small = call(line_sum, line_q, own_q, *plane_q, small)
-    parts_q = links.to_line(blocks_q)
-    parts_q, parts_r = [own_q, *parts_q], [own_r, *parts_r]
+    parts_q = [own_q, *links.to_line(blocks_q)]
+    own_r, block_r = call(
+        half_sum, [((48, 2 * WIDTH), F32), ((48, 2 * WIDTH), BF)], own_r, got_r,
+    )
+    parts_r = [own_r, links.send(block_r, z=1)]
     rows = 48
     if links.outer > 1:
         small = small + sum(p[48:].astype(F32) for p in parts_q[1:])
@@ -777,20 +817,12 @@
         parts_q = [links.outer_sum(sum(p[:48].astype(F32) for p in parts_q))]
         parts_r = [links.outer_sum(sum(p.astype(F32) for p in parts_r))]
         rows = parts_q[0].shape[0]
-
-    mlp_state = [exp_w, exp_m, exp_s, con_w.T, con_m.T, con_s.T]
-    third = call(
-        functools.partial(step_mlp, len(parts_r)), [(a.shape, F32) for a in mlp_state],
-        *parts_r, *(Far(a) for a in mlp_state), far=range(6), time=2,
-    )
-    state = [
-        qkv_w, qkv_m, qkv_s, out_w.T, out_m.T, out_s.T, qv_b, qv_m, qv_s, exp_b, eb_m, eb_s,
-        table_w.T, tab_m.T, tab_s.T, norm_p, norm_m, norm_s,
-    ]
-    fourth = call(
-        functools.partial(step_attention, len(parts_q), rows), [(a.shape, F32) for a in state],
-        *parts_q, small, *(Far(a) for a in state), scalars=idx, far=range(18), time=2,
-    )
+    news = call(
+        functools.partial(step_all, len(parts_r), len(parts_q), rows),
+        [(a.shape, F32) for a in state], *parts_r, *parts_q, small, *near, scalars=idx,
+        far=range(len(state)), time=2,
+    )
+    third, fourth = news[0:6], news[6:]
     return (
         block_out, grad_tokens, *fourth[0:3], *(a.T for a in fourth[3:6]), *third[0:3],
         *(a.T for a in third[3:6]), *fourth[6:12], *(a.T for a in fourth[12:15]), *fourth[15:],

time: 127 us -> 113 us (0.89)
  Pallas kernels: 75.4 us -> 65.2 us
  starting transfers between devices: 36 us -> 33.8 us
  waiting for transfers between devices: 13.6 us -> 11.5 us
    pallas_call x15 -> x16, Pallas kernels: 75.4 us -> 65.2 us  [call(): pl.pallas_call(kernel, in_specs=[SMEM] * len(lead) + [VMEM] * len(args),...]
    ppermute x37 -> x28, starting transfers between devices: 36 us -> 33.8 us  [send(): return lax.ppermute(value, ('dp', 'head'), self.perm(**flips))]
    ppermute x37 -> x28, waiting for transfers between devices: 13.6 us -> 11.5 us  [send(): return lax.ppermute(value, ('dp', 'head'), self.perm(**flips))]
  transfers between devices with their start and end apart: 37 -> 28, of which waited for: 6 -> 8; matrix products, arithmetic and copies ran while one was open for 1% -> 1% of each run, Pallas kernels for 42% -> 39%
where the time goes in v3:
time: 113 us
  Pallas kernels  65.2 us (58%)
  starting transfers between devices  33.8 us (30%)
  waiting for transfers between devices  11.5 us (10%)
  between operations  1.22 us (1%)
    pallas_call x16, Pallas kernels, call(): pl.pallas_call(kernel, in_specs=[SMEM] * len(lead) + [VMEM] * len(args),...  65.2 us
    ppermute x28, starting transfers between devices, send(): return lax.ppermute(value, ('dp', 'head'), self.perm(**flips))  33.8 us
    ppermute x28, waiting for transfers between devices, send(): return lax.ppermute(value, ('dp', 'head'), self.perm(**flips))  11.5 us
  transfers between devices with their start and end apart: 28, of which 8 were waited for; matrix products, arithmetic and copies ran while one was open for 1% of the time, Pallas kernels for 39%

profile of v3, /device:TPU:0, one launch (start us, length us, event | category | flops | bytes accessed | tf_op | source)
XLA Modules:
  0.0 112.8 jit_solution(4070602800289375285)
XLA Ops:
  0.7 1.0 pack_attention.1
  1.6 0.0 copy-start.8
  1.7 1.0 pack_mlp.1
  2.6 3.0 %collective-permute-start.4 = (bf16[16,384]{1,0:T(8,128)(2,1)S(1)}, bf16[16,384]{1,0:T(8,128)(2,1)S(1)}, u32[]{:S(2)}, u32[]{:S(2)}) collective-permute-start(bf16[16,384]{1,0:T(8,128)(2,1)S(1)} %get-tuple-element.168), channel_id=1, source_target_pairs={{0,2},{1,3},{2,0},{3,1},{4,6},{5,7},{6,4},{7,5},{8,10},{9,11},{10,... | collective-permute-start | bytes 36872 | tf_op jit(solution)/shard_map/ppermute | solution.py:610
  5.6 3.6 %collective-permute-start.2 = (bf16[48,384]{1,0:T(8,128)(2,1)S(1)}, bf16[48,384]{1,0:T(8,128)(2,1)S(1)}, u32[]{:S(2)}, u32[]{:S(2)}) collective-permute-start(bf16[48,384]{1,0:T(8,128)(2,1)S(1)} %pack_attention.1), channel_id=1, source_target_pairs={{0,24},{1,25},{2,26},{3,27},{4,28},{5,29},{6,30},{7,31},{8,16},{9,... | collective-permute-start | bytes 110600 | tf_op jit(solution)/shard_map/ppermute | solution.py:610
  9.2 0.0 collective-permute-start.1
  9.2 0.8 collective-permute-start
  10.0 2.1 %collective-permute-start.3 = (bf16[48,768]{1,0:T(8,128)(2,1)S(1)}, bf16[48,768]{1,0:T(8,128)(2,1)S(1)}, u32[]{:S(2)}, u32[]{:S(2)}) collective-permute-start(bf16[48,768]{1,0:T(8,128)(2,1)S(1)} %get-tuple-element.167), channel_id=1, source_target_pairs={{0,16},{1,17},{2,18},{3,19},{4,20},{5,21},{6,22},{7,23},{8,24},{9,... | collective-permute-start | bytes 221192 | tf_op jit(solution)/shard_map/ppermute | solution.py:610
  12.2 2.6 %collective-permute-done.1 = bf16[48,384]{1,0:T(8,128)(2,1)S(1)} collective-permute-done((bf16[48,384]{1,0:T(8,128)(2,1)S(1)}, bf16[48,384]{1,0:T(8,128)(2,1)S(1)}, u32[]{:S(2)}, u32[]{:S(2)}) %collective-permute-start.1) | collective-permute-done | bytes 36896 | tf_op jit(solution)/shard_map/ppermute | solution.py:610
  14.8 0.8 collective-permute-done.3
  15.6 0.1 collective-permute-start.8
  15.6 0.1 pad_add_fusion.idx
  15.7 0.7 reshape.55.crop
  16.4 1.5 %collective-permute-start.7 = (bf16[192,384]{1,0:T(8,128)(2,1)S(1)}, bf16[192,384]{1,0:T(8,128)(2,1)S(1)}, u32[]{:S(2)}, u32[]{:S(2)}) collective-permute-start(bf16[192,384]{1,0:T(8,128)(2,1)S(1)} %pad_maximum_fusion.1), channel_id=1, source_target_pairs={{0,6},{1,7},{2,4},{3,5},{4,2},{5,3},{6,0},{7,1},{8,14},{9,15},{10,... | collective-permute-start | bytes 442376 | tf_op jit(solution)/shard_map/ppermute | solution.py:610
  17.9 0.5 collective-permute-start.6
  18.4 1.5 %collective-permute-start.5 = (bf16[192,384]{1,0:T(8,128)(2,1)S(1)}, bf16[192,384]{1,0:T(8,128)(2,1)S(1)}, u32[]{:S(2)}, u32[]{:S(2)}) collective-permute-start(bf16[192,384]{1,0:T(8,128)(2,1)S(1)} %pad_maximum_fusion.1), channel_id=1, source_target_pairs={{0,2},{1,3},{2,0},{3,1},{4,6},{5,7},{6,4},{7,5},{8,10},{9,11},{10,... | collective-permute-start | bytes 442376 | tf_op jit(solution)/shard_map/ppermute | solution.py:610
  19.9 0.0 collective-permute-done.8.after.by_c
  19.9 1.4 %collective-permute-start.9 = (bf16[96,768]{1,0:T(8,128)(2,1)S(1)}, bf16[96,768]{1,0:T(8,128)(2,1)S(1)}, u32[]{:S(2)}, u32[]{:S(2)}) collective-permute-start(bf16[96,768]{1,0:T(8,128)(2,1)S(1)} %pad_maximum_fusion.2), channel_id=1, source_target_pairs={{0,8},{1,9},{2,10},{3,11},{4,12},{5,13},{6,14},{7,15},{8,0},{9,1},... | collective-permute-start | bytes 442376 | tf_op jit(solution)/shard_map/ppermute | solution.py:610
  21.3 4.2 %prepare.1 = (bf16[8,256,512]{2,1,0:T(8,128)(2,1)S(1)}, bf16[8,400,256]{2,1,0:T(8,128)(2,1)S(1)}, bf16[4,256,208]{2,1,0:T(8,128)(2,1)S(1)}, bf16[4,208,256]{2,1,...) custom-call(s32[4]{0:T(128)S(1)} %pad_add_fusion.idx, ...), custom_call_target="tpu_custom_call" | custom-call | flops 4600000000 | tf_op jit(solution)/shard_map/prepare/pallas_call | solution.py:664
  25.5 1.5 %spread_small.1 = (f32[3,64,256]{2,1,0:T(8,128)S(1)}, bf16[16,1152]{1,0:T(8,128)(2,1)S(1)}, bf16[16,1536]{1,0:T(8,128)(2,1)S(1)}) custom-call(s32[4]{0:T(128)S(1)} %pad_add_fusion.idx, bf16[32,384]{1,0:T(8,128)(2,1)S(1)} %pad_maximum_fusion.3.own, bf16[32,384]{1,0:T(8,128)(2,1)S(1)} %collective-permute-done.8.after.by_c, f32[256,8]{1,0:T(8,128)} %constant.58.clone.cols_c, ...), custom_call_target="tpu_custom_call" | custom-call | flops 1150000000 | tf_op jit(solution)/shard_map/spread_small/pallas_call | solution.py:664
  27.0 0.0 collective-permute-done.9
  27.1 0.0 collective-permute-done.7
  27.2 0.1 collective-permute-start.10
  27.3 1.6 %collective-permute-start.13 = (bf16[192,768]{1,0:T(8,128)(2,1)S(1)}, bf16[192,768]{1,0:T(8,128)(2,1)S(1)}, u32[]{:S(2)}, u32[]{:S(2)}) collective-permute-start(bf16[192,768]{1,0:T(8,128)(2,1)S(1)} %pad_maximum_fusion), channel_id=1, source_target_pairs={{0,6},{1,7},{2,4},{3,5},{4,2},{5,3},{6,0},{7,1},{8,14},{9,15},{10,... | collective-permute-start | bytes 884744 | tf_op jit(solution)/shard_map/ppermute | solution.py:610
  28.9 0.5 collective-permute-start.12
  29.4 1.5 %collective-permute-start.11 = (bf16[192,768]{1,0:T(8,128)(2,1)S(1)}, bf16[192,768]{1,0:T(8,128)(2,1)S(1)}, u32[]{:S(2)}, u32[]{:S(2)}) collective-permute-start(bf16[192,768]{1,0:T(8,128)(2,1)S(1)} %pad_maximum_fusion), channel_id=1, source_target_pairs={{0,2},{1,3},{2,0},{3,1},{4,6},{5,7},{6,4},{7,5},{8,10},{9,11},{10,... | collective-permute-start | bytes 884744 | tf_op jit(solution)/shard_map/ppermute | solution.py:610
  30.9 0.0 collective-permute-done.10.other
  30.9 11.0 %attention_forward.1 = (bf16[1568,384]{1,0:T(8,128)(2,1)S(1)}, bf16[8,384,256]{2,1,0:T(8,128)(2,1)S(1)}, bf16[8,384,256]{2,1,0:T(8,128)(2,1)S(1)}, bf16[8,256,38...) custom-call(s32[4]{0:T(128)S(1)} %pad_add_fusion.idx, ...), custom_call_target="tpu_custom_call" | custom-call | flops 12650000384 | tf_op jit(solution)/shard_map/attention_forward/pallas_call | solution.py:664
  41.9 0.0 copy-start
  41.9 0.0 collective-permute-done.13
  41.9 2.0 %collective-permute-done.12 = bf16[192,768]{1,0:T(8,128)(2,1)S(1)} collective-permute-done((bf16[192,768]{1,0:T(8,128)(2,1)S(1)}, bf16[192,768]{1,0:T(8,128)(2,1)S(1)}, u32[]{:S(2)}, u32[]{:S(2)}) %collective-permute-start.12) | collective-permute-done | bytes 294944 | tf_op jit(solution)/shard_map/ppermute | solution.py:610
  44.0 0.1 collective-permute-done.11
  44.2 0.1 collective-permute-start.14
  44.2 2.4 %mlp_begin.1 = (f32[1568,384]{1,0:T(8,128)S(1)}, bf16[1568,512]{1,0:T(8,128)(2,1)S(1)}, bf16[400,1568]{1,0:T(8,128)(2,1)S(1)}) custom-call(bf16[1568,384]{1,0:T(8,128)(2,1)S(1)} %get-tuple-element.188.mrg, bf16[1568,384]{1,0:T(8,128)(2,1)S(1)} %get-tuple-element.189.tok, bf16[384,384]{1,0:T(8,128)(2,1)S(1)} %get-tuple-element.190.outt, ...), custom_call_target="tpu_custom_call" | custom-call | flops 3449999872 | tf_op jit(solution)/shard_map/mlp_begin/pallas_call | solution.py:664
  46.7 0.4 collective-permute-done.14.other
  47.1 16.9 %mlp.1 = (f32[1568,384]{1,0:T(8,128)S(1)}, f32[1568,384]{1,0:T(8,128)S(1)}, bf16[768,768]{1,0:T(8,128)(2,1)S(1)}, bf16[768,768]{1,0:T(8,128)(2,1)S(1)}, f32[8,1536]{1,0:T(8,128)S(1)}) custom-call(s32[4]{0:T(128)S(1)} %pad_add_fusion.idx, bf16[768,768]{1,0:T(8,128)(2,1)S(1)} %constant_dynamic-update-slice_fusion.4.mine, ...), custom_call_target="tpu_custom_call" | custom-call | flops 19549999104 | tf_op jit(solution)/shard_map/mlp/pallas_call | solution.py:664
  64.0 0.2 collective-permute-start.15
  64.2 3.1 %mlp_end.1 = (bf16[1568,384]{1,0:T(8,128)(2,1)}, f32[1568,384]{1,0:T(8,128)S(1)}, f32[8,384]{1,0:T(8,128)S(1)}) custom-call(f32[1568,384]{1,0:T(8,128)S(1)} %get-tuple-element.192.mid, f32[1568,384]{1,0:T(8,128)S(1)} %get-tuple-element.202.acc_m, f32[1568,384]{1,0:T(8,128)S(1)} %get-tuple-element.203.acc_g, bf16[1568,384]{1,0:T(8,128)(2,1)S(1)} %get-tuple-element.200.gout, ...), custom_call_target="tpu_custom_call" | custom-call | flops 3449999872 | tf_op jit(solution)/shard_map/mlp_end/pallas_call | solution.py:664
  67.3 0.0 collective-permute-done.15.got
  67.3 0.3 plane_sum.2
  67.5 0.6 collective-permute-start.16
  68.2 1.4 %collective-permute-start.17 = (bf16[192,768]{1,0:T(8,128)(2,1)S(1)}, bf16[192,768]{1,0:T(8,128)(2,1)S(1)}, u32[]{:S(2)}, u32[]{:S(2)}) collective-permute-start(bf16[192,768]{1,0:T(8,128)(2,1)S(1)} %get-tuple-element.228), channel_id=1, source_target_pairs={{0,4},{1,5},{2,6},{3,7},{4,0},{5,1},{6,2},{7,3},{8,12},{9,13},{10,... | collective-permute-start | bytes 884744 | tf_op jit(solution)/shard_map/ppermute | solution.py:610
  69.6 1.5 %collective-permute-start.18 = (bf16[192,768]{1,0:T(8,128)(2,1)S(1)}, bf16[192,768]{1,0:T(8,128)(2,1)S(1)}, u32[]{:S(2)}, u32[]{:S(2)}) collective-permute-start(bf16[192,768]{1,0:T(8,128)(2,1)S(1)} %get-tuple-element.229), channel_id=1, source_target_pairs={{0,6},{1,7},{2,4},{3,5},{4,2},{5,3},{6,0},{7,1},{8,14},{9,15},{10,... | collective-permute-start | bytes 884744 | tf_op jit(solution)/shard_map/ppermute | solution.py:610
  71.1 14.7 %attention_backward.1 = (bf16[800,384]{1,0:T(8,128)(2,1)S(1)}, bf16[800,384]{1,0:T(8,128)(2,1)S(1)}, bf16[8,1152,256]{2,1,0:T(8,128)(2,1)S(1)}) custom-call(s32[4]{0:T(128)S(1)} %pad_add_fusion.idx, f32[1568,384]{1,0:T(8,128)S(1)} %get-tuple-element.213.gmid, bf16[8,384,256]{2,1,0:T(8,128)(2,1)S(1)} %copy-done.1, bf16[8,384,256]{2,1,0:T(8,128)(2,1)S(1)} %copy-done.3, ...), custom_call_target="tpu_custom_call" | custom-call | flops 17250000896 | tf_op jit(solution)/shard_map/attention_backward/pallas_call | solution.py:664
  85.9 0.0 collective-permute-done.16.refs_0_
  85.9 0.0 collective-permute-done.18.refs_2_
  85.9 0.1 collective-permute-start.19
  86.0 0.1 half_sum.2
  86.1 1.9 %collective-permute-done.19.got = bf16[800,384]{1,0:T(8,128)(2,1)S(1)} collective-permute-done((bf16[800,384]{1,0:T(8,128)(2,1)S(1)}, bf16[800,384]{1,0:T(8,128)(2,1)S(1)}, u32[]{:S(2)}, u32[]{:S(2)}) %collective-permute-start.19) | collective-permute-done | bytes 614432 | tf_op jit(solution)/shard_map/ppermute | solution.py:610
  88.0 0.1 plane_sum.3
  88.1 0.6 collective-permute-start.20
  88.8 1.4 %collective-permute-start.21 = (bf16[224,384]{1,0:T(8,128)(2,1)S(1)}, bf16[224,384]{1,0:T(8,128)(2,1)S(1)}, u32[]{:S(2)}, u32[]{:S(2)}) collective-permute-start(bf16[224,384]{1,0:T(8,128)(2,1)S(1)} %get-tuple-element.239), channel_id=1, source_target_pairs={{0,4},{1,5},{2,6},{3,7},{4,0},{5,1},{6,2},{7,3},{8,12},{9,13},{10,... | collective-permute-start | bytes 516104 | tf_op jit(solution)/shard_map/ppermute | solution.py:610
  90.2 1.5 %collective-permute-start.22 = (bf16[224,384]{1,0:T(8,128)(2,1)S(1)}, bf16[224,384]{1,0:T(8,128)(2,1)S(1)}, u32[]{:S(2)}, u32[]{:S(2)}) collective-permute-start(bf16[224,384]{1,0:T(8,128)(2,1)S(1)} %get-tuple-element.240), channel_id=1, source_target_pairs={{0,6},{1,7},{2,4},{3,5},{4,2},{5,3},{6,0},{7,1},{8,14},{9,15},{10,... | collective-permute-start | bytes 516104 | tf_op jit(solution)/shard_map/ppermute | solution.py:610
  91.7 2.8 %collective-permute-start.23 = (bf16[96,768]{1,0:T(8,128)(2,1)S(1)}, bf16[96,768]{1,0:T(8,128)(2,1)S(1)}, u32[]{:S(2)}, u32[]{:S(2)}) collective-permute-start(bf16[96,768]{1,0:T(8,128)(2,1)S(1)} %get-tuple-element.241), channel_id=1, source_target_pairs={{0,16},{1,17},{2,18},{3,19},{4,20},{5,21},{6,22},{7,23},{8,24},{9,... | collective-permute-start | bytes 442376 | tf_op jit(solution)/shard_map/ppermute | solution.py:610
  94.5 7.2 %tokens_end.1 = (f32[1568,384]{1,0:T(8,128)}, f32[48,384]{1,0:T(8,128)S(1)}, f32[48,384]{1,0:T(8,128)S(1)}, f32[48,384]{1,0:T(8,128)S(1)}, f32[48,384]{1,0:T(8,1...) custom-call(bf16[1568,384]{1,0:T(8,128)(2,1)S(1)} %get-tuple-element, ...), custom_call_target="tpu_custom_call" | custom-call | flops 5750000128 | tf_op jit(solution)/shard_map/tokens_end/pallas_call | solution.py:664
  101.7 0.0 collective-permute-done.23.refs_0_
  101.8 1.0 collective-permute-start.24
  102.8 0.1 line_sum.1
  102.9 1.1 collective-permute-start.25
  104.0 0.9 collective-permute-start.26
  104.9 2.5 %collective-permute-start.27 = (bf16[80,384]{1,0:T(8,128)(2,1)S(1)}, bf16[80,384]{1,0:T(8,128)(2,1)S(1)}, u32[]{:S(2)}, u32[]{:S(2)}) collective-permute-start(bf16[80,384]{1,0:T(8,128)(2,1)S(1)} %get-tuple-element.258), channel_id=1, source_target_pairs={{0,24},{1,25},{2,26},{3,27},{4,28},{5,29},{6,30},{7,31},{8,16},{9,... | collective-permute-start | bytes 184328 | tf_op jit(solution)/shard_map/ppermute | solution.py:610
  107.4 0.1 collective-permute-done.25.refs_3_
  107.5 3.5 %collective-permute-done.26.refs_4_ = bf16[80,384]{1,0:T(8,128)(2,1)S(1)} collective-permute-done((bf16[80,384]{1,0:T(8,128)(2,1)S(1)}, bf16[80,384]{1,0:T(8,128)(2,1)S(1)}, u32[]{:S(2)}, u32[]{:S(2)}) %collective-permute-start.26) | collective-permute-done | bytes 61472 | tf_op jit(solution)/shard_map/ppermute | solution.py:610
  111.1 1.6 %step_all.1 = (f32[48,384]{1,0:T(8,128)}, f32[48,384]{1,0:T(8,128)}, f32[48,384]{1,0:T(8,128)}, f32[48,384]{1,0:T(8,128)}, f32[48,384]{1,0:T(8,128)}, /*index=5*...) custom-call(s32[4]{0:T(128)S(1)} %pad_add_fusion.idx, ...), custom_call_target="tpu_custom_call" | custom-call | flops 2300000000 | tf_op jit(solution)/shard_map/step_all/pallas_call | solution.py:664
  (41 shorter events, 0.3 us)
Async XLA Ops:
  1.6 14.1 %copy-start.8 = (s32[6272]{0:T(1024)S(1)}, s32[6272]{0:T(1024)}, u32[]{:S(2)}) copy-start(s32[6272]{0:T(1024)} %param.30) | copy-start | bytes 75268
  2.6 9.5 %collective-permute-start.4 = (bf16[16,384]{1,0:T(8,128)(2,1)S(1)}, bf16[16,384]{1,0:T(8,128)(2,1)S(1)}, u32[]{:S(2)}, u32[]{:S(2)}) collective-permute-start(bf16[16,384]{1,0:T(8,128)(2,1)S(1)} %get-tuple-element.168), channel_id=1, source_target_pairs={{0,2},{1,3},{2,0},{3,1},{4,6},{5,7},{6,4},{7,5},{8,10},{9,11},{10,... | collective-permute-start | bytes 36872 | tf_op jit(solution)/shard_map/ppermute | solution.py:610
  5.6 6.5 %collective-permute-start.2 = (bf16[48,384]{1,0:T(8,128)(2,1)S(1)}, bf16[48,384]{1,0:T(8,128)(2,1)S(1)}, u32[]{:S(2)}, u32[]{:S(2)}) collective-permute-start(bf16[48,384]{1,0:T(8,128)(2,1)S(1)} %pack_attention.1), channel_id=1, source_target_pairs={{0,24},{1,25},{2,26},{3,27},{4,28},{5,29},{6,30},{7,31},{8,16},{9,... | collective-permute-start | bytes 110600 | tf_op jit(solution)/shard_map/ppermute | solution.py:610
  9.2 5.5 %collective-permute-start.1 = (bf16[48,384]{1,0:T(8,128)(2,1)S(1)}, bf16[48,384]{1,0:T(8,128)(2,1)S(1)}, u32[]{:S(2)}, u32[]{:S(2)}) collective-permute-start(bf16[48,384]{1,0:T(8,128)(2,1)S(1)} %pack_attention.1), channel_id=1, source_target_pairs={{0,16},{1,17},{2,18},{3,19},{4,20},{5,21},{6,22},{7,23},{8,24},{9,... | collective-permute-start | bytes 110600 | tf_op jit(solution)/shard_map/ppermute | solution.py:610
  9.2 5.5 %collective-permute-start = (bf16[48,384]{1,0:T(8,128)(2,1)S(1)}, bf16[48,384]{1,0:T(8,128)(2,1)S(1)}, u32[]{:S(2)}, u32[]{:S(2)}) collective-permute-start(bf16[48,384]{1,0:T(8,128)(2,1)S(1)} %pack_attention.1), channel_id=1, source_target_pairs={{0,8},{1,9},{2,10},{3,11},{4,12},{5,13},{6,14},{7,15},{8,0},{9,1},... | collective-permute-start | bytes 110600 | tf_op jit(solution)/shard_map/ppermute | solution.py:610
  10.0 5.5 %collective-permute-start.3 = (bf16[48,768]{1,0:T(8,128)(2,1)S(1)}, bf16[48,768]{1,0:T(8,128)(2,1)S(1)}, u32[]{:S(2)}, u32[]{:S(2)}) collective-permute-start(bf16[48,768]{1,0:T(8,128)(2,1)S(1)} %get-tuple-element.167), channel_id=1, source_target_pairs={{0,16},{1,17},{2,18},{3,19},{4,20},{5,21},{6,22},{7,23},{8,24},{9,... | collective-permute-start | bytes 221192 | tf_op jit(solution)/shard_map/ppermute | solution.py:610
  15.6 4.3 %collective-permute-start.8 = (bf16[32,384]{1,0:T(8,128)(2,1)S(1)}, bf16[32,384]{1,0:T(8,128)(2,1)S(1)}, u32[]{:S(2)}, u32[]{:S(2)}) collective-permute-start(bf16[32,384]{1,0:T(8,128)(2,1)S(1)} %pad_maximum_fusion.3.own), channel_id=1, source_target_pairs={{0,1},{1,0},{2,3},{3,2},{4,5},{5,4},{6,7},{7,6},{8,9},{9,8},{10,11... | collective-permute-start | bytes 73736 | tf_op jit(solution)/shard_map/ppermute | solution.py:610
  16.4 10.7 %collective-permute-start.7 = (bf16[192,384]{1,0:T(8,128)(2,1)S(1)}, bf16[192,384]{1,0:T(8,128)(2,1)S(1)}, u32[]{:S(2)}, u32[]{:S(2)}) collective-permute-start(bf16[192,384]{1,0:T(8,128)(2,1)S(1)} %pad_maximum_fusion.1), channel_id=1, source_target_pairs={{0,6},{1,7},{2,4},{3,5},{4,2},{5,3},{6,0},{7,1},{8,14},{9,15},{10,... | collective-permute-start | bytes 442376 | tf_op jit(solution)/shard_map/ppermute | solution.py:610
  17.9 9.2 %collective-permute-start.6 = (bf16[192,384]{1,0:T(8,128)(2,1)S(1)}, bf16[192,384]{1,0:T(8,128)(2,1)S(1)}, u32[]{:S(2)}, u32[]{:S(2)}) collective-permute-start(bf16[192,384]{1,0:T(8,128)(2,1)S(1)} %pad_maximum_fusion.1), channel_id=1, source_target_pairs={{0,4},{1,5},{2,6},{3,7},{4,0},{5,1},{6,2},{7,3},{8,12},{9,13},{10,... | collective-permute-start | bytes 442376 | tf_op jit(solution)/shard_map/ppermute | solution.py:610
  18.4 8.7 %collective-permute-start.5 = (bf16[192,384]{1,0:T(8,128)(2,1)S(1)}, bf16[192,384]{1,0:T(8,128)(2,1)S(1)}, u32[]{:S(2)}, u32[]{:S(2)}) collective-permute-start(bf16[192,384]{1,0:T(8,128)(2,1)S(1)} %pad_maximum_fusion.1), channel_id=1, source_target_pairs={{0,2},{1,3},{2,0},{3,1},{4,6},{5,7},{6,4},{7,5},{8,10},{9,11},{10,... | collective-permute-start | bytes 442376 | tf_op jit(solution)/shard_map/ppermute | solution.py:610
  19.9 7.1 %collective-permute-start.9 = (bf16[96,768]{1,0:T(8,128)(2,1)S(1)}, bf16[96,768]{1,0:T(8,128)(2,1)S(1)}, u32[]{:S(2)}, u32[]{:S(2)}) collective-permute-start(bf16[96,768]{1,0:T(8,128)(2,1)S(1)} %pad_maximum_fusion.2), channel_id=1, source_target_pairs={{0,8},{1,9},{2,10},{3,11},{4,12},{5,13},{6,14},{7,15},{8,0},{9,1},... | collective-permute-start | bytes 442376 | tf_op jit(solution)/shard_map/ppermute | solution.py:610
  27.2 3.6 %collective-permute-start.10 = (bf16[768,384]{1,0:T(8,128)(2,1)S(1)}, bf16[768,384]{1,0:T(8,128)(2,1)S(1)}, u32[]{:S(2)}, u32[]{:S(2)}) collective-permute-start(bf16[768,384]{1,0:T(8,128)(2,1)S(1)} %constant_dynamic-update-slice_fusion.mine), channel_id=1, source_target_pairs={{0,1},{1,0},{2,3},{3,2},{4,5},{5,4},{6,7},{7,6},{8,9},{9,8},{10,11... | collective-permute-start | bytes 1769480 | tf_op jit(solution)/shard_map/ppermute | solution.py:610
  27.3 14.6 %collective-permute-start.13 = (bf16[192,768]{1,0:T(8,128)(2,1)S(1)}, bf16[192,768]{1,0:T(8,128)(2,1)S(1)}, u32[]{:S(2)}, u32[]{:S(2)}) collective-permute-start(bf16[192,768]{1,0:T(8,128)(2,1)S(1)} %pad_maximum_fusion), channel_id=1, source_target_pairs={{0,6},{1,7},{2,4},{3,5},{4,2},{5,3},{6,0},{7,1},{8,14},{9,15},{10,... | collective-permute-start | bytes 884744 | tf_op jit(solution)/shard_map/ppermute | solution.py:610
  28.9 15.1 %collective-permute-start.12 = (bf16[192,768]{1,0:T(8,128)(2,1)S(1)}, bf16[192,768]{1,0:T(8,128)(2,1)S(1)}, u32[]{:S(2)}, u32[]{:S(2)}) collective-permute-start(bf16[192,768]{1,0:T(8,128)(2,1)S(1)} %pad_maximum_fusion), channel_id=1, source_target_pairs={{0,4},{1,5},{2,6},{3,7},{4,0},{5,1},{6,2},{7,3},{8,12},{9,13},{10,... | collective-permute-start | bytes 884744 | tf_op jit(solution)/shard_map/ppermute | solution.py:610
  29.4 14.7 %collective-permute-start.11 = (bf16[192,768]{1,0:T(8,128)(2,1)S(1)}, bf16[192,768]{1,0:T(8,128)(2,1)S(1)}, u32[]{:S(2)}, u32[]{:S(2)}) collective-permute-start(bf16[192,768]{1,0:T(8,128)(2,1)S(1)} %pad_maximum_fusion), channel_id=1, source_target_pairs={{0,2},{1,3},{2,0},{3,1},{4,6},{5,7},{6,4},{7,5},{8,10},{9,11},{10,... | collective-permute-start | bytes 884744 | tf_op jit(solution)/shard_map/ppermute | solution.py:610
  41.9 4.7 %copy-start = (bf16[8,384,256]{2,1,0:T(8,128)(2,1)}, bf16[8,384,256]{2,1,0:T(8,128)(2,1)S(1)}, u32[]{:S(2)}) copy-start(bf16[8,384,256]{2,1,0:T(8,128)(2,1)S(1)} %get-tuple-element.214.qt) | copy-start | bytes 4718596
  41.9 4.7 %copy-start.2 = (bf16[8,384,256]{2,1,0:T(8,128)(2,1)}, bf16[8,384,256]{2,1,0:T(8,128)(2,1)S(1)}, u32[]{:S(2)}) copy-start(bf16[8,384,256]{2,1,0:T(8,128)(2,1)S(1)} %get-tuple-element.215.kt) | copy-start | bytes 4718596
  41.9 4.7 %copy-start.4 = (bf16[8,256,384]{2,1,0:T(8,128)(2,1)}, bf16[8,256,384]{2,1,0:T(8,128)(2,1)S(1)}, u32[]{:S(2)}) copy-start(bf16[8,256,384]{2,1,0:T(8,128)(2,1)S(1)} %get-tuple-element.216.vv) | copy-start | bytes 4718596
  41.9 4.7 %copy-start.6 = (bf16[8,384,256]{2,1,0:T(8,128)(2,1)}, bf16[8,384,256]{2,1,0:T(8,128)(2,1)S(1)}, u32[]{:S(2)}) copy-start(bf16[8,384,256]{2,1,0:T(8,128)(2,1)S(1)} %get-tuple-element.218.mt) | copy-start | bytes 4718596
  44.2 2.9 %collective-permute-start.14 = (bf16[768,768]{1,0:T(8,128)(2,1)S(1)}, bf16[768,768]{1,0:T(8,128)(2,1)S(1)}, u32[]{:S(2)}, u32[]{:S(2)}) collective-permute-start(bf16[768,768]{1,0:T(8,128)(2,1)S(1)} %constant_dynamic-update-slice_fusion.4.mine), channel_id=1, source_target_pairs={{0,1},{1,0},{2,3},{3,2},{4,5},{5,4},{6,7},{7,6},{8,9},{9,8},{10,11... | collective-permute-start | bytes 3538952 | tf_op jit(solution)/shard_map/ppermute | solution.py:610
  64.0 3.3 %collective-permute-start.15 = (bf16[768,768]{1,0:T(8,128)(2,1)S(1)}, bf16[768,768]{1,0:T(8,128)(2,1)S(1)}, u32[]{:S(2)}, u32[]{:S(2)}) collective-permute-start(bf16[768,768]{1,0:T(8,128)(2,1)S(1)} %get-tuple-element.205), channel_id=1, source_target_pairs={{0,1},{1,0},{2,3},{3,2},{4,5},{5,4},{6,7},{7,6},{8,9},{9,8},{10,11... | collective-permute-start | bytes 3538952 | tf_op jit(solution)/shard_map/ppermute | solution.py:610
  64.2 6.9 %copy-start.5 = (bf16[8,256,384]{2,1,0:T(8,128)(2,1)S(1)}, bf16[8,256,384]{2,1,0:T(8,128)(2,1)}, u32[]{:S(2)}) copy-start(bf16[8,256,384]{2,1,0:T(8,128)(2,1)} %copy-done.4) | copy-start | bytes 4718596
  64.2 6.9 %copy-start.7 = (bf16[8,384,256]{2,1,0:T(8,128)(2,1)S(1)}, bf16[8,384,256]{2,1,0:T(8,128)(2,1)}, u32[]{:S(2)}) copy-start(bf16[8,384,256]{2,1,0:T(8,128)(2,1)} %copy-done.6) | copy-start | bytes 4718596
  67.3 3.8 %copy-start.1 = (bf16[8,384,256]{2,1,0:T(8,128)(2,1)S(1)}, bf16[8,384,256]{2,1,0:T(8,128)(2,1)}, u32[]{:S(2)}) copy-start(bf16[8,384,256]{2,1,0:T(8,128)(2,1)} %copy-done) | copy-start | bytes 4718596
  67.3 3.8 %copy-start.3 = (bf16[8,384,256]{2,1,0:T(8,128)(2,1)S(1)}, bf16[8,384,256]{2,1,0:T(8,128)(2,1)}, u32[]{:S(2)}) copy-start(bf16[8,384,256]{2,1,0:T(8,128)(2,1)} %copy-done.2) | copy-start | bytes 4718596
  67.5 18.3 %collective-permute-start.16 = (bf16[192,768]{1,0:T(8,128)(2,1)S(1)}, bf16[192,768]{1,0:T(8,128)(2,1)S(1)}, u32[]{:S(2)}, u32[]{:S(2)}) collective-permute-start(bf16[192,768]{1,0:T(8,128)(2,1)S(1)} %get-tuple-element.227), channel_id=1, source_target_pairs={{0,2},{1,3},{2,0},{3,1},{4,6},{5,7},{6,4},{7,5},{8,10},{9,11},{10,... | collective-permute-start | bytes 884744 | tf_op jit(solution)/shard_map/ppermute | solution.py:610
  68.2 17.7 %collective-permute-start.17 = (bf16[192,768]{1,0:T(8,128)(2,1)S(1)}, bf16[192,768]{1,0:T(8,128)(2,1)S(1)}, u32[]{:S(2)}, u32[]{:S(2)}) collective-permute-start(bf16[192,768]{1,0:T(8,128)(2,1)S(1)} %get-tuple-element.228), channel_id=1, source_target_pairs={{0,4},{1,5},{2,6},{3,7},{4,0},{5,1},{6,2},{7,3},{8,12},{9,13},{10,... | collective-permute-start | bytes 884744 | tf_op jit(solution)/shard_map/ppermute | solution.py:610
  69.6 16.3 %collective-permute-start.18 = (bf16[192,768]{1,0:T(8,128)(2,1)S(1)}, bf16[192,768]{1,0:T(8,128)(2,1)S(1)}, u32[]{:S(2)}, u32[]{:S(2)}) collective-permute-start(bf16[192,768]{1,0:T(8,128)(2,1)S(1)} %get-tuple-element.229), channel_id=1, source_target_pairs={{0,6},{1,7},{2,4},{3,5},{4,2},{5,3},{6,0},{7,1},{8,14},{9,15},{10,... | collective-permute-start | bytes 884744 | tf_op jit(solution)/shard_map/ppermute | solution.py:610
  85.9 2.1 %collective-permute-start.19 = (bf16[800,384]{1,0:T(8,128)(2,1)S(1)}, bf16[800,384]{1,0:T(8,128)(2,1)S(1)}, u32[]{:S(2)}, u32[]{:S(2)}) collective-permute-start(bf16[800,384]{1,0:T(8,128)(2,1)S(1)} %get-tuple-element.231), channel_id=1, source_target_pairs={{0,1},{1,0},{2,3},{3,2},{4,5},{5,4},{6,7},{7,6},{8,9},{9,8},{10,11... | collective-permute-start | bytes 1843208 | tf_op jit(solution)/shard_map/ppermute | solution.py:610
  88.1 13.6 %collective-permute-start.20 = (bf16[224,384]{1,0:T(8,128)(2,1)S(1)}, bf16[224,384]{1,0:T(8,128)(2,1)S(1)}, u32[]{:S(2)}, u32[]{:S(2)}) collective-permute-start(bf16[224,384]{1,0:T(8,128)(2,1)S(1)} %get-tuple-element.238), channel_id=1, source_target_pairs={{0,2},{1,3},{2,0},{3,1},{4,6},{5,7},{6,4},{7,5},{8,10},{9,11},{10,... | collective-permute-start | bytes 516104 | tf_op jit(solution)/shard_map/ppermute | solution.py:610
  88.8 13.0 %collective-permute-start.21 = (bf16[224,384]{1,0:T(8,128)(2,1)S(1)}, bf16[224,384]{1,0:T(8,128)(2,1)S(1)}, u32[]{:S(2)}, u32[]{:S(2)}) collective-permute-start(bf16[224,384]{1,0:T(8,128)(2,1)S(1)} %get-tuple-element.239), channel_id=1, source_target_pairs={{0,4},{1,5},{2,6},{3,7},{4,0},{5,1},{6,2},{7,3},{8,12},{9,13},{10,... | collective-permute-start | bytes 516104 | tf_op jit(solution)/shard_map/ppermute | solution.py:610
  90.2 11.5 %collective-permute-start.22 = (bf16[224,384]{1,0:T(8,128)(2,1)S(1)}, bf16[224,384]{1,0:T(8,128)(2,1)S(1)}, u32[]{:S(2)}, u32[]{:S(2)}) collective-permute-start(bf16[224,384]{1,0:T(8,128)(2,1)S(1)} %get-tuple-element.240), channel_id=1, source_target_pairs={{0,6},{1,7},{2,4},{3,5},{4,2},{5,3},{6,0},{7,1},{8,14},{9,15},{10,... | collective-permute-start | bytes 516104 | tf_op jit(solution)/shard_map/ppermute | solution.py:610
  91.7 10.0 %collective-permute-start.23 = (bf16[96,768]{1,0:T(8,128)(2,1)S(1)}, bf16[96,768]{1,0:T(8,128)(2,1)S(1)}, u32[]{:S(2)}, u32[]{:S(2)}) collective-permute-start(bf16[96,768]{1,0:T(8,128)(2,1)S(1)} %get-tuple-element.241), channel_id=1, source_target_pairs={{0,16},{1,17},{2,18},{3,19},{4,20},{5,21},{6,22},{7,23},{8,24},{9,... | collective-permute-start | bytes 442376 | tf_op jit(solution)/shard_map/ppermute | solution.py:610
  101.8 9.3 %collective-permute-start.24 = (bf16[48,768]{1,0:T(8,128)(2,1)S(1)}, bf16[48,768]{1,0:T(8,128)(2,1)S(1)}, u32[]{:S(2)}, u32[]{:S(2)}) collective-permute-start(bf16[48,768]{1,0:T(8,128)(2,1)S(1)} %get-tuple-element.249), channel_id=1, source_target_pairs={{0,8},{1,9},{2,10},{3,11},{4,12},{5,13},{6,14},{7,15},{8,0},{9,1},... | collective-permute-start | bytes 221192 | tf_op jit(solution)/shard_map/ppermute | solution.py:610
  102.9 4.6 %collective-permute-start.25 = (bf16[80,384]{1,0:T(8,128)(2,1)S(1)}, bf16[80,384]{1,0:T(8,128)(2,1)S(1)}, u32[]{:S(2)}, u32[]{:S(2)}) collective-permute-start(bf16[80,384]{1,0:T(8,128)(2,1)S(1)} %get-tuple-element.256), channel_id=1, source_target_pairs={{0,8},{1,9},{2,10},{3,11},{4,12},{5,13},{6,14},{7,15},{8,0},{9,1},... | collective-permute-start | bytes 184328 | tf_op jit(solution)/shard_map/ppermute | solution.py:610
  104.0 7.0 %collective-permute-start.26 = (bf16[80,384]{1,0:T(8,128)(2,1)S(1)}, bf16[80,384]{1,0:T(8,128)(2,1)S(1)}, u32[]{:S(2)}, u32[]{:S(2)}) collective-permute-start(bf16[80,384]{1,0:T(8,128)(2,1)S(1)} %get-tuple-element.257), channel_id=1, source_target_pairs={{0,16},{1,17},{2,18},{3,19},{4,20},{5,21},{6,22},{7,23},{8,24},{9,... | collective-permute-start | bytes 184328 | tf_op jit(solution)/shard_map/ppermute | solution.py:610
  104.9 6.1 %collective-permute-start.27 = (bf16[80,384]{1,0:T(8,128)(2,1)S(1)}, bf16[80,384]{1,0:T(8,128)(2,1)S(1)}, u32[]{:S(2)}, u32[]{:S(2)}) collective-permute-start(bf16[80,384]{1,0:T(8,128)(2,1)S(1)} %get-tuple-element.258), channel_id=1, source_target_pairs={{0,24},{1,25},{2,26},{3,27},{4,28},{5,29},{6,30},{7,31},{8,16},{9,... | collective-permute-start | bytes 184328 | tf_op jit(solution)/shard_map/ppermute | solution.py:610
